TPU v7x, 256 devices: a whole 4x4x8 slice. The times are simulated.
256 devices in a mesh: slab: 64 (over z, x, core), comp: 4 (over y).
Axes of the slice: x: 4, y: 4, z: 8, core: 2. Of those that a mesh axis runs over, the one named last changes fastest.
Arguments:
- kspace: bfloat16 [12, 4, 128, 16384], P('comp', None, None, 'slab'), may hold values from -4 to 4, as said below
- sensitivities: float32 [4, 128, 16384], P(None, 'slab'), may hold values from -2.5 to 2.5, as said below
- sampling: int32 [12, 128, 8192], P('comp', None, 'slab'), may hold values from 0 to 1, as said below
Outputs:
- coefficients: float32 [12, 128, 16384], P('comp', 'slab')
- residual: float32 [12, 128, 16384], P('comp', 'slab')
Inputs may be any that keep to these rules, and one draw needn't show every extreme that they name: `sampling`: sampled (1) or not (0) for each component and k-space point. `sensitivities`: real and imaginary parts of each coil's sensitivity. `kspace`: real and imaginary parts of the projected data.
All inputs are finite; a program needn't handle non-finite values.
Results may differ from a plain program's by a relative error of at most 0.025.
Values may be sent and summed in bfloat16 or wider, within the bound.
No kernel may reach another device: no remote copies, remote signals or barrier semaphores. Data moves between devices by JAX's collectives and lax.ppermute only.
A program may use at most 128 MiB of HBM per device.

v0:
```python
import math

import jax
import jax.numpy as jnp
from jax import lax
from jax.sharding import PartitionSpec as P

NX = 128
NY = 128
NZ = 64
ITERS = 2


def fourier_blocks(length, orientation):
    positions = jnp.arange(length, dtype=jnp.int32)
    angles = (positions[:, None] * positions[None, :] % length).astype(jnp.float32) * (
        2.0 * math.pi / length
    )
    scaling = 1.0 / math.sqrt(length)
    real_part = jnp.cos(angles) * scaling
    imaginary = orientation * jnp.sin(angles) * scaling
    top_rows = jnp.stack([real_part, -imaginary], 1)
    low_rows = jnp.stack([imaginary, real_part], 1)
    return jnp.stack([top_rows, low_rows], 0).astype(jnp.bfloat16)


def make_tables(orientation):
    last_matrix = fourier_blocks(NZ, orientation).reshape(2 * NZ, 2 * NZ).T
    middle_blocks = fourier_blocks(NY, orientation)
    first_blocks = fourier_blocks(NX, orientation)
    return (last_matrix, middle_blocks, first_blocks)


def complex_join(real_out, imag_out):
    shaped_real = real_out.reshape(real_out.shape[:-1] + (-1, 2, NZ))
    swapped = jnp.flip(imag_out.reshape(imag_out.shape[:-1] + (-1, 2, NZ)), -2)
    sign_row = jnp.array([-1.0, 1.0], jnp.float32)[:, None]
    return (shaped_real + sign_row * swapped).reshape(real_out.shape)


def along_last(values, last_matrix):
    shaped = values.reshape(values.shape[:-1] + (-1, last_matrix.shape[0]))
    result = jnp.dot(shaped, last_matrix, preferred_element_type=jnp.float32)
    return result.reshape(values.shape)


def along_middle(values, middle_blocks):
    real_matrix = middle_blocks[0, :, 0, :]
    imag_matrix = middle_blocks[1, :, 0, :]
    flattened = values.reshape((-1, middle_blocks.shape[1], 2 * NZ))
    real_out = jnp.einsum("ky,nyw->nkw", real_matrix, flattened, preferred_element_type=jnp.float32)
    imag_out = jnp.einsum("ky,nyw->nkw", imag_matrix, flattened, preferred_element_type=jnp.float32)
    return complex_join(real_out, imag_out).reshape(values.shape)


def along_first(values, first_blocks):
    real_matrix = first_blocks[0, :, 0, :]
    imag_matrix = first_blocks[1, :, 0, :]
    flattened = values.reshape((-1,) + values.shape[-2:])
    real_out = jnp.einsum("kx,nxw->nkw", real_matrix, flattened, preferred_element_type=jnp.float32)
    imag_out = jnp.einsum("kx,nxw->nkw", imag_matrix, flattened, preferred_element_type=jnp.float32)
    return complex_join(real_out, imag_out).reshape(values.shape)


def spread(component_maps, coil_maps):
    field_view = component_maps.reshape(component_maps.shape[:-1] + (-1, 2, NZ))
    coil_view = coil_maps.reshape(coil_maps.shape[:-1] + (-1, 2, NZ))
    real_part = (
        coil_view[..., 0, :] * field_view[..., 0, :] - coil_view[..., 1, :] * field_view[..., 1, :]
    )
    imaginary = (
        coil_view[..., 0, :] * field_view[..., 1, :] + coil_view[..., 1, :] * field_view[..., 0, :]
    )
    result = jnp.stack([real_part, imaginary], -2)
    return result.reshape(result.shape[:-3] + (-1,))


def unspread(images, coil_maps):
    image_view = images.reshape(images.shape[:-1] + (-1, 2, NZ))
    coil_view = coil_maps.reshape(coil_maps.shape[:-1] + (-1, 2, NZ))
    real_part = (
        coil_view[..., 0, :] * image_view[..., 0, :] + coil_view[..., 1, :] * image_view[..., 1, :]
    )
    imaginary = (
        coil_view[..., 0, :] * image_view[..., 1, :] - coil_view[..., 1, :] * image_view[..., 0, :]
    )
    result = jnp.stack([real_part, imaginary], -2)
    return result.reshape(result.shape[:-3] + (-1,))


def combine_coils(slab_images, sensitivities, inverse):
    section_two = along_middle(slab_images, inverse[1]).astype(jnp.bfloat16)
    section_three = along_last(section_two, inverse[0])
    return jnp.sum(unspread(section_three, sensitivities[None]), axis=1)


def kspace_step_for(pattern_part, forward_first, inverse_first):

    def kspace_step(portion):
        spectrum = along_first(portion, forward_first)
        shaped = spectrum.reshape(spectrum.shape[:3] + (-1, 2, NZ))
        masked = (
            (shaped * pattern_part[:, None, :, :, None, :])
            .reshape(spectrum.shape)
            .astype(jnp.bfloat16)
        )
        restored = along_first(masked, inverse_first).astype(jnp.bfloat16)
        return lax.all_to_all(restored, "slab", split_axis=2, concat_axis=3, tiled=True)

    return kspace_step


def squared_total(residual):
    return lax.psum(jnp.sum(residual * residual), ("slab", "comp"))


def shards(kspace, sensitivities, sampling):
    comps_here, coil_count, grid_rows, width_here = kspace.shape
    local_columns = width_here // (2 * NZ)
    forward = make_tables(-1.0)
    inverse = make_tables(1.0)
    pattern_rows = sampling.astype(jnp.float32).reshape(comps_here, grid_rows, local_columns, NZ)
    pattern_half = pattern_rows.astype(jnp.bfloat16)[:, None, :, :, None, :]
    masked_data = (
        kspace.reshape(comps_here, coil_count, grid_rows, local_columns, 2, NZ) * pattern_half
    ).reshape(kspace.shape)
    returned = along_first(masked_data, inverse[2]).astype(jnp.bfloat16)
    slab_images = lax.all_to_all(returned, "slab", split_axis=2, concat_axis=3, tiled=True)
    right_side = combine_coils(slab_images, sensitivities, inverse)
    coefficients = jnp.zeros_like(right_side)
    residual = right_side
    direction = right_side
    norm_now = squared_total(residual)
    for iteration in range(ITERS):
        images = spread(direction[:, None], sensitivities[None]).astype(jnp.bfloat16)
        section_one = along_last(images, forward[0]).astype(jnp.bfloat16)
        section_two = along_middle(section_one, forward[1]).astype(jnp.bfloat16)
        collected = []
        for position in range(comps_here):
            spectra_step = kspace_step_for(
                pattern_rows[position : position + 1], forward[2], inverse[2]
            )
            collected.append(
                spectra_step(
                    lax.all_to_all(
                        section_two[position : position + 1],
                        "slab",
                        split_axis=3,
                        concat_axis=2,
                        tiled=True,
                    )
                )
            )
        gathered = jnp.concatenate(collected, 0)
        applied = combine_coils(gathered, sensitivities, inverse)
        step_size = norm_now / lax.psum(jnp.sum(direction * applied), ("slab", "comp"))
        coefficients = coefficients + step_size * direction
        residual = residual - step_size * applied
        if iteration + 1 < ITERS:
            norm_next = squared_total(residual)
            direction = residual + norm_next / norm_now * direction
            norm_now = norm_next
    return (coefficients, residual)


def solution(mesh):
    in_specs = (P("comp", None, None, "slab"), P(None, "slab", None), P("comp", None, "slab"))
    out_specs = (P("comp", "slab", None), P("comp", "slab", None))
    return jax.shard_map(shards, mesh=mesh, in_specs=in_specs, out_specs=out_specs, check_vma=False)
```

profile of v0, /device:TPU:2, one launch (start us, length us, event | category | flops | bytes accessed | tf_op | source)
XLA Modules:
  0.0 855.3 jit_solution(4997428012043149161)
XLA Ops:
  7.0 12.7 %all-to-all-start = ((bf16[3,4,128,256]{3,1,0,2:T(4,128)(2,1)}), bf16[3,4,128,256]{3,1,0,2:T(4,128)(2,1)S(1)}, u32[]{:S(2)}, u32[]{:S(2)}) async-start(bf16[3,4,128,256]{3,1,0,2:T(4,128)(2,1)} %copy.393), calls=%async_computation | async-start | bytes 1572864 | tf_op jit(solution)/shard_map/all_to_all | solution.py:128
  23.6 19.1 %all-to-all-done = bf16[3,4,128,256]{3,1,0,2:T(4,128)(2,1)S(1)} async-done(((bf16[3,4,128,256]{3,1,0,2:T(4,128)(2,1)}), bf16[3,4,128,256]{3,1,0,2:T(4,128)(2,1)S(1)}, u32[]{:S(2)}, u32[]{:S(2)}) %all-to-all-start) | async-done | bytes 786464 | tf_op jit(solution)/shard_map/all_to_all | solution.py:128
  49.0 13.1 %copy.407 = bf16[1,4,2,16384]{1,2,0,3:T(2,128)(2,1)} copy(bf16[1,4,2,16384]{3,2,1,0:T(2,128)(2,1)S(1)} %slice.86) | data formatting | bytes 524288 | tf_op jit(solution)/shard_map/slice | solution.py:146
  62.1 16.9 %reshape.776 = bf16[64,2,1024]{2,1,0:T(2,128)(2,1)} reshape(bf16[16384,1,2,4]{3,2,1,0:T(2,128)(2,1)} %bitcast.356) | data formatting | bytes 524288
  86.6 13.1 %copy.415 = bf16[1,4,2,16384]{1,2,0,3:T(2,128)(2,1)} copy(bf16[1,4,2,16384]{3,2,1,0:T(2,128)(2,1)S(1)} %slice.177) | data formatting | bytes 524288 | tf_op jit(solution)/shard_map/slice | solution.py:146
  99.7 16.8 %reshape.774 = bf16[64,2,1024]{2,1,0:T(2,128)(2,1)} reshape(bf16[16384,1,2,4]{3,2,1,0:T(2,128)(2,1)} %bitcast.357) | data formatting | bytes 524288
  117.3 13.1 %copy.423 = bf16[1,4,2,16384]{1,2,0,3:T(2,128)(2,1)} copy(bf16[1,4,2,16384]{3,2,1,0:T(2,128)(2,1)S(1)} %slice.180) | data formatting | bytes 524288 | tf_op jit(solution)/shard_map/slice | solution.py:146
  130.4 16.8 %reshape.772 = bf16[64,2,1024]{2,1,0:T(2,128)(2,1)} reshape(bf16[16384,1,2,4]{3,2,1,0:T(2,128)(2,1)} %bitcast.358) | data formatting | bytes 524288
  157.5 19.1 %reshape.777 = bf16[16384,1,2,4]{3,2,1,0:T(2,128)(2,1)} reshape(bf16[64,2,1024]{2,1,0:T(2,128)(2,1)S(1)} %all-to-all-done.1) | data formatting | bytes 524288
  176.6 11.9 %copy.487 = bf16[1,4,2,64,256]{4,3,2,1,0:T(8,128)(2,1)S(1)} copy(bf16[1,4,2,64,256]{1,2,4,3,0:T(2,128)(2,1)} %bitcast.359) | data formatting | bytes 524288 | tf_op jit(solution)/shard_map/all_to_all | solution.py:145
  200.7 19.1 %reshape.775 = bf16[16384,1,2,4]{3,2,1,0:T(2,128)(2,1)} reshape(bf16[64,2,1024]{2,1,0:T(2,128)(2,1)S(1)} %all-to-all-done.3) | data formatting | bytes 524288
  219.8 11.9 %copy.488 = bf16[1,4,2,64,256]{4,3,2,1,0:T(8,128)(2,1)S(1)} copy(bf16[1,4,2,64,256]{1,2,4,3,0:T(2,128)(2,1)} %bitcast.360) | data formatting | bytes 524288 | tf_op jit(solution)/shard_map/all_to_all | solution.py:145
  233.5 19.1 %reshape.773 = bf16[16384,1,2,4]{3,2,1,0:T(2,128)(2,1)} reshape(bf16[64,2,1024]{2,1,0:T(2,128)(2,1)S(1)} %all-to-all-done.5) | data formatting | bytes 524288
  252.6 11.9 %copy.489 = bf16[1,4,2,64,256]{4,3,2,1,0:T(8,128)(2,1)S(1)} copy(bf16[1,4,2,64,256]{1,2,4,3,0:T(2,128)(2,1)} %bitcast.361) | data formatting | bytes 524288 | tf_op jit(solution)/shard_map/all_to_all | solution.py:145
  280.2 11.3 %all-to-all-done.4 = bf16[1,4,128,256]{3,1,0,2:T(4,128)(2,1)S(1)} async-done(((bf16[1,4,128,256]{3,1,0,2:T(4,128)(2,1)}), bf16[1,4,128,256]{3,1,0,2:T(4,128)(2,1)S(1)}, u32[]{:S(2)}, u32[]{:S(2)}) %all-to-all-start.4) | async-done | bytes 262176 | tf_op jit(solution)/shard_map/all_to_all | solution.py:108
  315.8 11.8 %all-to-all-done.2 = bf16[1,4,128,256]{3,1,0,2:T(4,128)(2,1)S(1)} async-done(((bf16[1,4,128,256]{3,1,0,2:T(4,128)(2,1)}), bf16[1,4,128,256]{3,1,0,2:T(4,128)(2,1)S(1)}, u32[]{:S(2)}, u32[]{:S(2)}) %all-to-all-start.2) | async-done | bytes 262176 | tf_op jit(solution)/shard_map/all_to_all | solution.py:108
  332.7 74.8 %all-reduce = (f32[]{:T(128)}, f32[]{:T(128)}) all-reduce(f32[]{:T(128)} %get-tuple-element.3, f32[]{:T(128)} %get-tuple-element.2), channel_id=1, replica_groups=mesh['slab'=64,'comp'=4] {'slab','comp'}, use_global_device_ids=true, to_apply=%region_2.3 | all-reduce | flops 2 | bytes 16 | tf_op jit(solution)/shard_map/psum | solution.py:114
  409.6 74.3 %psum.30 = f32[]{:T(128)} all-reduce(f32[]{:T(128)} %multiply_reduce_fusion.1), channel_id=1, replica_groups=mesh['slab'=64,'comp'=4] {'slab','comp'}, use_global_device_ids=true, to_apply=%region_7.8 | all-reduce | flops 1 | bytes 8 | tf_op jit(solution)/shard_map/psum | solution.py:114
  488.9 13.1 %copy.437 = bf16[1,4,2,16384]{1,2,0,3:T(2,128)(2,1)} copy(bf16[1,4,2,16384]{3,2,1,0:T(2,128)(2,1)S(1)} %slice.187) | data formatting | bytes 524288 | tf_op jit(solution)/shard_map/slice | solution.py:146
  502.1 16.8 %reshape.782 = bf16[64,2,1024]{2,1,0:T(2,128)(2,1)} reshape(bf16[16384,1,2,4]{3,2,1,0:T(2,128)(2,1)} %bitcast.362) | data formatting | bytes 524288
  527.1 13.1 %copy.445 = bf16[1,4,2,16384]{1,2,0,3:T(2,128)(2,1)} copy(bf16[1,4,2,16384]{3,2,1,0:T(2,128)(2,1)S(1)} %slice.189) | data formatting | bytes 524288 | tf_op jit(solution)/shard_map/slice | solution.py:146
  540.2 16.8 %reshape.780 = bf16[64,2,1024]{2,1,0:T(2,128)(2,1)} reshape(bf16[16384,1,2,4]{3,2,1,0:T(2,128)(2,1)} %bitcast.363) | data formatting | bytes 524288
  557.8 13.1 %copy.453 = bf16[1,4,2,16384]{1,2,0,3:T(2,128)(2,1)} copy(bf16[1,4,2,16384]{3,2,1,0:T(2,128)(2,1)S(1)} %slice.191) | data formatting | bytes 524288 | tf_op jit(solution)/shard_map/slice | solution.py:146
  571.0 16.8 %reshape.778 = bf16[64,2,1024]{2,1,0:T(2,128)(2,1)} reshape(bf16[16384,1,2,4]{3,2,1,0:T(2,128)(2,1)} %bitcast.364) | data formatting | bytes 524288
  598.1 19.1 %reshape.783 = bf16[16384,1,2,4]{3,2,1,0:T(2,128)(2,1)} reshape(bf16[64,2,1024]{2,1,0:T(2,128)(2,1)S(1)} %all-to-all-done.7) | data formatting | bytes 524288
  617.2 11.9 %copy.492 = bf16[1,4,2,64,256]{4,3,2,1,0:T(8,128)(2,1)S(1)} copy(bf16[1,4,2,64,256]{1,2,4,3,0:T(2,128)(2,1)} %bitcast.365) | data formatting | bytes 524288 | tf_op jit(solution)/shard_map/all_to_all | solution.py:145
  641.6 19.1 %reshape.781 = bf16[16384,1,2,4]{3,2,1,0:T(2,128)(2,1)} reshape(bf16[64,2,1024]{2,1,0:T(2,128)(2,1)S(1)} %all-to-all-done.9) | data formatting | bytes 524288
  660.7 11.9 %copy.493 = bf16[1,4,2,64,256]{4,3,2,1,0:T(8,128)(2,1)S(1)} copy(bf16[1,4,2,64,256]{1,2,4,3,0:T(2,128)(2,1)} %bitcast.366) | data formatting | bytes 524288 | tf_op jit(solution)/shard_map/all_to_all | solution.py:145
  674.5 19.9 %reshape.779 = bf16[16384,1,2,4]{3,2,1,0:T(2,128)(2,1)} reshape(bf16[64,2,1024]{2,1,0:T(2,128)(2,1)} %all-to-all-done.11) | data formatting | bytes 524288
  694.4 11.9 %copy.494 = bf16[1,4,2,64,256]{4,3,2,1,0:T(8,128)(2,1)S(1)} copy(bf16[1,4,2,64,256]{1,2,4,3,0:T(2,128)(2,1)} %bitcast.367) | data formatting | bytes 524288 | tf_op jit(solution)/shard_map/all_to_all | solution.py:145
  760.1 11.8 %all-to-all-done.8 = bf16[1,4,128,256]{3,1,0,2:T(4,128)(2,1)S(1)} async-done(((bf16[1,4,128,256]{3,1,0,2:T(4,128)(2,1)}), bf16[1,4,128,256]{3,1,0,2:T(4,128)(2,1)S(1)}, u32[]{:S(2)}, u32[]{:S(2)}) %all-to-all-start.8) | async-done | bytes 262176 | tf_op jit(solution)/shard_map/all_to_all | solution.py:108
  777.0 72.6 %psum.31 = f32[]{:T(128)} all-reduce(f32[]{:T(128)} %multiply_reduce_fusion), channel_id=1, replica_groups=mesh['slab'=64,'comp'=4] {'slab','comp'}, use_global_device_ids=true, to_apply=%region_10.11 | all-reduce | flops 1 | bytes 8 | tf_op jit(solution)/shard_map/psum | solution.py:156
  (217 shorter events, 194.3 us)
Async XLA Ops:
  0.6 2.8 copy-start.8
  5.6 15.3 %copy-start.12 = (f32[4,2,16384]{2,1,0:T(2,128)S(1)}, f32[4,2,16384]{2,1,0:T(2,128)}, u32[]{:S(2)}) copy-start(f32[4,2,16384]{2,1,0:T(2,128)} %param.22) | copy-start | bytes 1572868
  7.0 35.7 %all-to-all-start = ((bf16[3,4,128,256]{3,1,0,2:T(4,128)(2,1)}), bf16[3,4,128,256]{3,1,0,2:T(4,128)(2,1)S(1)}, u32[]{:S(2)}, u32[]{:S(2)}) async-start(bf16[3,4,128,256]{3,1,0,2:T(4,128)(2,1)} %copy.393), calls=%async_computation | async-start | bytes 1572864 | tf_op jit(solution)/shard_map/all_to_all | solution.py:128
  23.5 22.5 %copy-start.13 = (bf16[128,128,1,1,1]{1,0,2,3,4:T(8,128)(2,1)}, bf16[128,128,1,1,1]{1,0,2,3,4:T(8,128)(2,1)S(1)}, u32[]{:S(2)}) copy-start(bf16[128,128,1,1,1]{1,0,2,3,4:T(8,128)(2,1)S(1)} %reshape.766) | copy-start | bytes 98308
  45.9 0.8 copy-start.1
  46.4 0.8 copy-start.4
  62.1 23.0 %copy-start.9 = (f32[3,128,128]{1,2,0:T(8,128)S(1)}, f32[3,128,128]{1,2,0:T(8,128)}, u32[]{:S(2)}) copy-start(f32[3,128,128]{1,2,0:T(8,128)} %get-tuple-element.33) | copy-start | bytes 589828
  79.0 68.3 %all-to-all-start.1 = ((bf16[64,2,1024]{2,1,0:T(2,128)(2,1)}), bf16[64,2,1024]{2,1,0:T(2,128)(2,1)S(1)}, u32[]{:S(2)}, u32[]{:S(2)}) async-start(bf16[64,2,1024]{2,1,0:T(2,128)(2,1)} %reshape.776), calls=%async_computation.1 | async-start | bytes 524288 | tf_op jit(solution)/shard_map/all_to_all | solution.py:145
  85.8 103.7 %copy-start.10 = (f32[1,128,128]{1,2,0:T(8,128)}, f32[1,128,128]{1,2,0:T(8,128)S(1)}, u32[]{:S(2)}) copy-start(f32[1,128,128]{1,2,0:T(8,128)S(1)} %get-tuple-element.30) | copy-start | bytes 196612
  147.2 42.6 %all-to-all-start.3 = ((bf16[64,2,1024]{2,1,0:T(2,128)(2,1)}), bf16[64,2,1024]{2,1,0:T(2,128)(2,1)S(1)}, u32[]{:S(2)}, u32[]{:S(2)}) async-start(bf16[64,2,1024]{2,1,0:T(2,128)(2,1)} %reshape.774), calls=%async_computation.3 | async-start | bytes 524288 | tf_op jit(solution)/shard_map/all_to_all | solution.py:145
  189.9 43.6 %all-to-all-start.5 = ((bf16[64,2,1024]{2,1,0:T(2,128)(2,1)}), bf16[64,2,1024]{2,1,0:T(2,128)(2,1)S(1)}, u32[]{:S(2)}, u32[]{:S(2)}) async-start(bf16[64,2,1024]{2,1,0:T(2,128)(2,1)} %reshape.772), calls=%async_computation.5 | async-start | bytes 524288 | tf_op jit(solution)/shard_map/all_to_all | solution.py:145
  266.9 0.9 copy-start.20
  269.0 22.5 %all-to-all-start.4 = ((bf16[1,4,128,256]{3,1,0,2:T(4,128)(2,1)}), bf16[1,4,128,256]{3,1,0,2:T(4,128)(2,1)S(1)}, u32[]{:S(2)}, u32[]{:S(2)}) async-start(bf16[1,4,128,256]{3,1,0,2:T(4,128)(2,1)} %copy.420), calls=%async_computation.4 | async-start | bytes 524288 | tf_op jit(solution)/shard_map/all_to_all | solution.py:108
  291.5 17.9 %all-to-all-start.6 = ((bf16[1,4,128,256]{3,1,0,2:T(4,128)(2,1)}), bf16[1,4,128,256]{3,1,0,2:T(4,128)(2,1)S(1)}, u32[]{:S(2)}, u32[]{:S(2)}) async-start(bf16[1,4,128,256]{3,1,0,2:T(4,128)(2,1)} %copy.428), calls=%async_computation.6 | async-start | bytes 524288 | tf_op jit(solution)/shard_map/all_to_all | solution.py:108
  309.4 18.3 %all-to-all-start.2 = ((bf16[1,4,128,256]{3,1,0,2:T(4,128)(2,1)}), bf16[1,4,128,256]{3,1,0,2:T(4,128)(2,1)S(1)}, u32[]{:S(2)}, u32[]{:S(2)}) async-start(bf16[1,4,128,256]{3,1,0,2:T(4,128)(2,1)} %copy.412), calls=%async_computation.2 | async-start | bytes 524288 | tf_op jit(solution)/shard_map/all_to_all | solution.py:108
  485.2 0.8 copy-start.14
  485.5 0.9 copy-start.2
  486.4 0.8 copy-start.5
  518.9 68.9 %all-to-all-start.7 = ((bf16[64,2,1024]{2,1,0:T(2,128)(2,1)}), bf16[64,2,1024]{2,1,0:T(2,128)(2,1)S(1)}, u32[]{:S(2)}, u32[]{:S(2)}) async-start(bf16[64,2,1024]{2,1,0:T(2,128)(2,1)} %reshape.782), calls=%async_computation.7 | async-start | bytes 524288 | tf_op jit(solution)/shard_map/all_to_all | solution.py:145
  587.8 42.6 %all-to-all-start.9 = ((bf16[64,2,1024]{2,1,0:T(2,128)(2,1)}), bf16[64,2,1024]{2,1,0:T(2,128)(2,1)S(1)}, u32[]{:S(2)}, u32[]{:S(2)}) async-start(bf16[64,2,1024]{2,1,0:T(2,128)(2,1)} %reshape.780), calls=%async_computation.9 | async-start | bytes 524288 | tf_op jit(solution)/shard_map/all_to_all | solution.py:145
  629.1 0.9 copy-start.11
  629.1 0.9 copy-start.21
  630.4 44.1 %all-to-all-start.11 = ((bf16[64,2,1024]{2,1,0:T(2,128)(2,1)}), bf16[64,2,1024]{2,1,0:T(2,128)(2,1)}, u32[]{:S(2)}, u32[]{:S(2)}) async-start(bf16[64,2,1024]{2,1,0:T(2,128)(2,1)} %reshape.778), calls=%async_computation.11 | async-start | bytes 524288 | tf_op jit(solution)/shard_map/all_to_all | solution.py:145
  660.7 12.4 %copy-start.6 = (bf16[1,128,2,128]{3,1,2,0:T(8,128)(2,1)S(1)}, bf16[1,128,2,128]{3,1,2,0:T(8,128)(2,1)}, u32[]{:S(2)}) copy-start(bf16[1,128,2,128]{3,1,2,0:T(8,128)(2,1)} %get-tuple-element.36) | copy-start | bytes 196612
  672.6 0.8 copy-start.3
  708.3 1.0 copy-start
  711.4 0.9 copy-start.22
  712.6 29.1 %copy-start.7 = (bf16[4,128,2,2,64]{1,4,3,2,0:T(8,128)(2,1)S(1)}, bf16[4,128,2,2,64]{1,4,3,2,0:T(8,128)(2,1)}, u32[]{:S(2)}) copy-start(bf16[4,128,2,2,64]{1,4,3,2,0:T(8,128)(2,1)} %get-tuple-element.43) | copy-start | bytes 786436
  713.5 22.5 %all-to-all-start.10 = ((bf16[1,4,128,256]{3,1,0,2:T(4,128)(2,1)}), bf16[1,4,128,256]{3,1,0,2:T(4,128)(2,1)S(1)}, u32[]{:S(2)}, u32[]{:S(2)}) async-start(bf16[1,4,128,256]{3,1,0,2:T(4,128)(2,1)} %copy.450), calls=%async_computation.10 | async-start | bytes 524288 | tf_op jit(solution)/shard_map/all_to_all | solution.py:108
  736.0 17.9 %all-to-all-start.12 = ((bf16[1,4,128,256]{3,1,0,2:T(4,128)(2,1)}), bf16[1,4,128,256]{3,1,0,2:T(4,128)(2,1)S(1)}, u32[]{:S(2)}, u32[]{:S(2)}) async-start(bf16[1,4,128,256]{3,1,0,2:T(4,128)(2,1)} %copy.458), calls=%async_computation.12 | async-start | bytes 524288 | tf_op jit(solution)/shard_map/all_to_all | solution.py:108
  753.9 18.1 %all-to-all-start.8 = ((bf16[1,4,128,256]{3,1,0,2:T(4,128)(2,1)}), bf16[1,4,128,256]{3,1,0,2:T(4,128)(2,1)S(1)}, u32[]{:S(2)}, u32[]{:S(2)}) async-start(bf16[1,4,128,256]{3,1,0,2:T(4,128)(2,1)} %copy.442), calls=%async_computation.8 | async-start | bytes 524288 | tf_op jit(solution)/shard_map/all_to_all | solution.py:108
  774.8 0.7 copy-start.17
  (4 other events, 2.8 us)
where the time goes:
time: 864 us; the launch traced here: 855 us
  local copies, waits for them, and re-layouts  397 us (46%)
  blocking collectives  222 us (26%)
  starting transfers between devices  112 us (13%)
  waiting for transfers between devices  88.2 us (10%)
  other arithmetic  16.2 us (2%)
  matrix products  13.7 us (2%)
    unnamed x59, local copies, waits for them, and re-layouts  221 us
    psum x2, blocking collectives, squared_total(): return lax.psum(jnp.sum(residual * residual), ('slab', 'comp'))  149 us
    slice x20, local copies, waits for them, and re-layouts, shards(): section_two[position:position + 1]  83.6 us
    all_to_all x12, local copies, waits for them, and re-layouts, shards(): lax.all_to_all(section_two[position:position + 1], 'slab', split_axis=3,...  73.4 us
    psum x1, blocking collectives, shards(): lax.psum(jnp.sum(direction * applied), ('slab', 'comp'))  72.6 us
    all_to_all x6, waiting for transfers between devices, kspace_step(): lax.all_to_all(restored, 'slab', split_axis=2, concat_axis=3, tiled=True)  69 us
    all_to_all x6, starting transfers between devices, shards(): lax.all_to_all(section_two[position:position + 1], 'slab', split_axis=3,...  55.7 us
    all_to_all x6, starting transfers between devices, kspace_step(): lax.all_to_all(restored, 'slab', split_axis=2, concat_axis=3, tiled=True)  44.1 us
  transfers between devices with their start and end apart: 13, of which 7 were waited for; matrix products, arithmetic and copies ran while one was open for 31% of the time, Pallas kernels for 0%

commit v1 on v0

v1 whole, which is shorter than its diff:
```python
import functools
import math

import jax
import jax.numpy as jnp
import numpy as np
from jax import lax
from jax.experimental import pallas as pl
from jax.experimental.pallas import tpu as pltpu
from jax.sharding import PartitionSpec as P

NX = 128
NY = 128
NZ = 64
COILS = 4
PAIRS = COILS // 2
LANES = 2 * NZ
CHUNK = 3


def fourier_blocks(length, orientation):
    positions = np.arange(length)
    angles = (positions[:, None] * positions[None, :] % length) * (2.0 * math.pi / length)
    scaling = 1.0 / math.sqrt(length)
    real_part = np.cos(angles) * scaling
    imaginary = orientation * np.sin(angles) * scaling
    top_rows = np.stack([real_part, -imaginary], 1)
    low_rows = np.stack([imaginary, real_part], 1)
    return np.stack([top_rows, low_rows], 0).astype(np.float32)


def table(spec, *factors, shape):
    return np.einsum(spec, *factors).reshape(shape).astype(jnp.bfloat16)


def make_tables():
    two = np.eye(2, dtype=np.float32)
    slabs = NX // 2
    zf, zi = fourier_blocks(NZ, -1.0), fourier_blocks(NZ, 1.0)
    yf, yi = fourier_blocks(NY, -1.0), fourier_blocks(NY, 1.0)
    xf = fourier_blocks(NX, -1.0).reshape(2, NX, 2, slabs, 2)
    xi = fourier_blocks(NX, 1.0).reshape(2, slabs, 2, 2, NX)
    return {
        "zf": table("akbj,cd->cbjadk", zf, two, shape=(4 * NZ, 4 * NZ)),
        "zi": table("akbj,cd->bcjdak", zi, two, shape=(4 * NZ, 4 * NZ)),
        "yf": table("akbj,cd->kcabjd", yf, two, shape=(4 * NY, 4 * NY)),
        "yi": table("akbj,cd->akcjdb", yi, two, shape=(4 * NY, 4 * NY)),
        "xf": table("akbst,cd->caksdtb", xf, two, shape=(4 * NX, 4 * NX)),
        "xi": table("astbk,cd->sctadbk", xi, two, shape=(4 * NX, 4 * NX)),
        "order": table(
            "ab,cd,ef,gh->acegdfbh",
            two,
            two,
            two,
            np.eye(NZ, dtype=np.float32),
            shape=(8 * NZ, 8 * NZ),
        ),
    }


def product(left, right):
    return jnp.dot(left, right, preferred_element_type=jnp.float32)


def swap_halves(values):
    return pltpu.roll(values, NZ, values.ndim - 1)


def low_half(shape):
    return lax.broadcasted_iota(jnp.int32, shape, len(shape) - 1) < NZ


def masks_of(sampling):
    pattern = sampling.astype(jnp.float32)
    other = swap_halves(pattern)
    low = low_half(pattern.shape)
    return jnp.where(low, pattern, other), jnp.where(low, other, pattern)


def coil_factors(maps):
    other = swap_halves(maps)
    low = low_half(maps.shape)
    return jnp.where(low, maps, other), jnp.where(low, -other, maps)


def kspace_back(masked, xi):
    return product(xi, masked).astype(jnp.bfloat16)


def first_step(kspace, sampling, order, xi):
    columns = []
    for comp in range(kspace.shape[0]):
        masks = masks_of(sampling[comp])
        for pair in range(PAIRS):
            both = jnp.concatenate([kspace[comp, 2 * pair], kspace[comp, 2 * pair + 1]], 1)
            ordered = product(both, order)
            rows = [
                ordered[:, part * LANES : (part + 1) * LANES] * masks[part // 2]
                for part in range(4)
            ]
            columns.append(jnp.concatenate(rows, 0).astype(jnp.bfloat16))
    return kspace_back(jnp.concatenate(columns, 1), xi)


def kspace_step(portion, sampling, xf, xi):
    spectrum = product(xf, portion)
    columns = []
    for comp in range(sampling.shape[0]):
        masks = masks_of(sampling[comp])
        for pair in range(PAIRS):
            at = (comp * PAIRS + pair) * LANES
            rows = [
                spectrum[part * NX : (part + 1) * NX, at : at + LANES] * masks[part // 2]
                for part in range(4)
            ]
            columns.append(jnp.concatenate(rows, 0).astype(jnp.bfloat16))
    return kspace_back(jnp.concatenate(columns, 1), xi)


def combine_coils(arrived, factors, yi, zi):
    rows = product(yi, arrived).astype(jnp.bfloat16)
    images = []
    for comp in range(arrived.shape[1] // (PAIRS * LANES)):
        total = None
        for pair in range(PAIRS):
            at = (comp * PAIRS + pair) * LANES
            both = jnp.concatenate(
                [rows[: 2 * NY, at : at + LANES], rows[2 * NY :, at : at + LANES]], 1
            )
            depth = product(both, zi)
            for coil in range(2):
                real_map, turn_map = factors[2 * pair + coil]
                image = depth[:, coil * LANES : (coil + 1) * LANES]
                term = real_map * image - turn_map * swap_halves(image)
                total = term if total is None else total + term
        images.append(total)
    return images


def spread_out(images, factors, zf, yf):
    columns = []
    for image in images:
        turned = swap_halves(image)
        for pair in range(PAIRS):
            both = jnp.concatenate(
                [
                    (real_map * image + turn_map * turned).astype(jnp.bfloat16)
                    for real_map, turn_map in factors[2 * pair : 2 * pair + 2]
                ],
                1,
            )
            depth = product(both, zf).astype(jnp.bfloat16)
            columns.append(jnp.concatenate([depth[:, :LANES], depth[:, LANES:]], 0))
    return product(yf, jnp.concatenate(columns, 1)).astype(jnp.bfloat16)


def partial_dot(left, right):
    total = None
    for one, other in zip(left, right):
        folded = (one * other).reshape(-1, 8, LANES).sum(0)
        total = folded if total is None else total + folded
    return total


def first_kernel(kspace, sampling, order, xi, out):
    out[...] = first_step(kspace[...], sampling[...], order[...], xi[...])


def kspace_kernel(portion, sampling, xf, xi, out):
    out[...] = kspace_step(portion[...], sampling[...], xf[...], xi[...])


def image_kernel(*refs, earlier, onward):
    refs = list(refs)
    arrived, coils, yi, zi = refs[:4]
    refs = refs[4:]
    old = [refs.pop(0) for _ in range(earlier)]
    if onward:
        zf, yf = refs.pop(0), refs.pop(0)
    image_out, dots_out = refs[:2]
    factors = [coil_factors(coils[coil]) for coil in range(COILS)]
    images = combine_coils(arrived[...], factors, yi[...], zi[...])
    if onward:
        refs[2][...] = spread_out(images, factors, zf[...], yf[...])
    for comp, image in enumerate(images):
        image_out[comp] = image
    for place in range(earlier):
        dots_out[place] = partial_dot([old[place][comp] for comp in range(len(images))], images)
    if onward:
        dots_out[earlier] = partial_dot(images, images)


def call(body, operands, shapes, flops):
    held = sum(math.prod(o.shape) * o.dtype.itemsize for o in operands)
    held += sum(math.prod(s.shape) * s.dtype.itemsize for s in shapes)
    return pl.pallas_call(
        body,
        out_shape=shapes,
        in_specs=[pl.BlockSpec(memory_space=pltpu.VMEM)] * len(operands),
        out_specs=[pl.BlockSpec(memory_space=pltpu.VMEM)] * len(shapes),
        compiler_params=pltpu.CompilerParams(vmem_limit_bytes=32 * 1024 * 1024),
        cost_estimate=pl.CostEstimate(flops=flops, bytes_accessed=held, transcendentals=0),
    )(*operands)


def exchange(values):
    return lax.all_to_all(values, "slab", split_axis=0, concat_axis=0, tiled=True)


def total_of(values):
    devices = lax.axis_size("slab") * lax.axis_size("comp")
    row = jnp.zeros((1, 1, LANES), jnp.float32).at[0, 0, : values.shape[0]].set(values)
    handed = jnp.broadcast_to(row, (devices, 1, LANES))
    gathered = lax.all_to_all(handed, ("slab", "comp"), split_axis=0, concat_axis=0, tiled=True)
    return gathered.sum((0, 1))[: values.shape[0]]


def shards(kspace, sensitivities, sampling):
    comps_here = kspace.shape[0]
    tables = make_tables()
    tables = {name: jnp.asarray(value) for name, value in tables.items()}
    coils = sensitivities.reshape(COILS, 2, NY, LANES).transpose(0, 2, 1, 3)
    coils = coils.reshape(COILS, 2 * NY, LANES)
    starts = range(0, comps_here, CHUNK)
    patterns = [sampling[start : start + CHUNK] for start in starts]
    width = CHUNK * PAIRS * LANES
    sent_shape = jax.ShapeDtypeStruct((4 * NX, width), jnp.bfloat16)
    image_shape = jax.ShapeDtypeStruct((CHUNK, 2 * NY, LANES), jnp.float32)
    square = 2 * (4 * NX) * (4 * NX) * width

    def image_step(arrived, old, onward):
        operands = [arrived, coils, tables["yi"], tables["zi"], *old]
        shapes = [image_shape]
        shapes.append(jax.ShapeDtypeStruct((len(old) + onward, 8, LANES), jnp.float32))
        if onward:
            operands += [tables["zf"], tables["yf"]]
            shapes.append(sent_shape)
        body = functools.partial(image_kernel, earlier=len(old), onward=onward)
        return call(body, operands, shapes, 3 * square)

    sent = [
        call(
            first_kernel,
            [kspace[start : start + CHUNK], pattern, tables["order"], tables["xi"]],
            [sent_shape],
            2 * square,
        )[0]
        for start, pattern in zip(starts, patterns)
    ]
    chains = [[] for _ in starts]
    dots = [[] for _ in starts]
    for stage in range(3):
        if stage > 0:
            arrived = [exchange(values) for values in sent]
            sent = [
                call(kspace_kernel, [values, pattern, tables["xf"], tables["xi"]], [sent_shape], 2 * square)[0]
                for values, pattern in zip(arrived, patterns)
            ]
        arrived = [exchange(values) for values in sent]
        sent = []
        for place, values in enumerate(arrived):
            image, dot, *more = image_step(values, chains[place], stage < 2)
            chains[place].append(image)
            dots[place].append(dot)
            sent += more
    here = sum(jnp.concatenate(dot, 0) for dot in dots).sum((1, 2))
    bb, bq, qq, bt, qt = total_of(here)
    step_one = bb / bq
    norm_next = bb - 2.0 * step_one * bq + step_one * step_one * qq
    ratio = norm_next / bb
    more = 1.0 + ratio
    curve = more * more * bq - more * step_one * (bt + qq) + step_one * step_one * qt
    step_two = norm_next / curve
    images = [jnp.concatenate([chain[power] for chain in chains], 0) for power in range(3)]
    images = [
        image.reshape(comps_here, NY, 2, LANES).transpose(0, 2, 1, 3).reshape(comps_here, 2, -1)
        for image in images
    ]
    b, q, t = images
    along_b, along_q = step_one + step_two * more, step_two * step_one
    coefficients = along_b * b - along_q * q
    residual = b - along_b * q + along_q * t
    return (coefficients, residual)


def solution(mesh):
    in_specs = (P("comp", None, None, "slab"), P(None, "slab", None), P("comp", None, "slab"))
    out_specs = (P("comp", "slab", None), P("comp", "slab", None))
    return jax.shard_map(shards, mesh=mesh, in_specs=in_specs, out_specs=out_specs, check_vma=False)
```

time: 864 us -> 194 us (0.22)
  local copies, waits for them, and re-layouts: 397 us -> 4.92 us
  starting transfers between devices: 112 us -> 0 us
  waiting for transfers between devices: 88.2 us -> 0 us
  blocking collectives: 222 us -> 171 us
  other arithmetic: 16.2 us -> 1.14 us
  matrix products: 13.7 us -> 0 us
    psum x3 -> x0, blocking collectives: 222 us -> none  [the longest x2 149 us: squared_total(): return lax.psum(jnp.sum(residual * residual), ('slab', 'comp'))]
    unnamed x59 -> x24, local copies, waits for them, and re-layouts: 221 us -> 4.18 us
    all_to_all x0 -> x6, blocking collectives: none -> 171 us  [the longest x5 150 us: exchange(): lax.all_to_all(values, 'slab', split_axis=0, concat_axis=0, tiled=True)]
    all_to_all x13 -> x0, starting transfers between devices: 112 us -> none  [the longest x6 55.7 us: shards(): lax.all_to_all(section_two[position:position + 1], 'slab', split_axis=3,...]
    all_to_all x13 -> x0, waiting for transfers between devices: 88.2 us -> none  [the longest x6 69 us: kspace_step(): lax.all_to_all(restored, 'slab', split_axis=2, concat_axis=3, tiled=True)]
    slice x22 -> x0, local copies, waits for them, and re-layouts: 85.3 us -> none  [the longest x20 83.6 us: shards(): section_two[position:position + 1]]
    all_to_all x25 -> x0, local copies, waits for them, and re-layouts: 74.2 us -> none  [the longest x12 73.4 us: shards(): lax.all_to_all(section_two[position:position + 1], 'slab', split_axis=3,...]
    dot_general x41 -> x0, matrix products: 13.7 us -> none  [the longest x13 4.74 us: along_first(): jnp.einsum('kx,nxw->nkw', imag_matrix, flattened, preferred_element_type=...]
  transfers between devices with their start and end apart: 13 -> 0, of which waited for: 7 -> 0; matrix products, arithmetic and copies ran while one was open for 31% -> 0% of each run, Pallas kernels for 0% -> 0%
where the time goes in v1:
time: 194 us; the launch traced here: 192 us
  blocking collectives  171 us (88%)
  Pallas kernels  8.2 us (4%)
  between operations  7.02 us (4%)
  local copies, waits for them, and re-layouts  4.92 us (3%)
    all_to_all x5, blocking collectives, exchange(): lax.all_to_all(values, 'slab', split_axis=0, concat_axis=0, tiled=True)  150 us
    all_to_all x1, blocking collectives, total_of(): lax.all_to_all(handed, ('slab', 'comp'), split_axis=0, concat_axis=0, til...  20.3 us
    pallas_call x6, Pallas kernels, call(): pl.pallas_call(body, out_shape=shapes, in_specs=[pl.BlockSpec(memory_spac...  8.2 us
    unnamed x24, local copies, waits for them, and re-layouts  4.18 us

profile of v1, /device:TPU:2, one launch (start us, length us, event | category | flops | bytes accessed | tf_op | source)
XLA Modules:
  0.0 192.0 jit_solution(214006254534867659)
XLA Ops:
  0.6 0.0 copy-start
  0.6 1.1 copy-done
  1.8 0.9 copy-done.2
  2.7 1.0 copy-done.5
  3.7 1.0 copy-done.9
  4.8 1.0 shard_map.113
  5.8 0.0 copy-start.1
  5.8 0.0 copy-start.4
  5.8 0.0 copy-start.8
  5.8 35.1 %all_to_all.60 = bf16[64,8,768]{2,1,0:T(8,128)(2,1)S(1)} all-to-all(bf16[64,8,768]{2,1,0:T(8,128)(2,1)S(1)} %bitcast.38), channel_id=1, replica_groups=mesh['slab'=64,'comp'=4] {'slab'}, dimensions={0} | all-to-all | bytes 1572864 | tf_op jit(solution)/shard_map/all_to_all | solution.py:207
  40.9 0.0 copy-done.10
  40.9 0.0 copy-done.11
  40.9 0.0 copy-done.1
  41.0 0.0 copy-done.4
  41.0 2.0 %shard_map.114 = (f32[3,256,128]{2,1,0:T(8,128)S(1)}, f32[1,8,128]{2,1,0:T(8,128)S(1)}, bf16[512,768]{1,0:T(8,128)(2,1)S(1)}) custom-call(bf16[512,768]{1,0:T(8,128)(2,1)S(1)} %bitcast.34, f32[4,256,128]{2,1,0:T(8,128)S(1)} %bitcast.41, bf16[512,512]{1,0:T(8,128)(2,1)S(1)} %copy-done.4, bf16[256,256]{1,0:T(8,128)(2,1)S(1)} %copy-done.10, ...), custom_call_target="tpu_custom_call" | custom-call | flops 1207959552 | bytes 3805184 | tf_op jit(solution)/shard_map/pallas_call | solution.py:196
  43.0 0.0 copy-start.3
  43.0 0.0 copy-start.6
  43.0 0.0 copy-start.7
  43.1 28.9 %all_to_all.61 = bf16[64,8,768]{2,1,0:T(8,128)(2,1)S(1)} all-to-all(bf16[64,8,768]{2,1,0:T(8,128)(2,1)S(1)} %bitcast.35), channel_id=1, replica_groups=mesh['slab'=64,'comp'=4] {'slab'}, dimensions={0} | all-to-all | bytes 1572864 | tf_op jit(solution)/shard_map/all_to_all | solution.py:207
  72.0 0.0 copy-done.7
  72.0 1.0 shard_map.115
  73.0 28.8 %all_to_all.62 = bf16[64,8,768]{2,1,0:T(8,128)(2,1)S(1)} all-to-all(bf16[64,8,768]{2,1,0:T(8,128)(2,1)S(1)} %bitcast.40), channel_id=1, replica_groups=mesh['slab'=64,'comp'=4] {'slab'}, dimensions={0} | all-to-all | bytes 1572864 | tf_op jit(solution)/shard_map/all_to_all | solution.py:207
  101.8 2.0 %shard_map.116 = (f32[3,256,128]{2,1,0:T(8,128)S(1)}, f32[2,8,128]{2,1,0:T(8,128)S(1)}, bf16[512,768]{1,0:T(8,128)(2,1)S(1)}) custom-call(bf16[512,768]{1,0:T(8,128)(2,1)S(1)} %bitcast.31, f32[4,256,128]{2,1,0:T(8,128)S(1)} %bitcast.42, bf16[512,512]{1,0:T(8,128)(2,1)S(1)} %copy-done.4, bf16[256,256]{1,0:T(8,128)(2,1)S(1)} %copy-done.10, ...), custom_call_target="tpu_custom_call" | custom-call | flops 1207959552 | bytes 4202496 | tf_op jit(solution)/shard_map/pallas_call | solution.py:196
  103.9 28.8 %all_to_all.63 = bf16[64,8,768]{2,1,0:T(8,128)(2,1)S(1)} all-to-all(bf16[64,8,768]{2,1,0:T(8,128)(2,1)S(1)} %bitcast.32), channel_id=1, replica_groups=mesh['slab'=64,'comp'=4] {'slab'}, dimensions={0} | all-to-all | bytes 1572864 | tf_op jit(solution)/shard_map/all_to_all | solution.py:207
  132.7 1.0 shard_map.117
  133.7 28.8 %all_to_all.64 = bf16[64,8,768]{2,1,0:T(8,128)(2,1)S(1)} all-to-all(bf16[64,8,768]{2,1,0:T(8,128)(2,1)S(1)} %bitcast.37), channel_id=1, replica_groups=mesh['slab'=64,'comp'=4] {'slab'}, dimensions={0} | all-to-all | bytes 1572864 | tf_op jit(solution)/shard_map/all_to_all | solution.py:207
  162.5 1.0 shard_map.118
  163.6 0.1 maximum_reduce_fusion
  163.7 0.1 broadcast_in_dim.2
  163.8 20.3 %all_to_all.65 = f32[256,1,128]{2,1,0:T(1,128)S(1)} all-to-all(f32[256,1,128]{2,1,0:T(1,128)S(1)} %broadcast_in_dim.2), channel_id=1, replica_groups=mesh['slab'=64,'comp'=4] {'slab','comp'}, dimensions={0} | all-to-all | bytes 262144 | tf_op jit(solution)/shard_map/all_to_all | solution.py:214
  184.1 0.7 fusion
  191.0 1.0 multiply_add_fusion
  (10 shorter events, 0.1 us)
Async XLA Ops:
  0.6 1.1 copy-start
  1.8 0.9 copy-start.2
  2.7 1.0 copy-start.5
  3.7 1.0 copy-start.9
  4.8 36.2 %copy-start.10 = (bf16[256,256]{1,0:T(8,128)(2,1)S(1)}, bf16[256,256]{1,0:T(8,128)(2,1)}, u32[]{:S(2)}) copy-start(bf16[256,256]{1,0:T(8,128)(2,1)} %constant.52.clone.refs_3_) | copy-start | bytes 393220
  4.8 36.2 %copy-start.11 = (bf16[256,256]{1,0:T(8,128)(2,1)S(1)}, bf16[256,256]{1,0:T(8,128)(2,1)}, u32[]{:S(2)}) copy-start(bf16[256,256]{1,0:T(8,128)(2,1)} %constant.51.clone.refs_4_.refs_5_) | copy-start | bytes 393220
  5.8 35.2 %copy-start.1 = (f32[4,2,16384]{2,1,0:T(2,128)S(1)}, f32[4,2,16384]{2,1,0:T(2,128)}, u32[]{:S(2)}) copy-start(f32[4,2,16384]{2,1,0:T(2,128)} %param.13) | copy-start | bytes 1572868
  5.8 35.2 %copy-start.4 = (bf16[512,512]{1,0:T(8,128)(2,1)S(1)}, bf16[512,512]{1,0:T(8,128)(2,1)}, u32[]{:S(2)}) copy-start(bf16[512,512]{1,0:T(8,128)(2,1)} %constant.54.clone.refs_2_) | copy-start | bytes 1572868
  5.8 35.2 %copy-start.8 = (bf16[512,512]{1,0:T(8,128)(2,1)S(1)}, bf16[512,512]{1,0:T(8,128)(2,1)}, u32[]{:S(2)}) copy-start(bf16[512,512]{1,0:T(8,128)(2,1)} %constant.53.clone.refs_5_.refs_6_) | copy-start | bytes 1572868
  43.0 29.0 %copy-start.3 = (s32[3,128,128]{2,1,0:T(8,128)S(1)}, s32[3,128,128]{2,1,0:T(8,128)}, u32[]{:S(2)}) copy-start(s32[3,128,128]{2,1,0:T(8,128)} %sampling.5) | copy-start | bytes 589828
  43.0 29.0 %copy-start.6 = (bf16[512,512]{1,0:T(8,128)(2,1)S(1)}, bf16[512,512]{1,0:T(8,128)(2,1)}, u32[]{:S(2)}) copy-start(bf16[512,512]{1,0:T(8,128)(2,1)} %constant.56.clone.xi) | copy-start | bytes 1572868
  43.0 28.9 %copy-start.7 = (bf16[512,512]{1,0:T(8,128)(2,1)S(1)}, bf16[512,512]{1,0:T(8,128)(2,1)}, u32[]{:S(2)}) copy-start(bf16[512,512]{1,0:T(8,128)(2,1)} %constant.55.clone.xf) | copy-start | bytes 1572868

commit v2 on v1

v2 whole, which is shorter than its diff:
```python
import math

import jax
import jax.numpy as jnp
import numpy as np
from jax import lax
from jax.experimental import pallas as pl
from jax.experimental.pallas import tpu as pltpu
from jax.sharding import PartitionSpec as P

NX = 128
NY = 128
NZ = 64
COILS = 4
PAIRS = COILS // 2
LANES = 2 * NZ


def fourier_blocks(length, orientation):
    positions = np.arange(length)
    angles = (positions[:, None] * positions[None, :] % length) * (2.0 * math.pi / length)
    scaling = 1.0 / math.sqrt(length)
    real_part = np.cos(angles) * scaling
    imaginary = orientation * np.sin(angles) * scaling
    top_rows = np.stack([real_part, -imaginary], 1)
    low_rows = np.stack([imaginary, real_part], 1)
    return np.stack([top_rows, low_rows], 0).astype(np.float32)


def table(spec, *factors, shape):
    return np.einsum(spec, *factors).reshape(shape).astype(jnp.bfloat16)


def make_tables():
    two = np.eye(2, dtype=np.float32)
    slabs = NX // 2
    zf, zi = fourier_blocks(NZ, -1.0), fourier_blocks(NZ, 1.0)
    yf, yi = fourier_blocks(NY, -1.0), fourier_blocks(NY, 1.0)
    xf = fourier_blocks(NX, -1.0).reshape(2, NX, 2, slabs, 2)
    xi = fourier_blocks(NX, 1.0).reshape(2, slabs, 2, 2, NX)
    return {
        "zf": table("akbj,cd->cbjadk", zf, two, shape=(4 * NZ, 4 * NZ)),
        "zi": table("akbj,cd->bcjdak", zi, two, shape=(4 * NZ, 4 * NZ)),
        "yf": table("akbj,cd->kcabjd", yf, two, shape=(4 * NY, 4 * NY)),
        "yi": table("akbj,cd->akcjdb", yi, two, shape=(4 * NY, 4 * NY)),
        "xf": table("akbst,cd->caksdtb", xf, two, shape=(4 * NX, 4 * NX)),
        "xi": table("astbk,cd->sctadbk", xi, two, shape=(4 * NX, 4 * NX)),
        "order": table(
            "ab,ef,gh->aegfbh", two, two, np.eye(NZ, dtype=np.float32), shape=(4 * NZ, 4 * NZ)
        ),
    }


def product(left, right):
    return jnp.dot(left, right, preferred_element_type=jnp.float32)


def swap_halves(values):
    return pltpu.roll(values, NZ, values.ndim - 1)


def low_half(shape):
    return lax.broadcasted_iota(jnp.int32, shape, len(shape) - 1) < NZ


def masks_of(sampling):
    pattern = sampling.astype(jnp.float32)
    other = swap_halves(pattern)
    low = low_half(pattern.shape)
    return jnp.where(low, pattern, other), jnp.where(low, other, pattern)


def coil_factors(maps):
    other = swap_halves(maps)
    low = low_half(maps.shape)
    return jnp.where(low, maps, other), jnp.where(low, -other, maps)


def first_masked(kspace, sampling, order):
    masks = masks_of(sampling)
    columns = []
    for pair in range(PAIRS):
        rows = []
        for place in range(2):
            lanes = slice(place * LANES, (place + 1) * LANES)
            both = jnp.concatenate([kspace[2 * pair][:, lanes], kspace[2 * pair + 1][:, lanes]], 1)
            ordered = product(both, order)
            rows += [ordered[:, :LANES] * masks[place], ordered[:, LANES:] * masks[place]]
        columns.append(jnp.concatenate(rows, 0).astype(jnp.bfloat16))
    return jnp.concatenate(columns, 1)


def masked_spectrum(portion, sampling, xf):
    spectrum = product(xf, portion)
    columns = []
    for comp in range(sampling.shape[0]):
        masks = masks_of(sampling[comp])
        for pair in range(PAIRS):
            at = (comp * PAIRS + pair) * LANES
            rows = [
                spectrum[part * NX : (part + 1) * NX, at : at + LANES] * masks[part // 2]
                for part in range(4)
            ]
            columns.append(jnp.concatenate(rows, 0).astype(jnp.bfloat16))
    return jnp.concatenate(columns, 1)


def combine_coils(arrived, factors, yi, zi):
    rows = product(yi, arrived).astype(jnp.bfloat16)
    images = []
    for comp in range(arrived.shape[1] // (PAIRS * LANES)):
        total = None
        for pair in range(PAIRS):
            at = (comp * PAIRS + pair) * LANES
            both = jnp.concatenate(
                [rows[: 2 * NY, at : at + LANES], rows[2 * NY :, at : at + LANES]], 1
            )
            depth = product(both, zi)
            for coil in range(2):
                real_map, turn_map = factors[2 * pair + coil]
                image = depth[:, coil * LANES : (coil + 1) * LANES]
                term = real_map * image - turn_map * swap_halves(image)
                total = term if total is None else total + term
        images.append(total)
    return images


def spread_out(images, factors, zf, yf):
    columns = []
    for image in images:
        turned = swap_halves(image)
        for pair in range(PAIRS):
            both = jnp.concatenate(
                [
                    (real_map * image + turn_map * turned).astype(jnp.bfloat16)
                    for real_map, turn_map in factors[2 * pair : 2 * pair + 2]
                ],
                1,
            )
            depth = product(both, zf).astype(jnp.bfloat16)
            columns.append(jnp.concatenate([depth[:, :LANES], depth[:, LANES:]], 0))
    return product(yf, jnp.concatenate(columns, 1)).astype(jnp.bfloat16)


def fold_rows(values):
    rows = values.sum(0, keepdims=True)
    return sum(rows[:, at : at + LANES] for at in range(0, rows.shape[1], LANES))


def row_of(one, other):
    return fold_rows(one.astype(jnp.float32) * other.astype(jnp.float32))


def final_scales(sums):
    totals = sums.sum(1, keepdims=True)
    bb, bq, qq, bt, qt = (totals[place : place + 1] for place in range(5))
    step_one = bb / bq
    norm_next = bb - 2.0 * step_one * bq + step_one * step_one * qq
    more = 1.0 + norm_next / bb
    curve = more * more * bq - more * step_one * (bt + qq) + step_one * step_one * qt
    step_two = norm_next / curve
    return step_one + step_two * more, step_two * step_one


def first_kernel(kspace_at, sampling_at, order_at, xi_at, out, kspace, sampling, order, xi, sems):
    copies = [pltpu.make_async_copy(order_at, order, sems.at[0])]
    copies.append(pltpu.make_async_copy(sampling_at, sampling, sems.at[1]))
    for comp in range(kspace.shape[0]):
        copies.append(pltpu.make_async_copy(kspace_at.at[comp], kspace.at[comp], sems.at[2 + comp]))
    copies.append(pltpu.make_async_copy(xi_at, xi, sems.at[2 + kspace.shape[0]]))
    for copy in copies:
        copy.start()
    copies[0].wait()
    copies[1].wait()
    columns = []
    for comp in range(kspace.shape[0]):
        copies[2 + comp].wait()
        columns.append(first_masked(kspace[comp], sampling[comp], order[...]))
    copies[-1].wait()
    out[...] = product(xi[...], jnp.concatenate(columns, 1)).astype(jnp.bfloat16)


def kspace_kernel(portion, sampling, xf, xi, out, masked_out, sum_out):
    masked = masked_spectrum(portion[...], sampling[...], xf[...])
    masked_out[...] = masked
    sum_out[...] = row_of(masked, masked)
    out[...] = product(xi[...], masked).astype(jnp.bfloat16)


def kspace_last_kernel(portion, sampling, xf, xi, masked_b, bb, bq, qq, out, sums_out):
    masked = masked_spectrum(portion[...], sampling[...], xf[...])
    out[...] = product(xi[...], masked).astype(jnp.bfloat16)
    sums_out[0:1] = bb[...]
    sums_out[1:2] = bq[...]
    sums_out[2:3] = qq[...]
    sums_out[3:4] = row_of(masked_b[...], masked)
    sums_out[4:5] = row_of(masked, masked)
    sums_out[5:8] = jnp.zeros((3, LANES), jnp.float32)


def image_kernel(arrived, coils, yi, zi, zf, yf, image_out, sum_out, out):
    factors = [coil_factors(coils[coil]) for coil in range(COILS)]
    images = combine_coils(arrived[...], factors, yi[...], zi[...])
    out[...] = spread_out(images, factors, zf[...], yf[...])
    for comp, image in enumerate(images):
        image_out[comp] = image
    sum_out[...] = sum(row_of(image, image) for image in images)


def last_kernel(arrived, coils, yi, zi, b, q, sums, coefficients, residual):
    factors = [coil_factors(coils[coil]) for coil in range(COILS)]
    images = combine_coils(arrived[...], factors, yi[...], zi[...])
    along_b, along_q = final_scales(sums[...])
    for comp, image in enumerate(images):
        coefficients[comp] = along_b * b[comp] - along_q * q[comp]
        residual[comp] = b[comp] - along_b * q[comp] + along_q * image


def call(body, operands, shapes, flops, space=pltpu.VMEM, scratch=()):
    held = sum(math.prod(o.shape) * o.dtype.itemsize for o in operands)
    held += sum(math.prod(s.shape) * s.dtype.itemsize for s in shapes)
    return pl.pallas_call(
        body,
        out_shape=shapes,
        in_specs=[pl.BlockSpec(memory_space=space)] * len(operands),
        out_specs=[pl.BlockSpec(memory_space=pltpu.VMEM)] * len(shapes),
        scratch_shapes=scratch,
        compiler_params=pltpu.CompilerParams(vmem_limit_bytes=32 * 1024 * 1024),
        cost_estimate=pl.CostEstimate(flops=flops, bytes_accessed=held, transcendentals=0),
    )(*operands)


def exchange(values):
    return lax.all_to_all(values, "slab", split_axis=0, concat_axis=0, tiled=True)


def exclusive(axis, flips):
    return [(place, place ^ flips) for place in range(lax.axis_size(axis))]


def total_of(values):
    for axis, low in (("comp", 1), ("slab", 1), ("slab", 4), ("slab", 16)):
        one, two, three = (
            lax.ppermute(values, axis, exclusive(axis, flips * low)) for flips in (1, 2, 3)
        )
        values = (values + one) + (two + three)
    return values


def shards(kspace, sensitivities, sampling):
    comps = kspace.shape[0]
    tables = {name: jnp.asarray(value) for name, value in make_tables().items()}
    coils = sensitivities.reshape(COILS, 2, NY, LANES).transpose(0, 2, 1, 3)
    coils = coils.reshape(COILS, 2 * NY, LANES)
    width = comps * PAIRS * LANES
    sent_shape = jax.ShapeDtypeStruct((4 * NX, width), jnp.bfloat16)
    image_shape = jax.ShapeDtypeStruct((comps, 2 * NY, LANES), jnp.float32)
    sum_shape = jax.ShapeDtypeStruct((1, LANES), jnp.float32)
    sums_shape = jax.ShapeDtypeStruct((8, LANES), jnp.float32)
    square = 2 * (4 * NX) * (4 * NX) * width

    def image_step(arrived):
        operands = [arrived, coils] + [tables[name] for name in ("yi", "zi", "zf", "yf")]
        return call(image_kernel, operands, [image_shape, sum_shape, sent_shape], 3 * square)

    first = [kspace, sampling, tables["order"], tables["xi"]]
    scratch = [pltpu.VMEM(array.shape, array.dtype) for array in first]
    scratch.append(pltpu.SemaphoreType.DMA((3 + comps,)))
    (sent,) = call(first_kernel, first, [sent_shape], 2 * square, pltpu.HBM, scratch)
    b, bb, sent = image_step(exchange(sent))
    operands = [exchange(sent), sampling, tables["xf"], tables["xi"]]
    sent, masked_b, bq = call(
        kspace_kernel, operands, [sent_shape, sent_shape, sum_shape], 2 * square
    )
    q, qq, sent = image_step(exchange(sent))
    operands = [exchange(sent), sampling, tables["xf"], tables["xi"], masked_b, bb, bq, qq]
    sent, sums = call(kspace_last_kernel, operands, [sent_shape, sums_shape], 2 * square)
    arrived = exchange(sent)
    operands = [arrived, coils, tables["yi"], tables["zi"], b, q, total_of(sums)]
    outputs = call(last_kernel, operands, [image_shape] * 2, 2 * square)
    return tuple(
        output.reshape(comps, NY, 2, LANES).transpose(0, 2, 1, 3).reshape(comps, 2, -1)
        for output in outputs
    )


def solution(mesh):
    in_specs = (P("comp", None, None, "slab"), P(None, "slab", None), P("comp", None, "slab"))
    out_specs = (P("comp", "slab", None), P("comp", "slab", None))
    return jax.shard_map(shards, mesh=mesh, in_specs=in_specs, out_specs=out_specs, check_vma=False)
```

time: 194 us -> 176 us (0.907)
  blocking collectives: 171 us -> 122 us
  starting transfers between devices: 0 us -> 23.6 us
  waiting for transfers between devices: 0 us -> 14.4 us
  between operations: 7.02 us -> 0.79 us
  Pallas kernels: 8.2 us -> 10.9 us
    all_to_all x5 -> x4, blocking collectives: 150 us -> 122 us  [exchange(): lax.all_to_all(values, 'slab', split_axis=0, concat_axis=0, tiled=True)]
    all_to_all x1 -> x0, blocking collectives: 20.3 us -> none  [total_of(): lax.all_to_all(handed, ('slab', 'comp'), split_axis=0, concat_axis=0, til...]
    ppermute x0 -> x12, starting transfers between devices: none -> 17.7 us  [total_of(): lax.ppermute(values, axis, exclusive(axis, flips * low))]
    ppermute x0 -> x12, waiting for transfers between devices: none -> 14.4 us  [total_of(): lax.ppermute(values, axis, exclusive(axis, flips * low))]
    all_to_all x0 -> x1, starting transfers between devices: none -> 5.81 us  [exchange(): lax.all_to_all(values, 'slab', split_axis=0, concat_axis=0, tiled=True)]
    pallas_call x6, Pallas kernels: 8.2 us -> 10.9 us  [call(): pl.pallas_call(body, out_shape=shapes, in_specs=[pl.BlockSpec(memory_spac...]
  transfers between devices with their start and end apart: 0 -> 13, of which waited for: 0 -> 7; matrix products, arithmetic and copies ran while one was open for 0% -> 0% of each run, Pallas kernels for 0% -> 0%
where the time goes in v2:
time: 176 us; the launch traced here: 175 us
  blocking collectives  122 us (69%)
  starting transfers between devices  23.6 us (13%)
  waiting for transfers between devices  14.4 us (8%)
  Pallas kernels  10.9 us (6%)
  local copies, waits for them, and re-layouts  4.04 us (2%)
    all_to_all x4, blocking collectives, exchange(): lax.all_to_all(values, 'slab', split_axis=0, concat_axis=0, tiled=True)  122 us
    ppermute x12, starting transfers between devices, total_of(): lax.ppermute(values, axis, exclusive(axis, flips * low))  17.7 us
    ppermute x12, waiting for transfers between devices, total_of(): lax.ppermute(values, axis, exclusive(axis, flips * low))  14.4 us
    pallas_call x6, Pallas kernels, call(): pl.pallas_call(body, out_shape=shapes, in_specs=[pl.BlockSpec(memory_spac...  10.9 us
    all_to_all x1, starting transfers between devices, exchange(): lax.all_to_all(values, 'slab', split_axis=0, concat_axis=0, tiled=True)  5.81 us
    unnamed x24, local copies, waits for them, and re-layouts  4.04 us
  transfers between devices with their start and end apart: 13, of which 7 were waited for; matrix products, arithmetic and copies ran while one was open for 0% of the time, Pallas kernels for 0%

profile of v2, /device:TPU:2, one launch (start us, length us, event | category | flops | bytes accessed | tf_op | source)
XLA Modules:
  0.0 175.3 jit_solution(4833268400434465725)
XLA Ops:
  0.6 1.1 copy-done
  1.8 0.9 copy-done.2
  2.7 1.0 copy-done.5
  3.7 0.9 copy-done.11
  4.6 1.8 %shard_map.113 = bf16[512,768]{1,0:T(8,128)(2,1)S(1)} custom-call(bf16[3,4,128,256]{3,2,1,0:T(8,128)(2,1)S(1)} %copy-done, s32[3,128,128]{2,1,0:T(8,128)S(1)} %copy-done.2, bf16[256,256]{1,0:T(8,128)(2,1)S(1)} %copy-done.11, bf16[512,512]{1,0:T(8,128)(2,1)S(1)} %copy-done.5), custom_call_target="tpu_custom_call" | custom-call | flops 805306368 | bytes 2424832 | tf_op jit(solution)/shard_map/pallas_call | solution.py:222
  6.5 35.1 %all_to_all.55 = bf16[64,8,768]{2,1,0:T(8,128)(2,1)S(1)} all-to-all(bf16[64,8,768]{2,1,0:T(8,128)(2,1)S(1)} %bitcast.33), channel_id=1, replica_groups=mesh['slab'=64,'comp'=4] {'slab'}, dimensions={0} | all-to-all | bytes 1572864 | tf_op jit(solution)/shard_map/all_to_all | solution.py:234
  41.7 2.0 %shard_map.114 = (f32[3,256,128]{2,1,0:T(8,128)S(1)}, f32[1,128]{1,0:T(1,128)S(1)}, bf16[512,768]{1,0:T(8,128)(2,1)S(1)}) custom-call(bf16[512,768]{1,0:T(8,128)(2,1)S(1)} %bitcast.29, f32[4,256,128]{2,1,0:T(8,128)S(1)} %bitcast.34, bf16[512,512]{1,0:T(8,128)(2,1)S(1)} %copy-done.4, bf16[256,256]{1,0:T(8,128)(2,1)S(1)} %copy-done.9, ...), custom_call_target="tpu_custom_call" | custom-call | flops 1207959552 | bytes 3801600 | tf_op jit(solution)/shard_map/pallas_call | solution.py:222
  43.8 28.9 %all_to_all.56 = bf16[64,8,768]{2,1,0:T(8,128)(2,1)S(1)} all-to-all(bf16[64,8,768]{2,1,0:T(8,128)(2,1)S(1)} %bitcast.30), channel_id=1, replica_groups=mesh['slab'=64,'comp'=4] {'slab'}, dimensions={0} | all-to-all | bytes 1572864 | tf_op jit(solution)/shard_map/all_to_all | solution.py:234
  72.7 1.0 shard_map.115
  73.8 28.8 %all_to_all.57 = bf16[64,8,768]{2,1,0:T(8,128)(2,1)S(1)} all-to-all(bf16[64,8,768]{2,1,0:T(8,128)(2,1)S(1)} %bitcast.32), channel_id=1, replica_groups=mesh['slab'=64,'comp'=4] {'slab'}, dimensions={0} | all-to-all | bytes 1572864 | tf_op jit(solution)/shard_map/all_to_all | solution.py:234
  102.5 2.0 %shard_map.116 = (f32[3,256,128]{2,1,0:T(8,128)S(1)}, f32[1,128]{1,0:T(1,128)S(1)}, bf16[512,768]{1,0:T(8,128)(2,1)S(1)}) custom-call(bf16[512,768]{1,0:T(8,128)(2,1)S(1)} %bitcast.27, f32[4,256,128]{2,1,0:T(8,128)S(1)} %bitcast.35, bf16[512,512]{1,0:T(8,128)(2,1)S(1)} %copy-done.4, bf16[256,256]{1,0:T(8,128)(2,1)S(1)} %copy-done.9, ...), custom_call_target="tpu_custom_call" | custom-call | flops 1207959552 | bytes 3801600 | tf_op jit(solution)/shard_map/pallas_call | solution.py:222
  104.6 28.8 %all_to_all.58 = bf16[64,8,768]{2,1,0:T(8,128)(2,1)S(1)} all-to-all(bf16[64,8,768]{2,1,0:T(8,128)(2,1)S(1)} %bitcast.28), channel_id=1, replica_groups=mesh['slab'=64,'comp'=4] {'slab'}, dimensions={0} | all-to-all | bytes 1572864 | tf_op jit(solution)/shard_map/all_to_all | solution.py:234
  133.4 2.0 %shard_map.117 = (bf16[512,768]{1,0:T(8,128)(2,1)}, f32[8,128]{1,0:T(8,128)S(1)}) custom-call(bf16[512,768]{1,0:T(8,128)(2,1)S(1)} %bitcast.26, s32[3,128,128]{2,1,0:T(8,128)S(1)} %copy-done.3, bf16[512,512]{1,0:T(8,128)(2,1)S(1)} %copy-done.7, bf16[512,512]{1,0:T(8,128)(2,1)S(1)} %copy-done.6, bf16[512,768]{1,0:T(8,128)(2,1)S(1)} %get-tuple-element.18.masked_b, ...), custom_call_target="tpu_custom_call" | custom-call | flops 805306368 | bytes 3610112 | tf_op jit(solution)/shard_map/pallas_call | solution.py:222
  135.4 5.8 %all-to-all-start.4 = ((bf16[64,8,768]{2,1,0:T(8,128)(2,1)}), bf16[64,8,768]{2,1,0:T(8,128)(2,1)S(1)}, u32[]{:S(2)}, u32[]{:S(2)}) async-start(bf16[64,8,768]{2,1,0:T(8,128)(2,1)} %bitcast.11), calls=%async_computation.4 | async-start | bytes 1572864 | tf_op jit(solution)/shard_map/all_to_all | solution.py:234
  141.2 3.1 %collective-permute-start.2 = (f32[8,128]{1,0:T(8,128)S(1)}, f32[8,128]{1,0:T(8,128)S(1)}, u32[]{:S(2)}, u32[]{:S(2)}) collective-permute-start(f32[8,128]{1,0:T(8,128)S(1)} %get-tuple-element.25), channel_id=1, source_target_pairs={{0,3},{1,2},{2,1},{3,0},{4,7},{5,6},{6,5},{7,4},{8,11},{9,10},{10,... | collective-permute-start | bytes 12296 | tf_op jit(solution)/shard_map/ppermute | solution.py:244
  144.3 0.6 collective-permute-start.1
  144.9 0.5 collective-permute-start
  145.4 0.7 collective-permute-done.2
  146.1 3.3 %collective-permute-done.1 = f32[8,128]{1,0:T(8,128)S(1)} collective-permute-done((f32[8,128]{1,0:T(8,128)S(1)}, f32[8,128]{1,0:T(8,128)S(1)}, u32[]{:S(2)}, u32[]{:S(2)}) %collective-permute-start.1) | collective-permute-done | bytes 4128 | tf_op jit(solution)/shard_map/ppermute | solution.py:244
  149.5 0.6 collective-permute-start.4
  150.1 1.2 collective-permute-start.3
  151.4 1.2 collective-permute-done.5
  152.6 0.7 collective-permute-done.4
  153.2 3.1 %collective-permute-start.8 = (f32[8,128]{1,0:T(8,128)S(1)}, f32[8,128]{1,0:T(8,128)S(1)}, u32[]{:S(2)}, u32[]{:S(2)}) collective-permute-start(f32[8,128]{1,0:T(8,128)S(1)} %add_add_fusion.2), channel_id=1, source_target_pairs={{0,48},{4,52},{8,56},{12,60},{16,32},{20,36},{24,40},{28,44},{32,1... | collective-permute-start | bytes 12296 | tf_op jit(solution)/shard_map/ppermute | solution.py:244
  156.3 0.9 collective-permute-start.7
  157.2 1.1 collective-permute-start.6
  158.3 3.5 %collective-permute-done.8 = f32[8,128]{1,0:T(8,128)S(1)} collective-permute-done((f32[8,128]{1,0:T(8,128)S(1)}, f32[8,128]{1,0:T(8,128)S(1)}, u32[]{:S(2)}, u32[]{:S(2)}) %collective-permute-start.8) | collective-permute-done | bytes 4128 | tf_op jit(solution)/shard_map/ppermute | solution.py:244
  162.3 3.5 %collective-permute-start.11 = (f32[8,128]{1,0:T(8,128)S(1)}, f32[8,128]{1,0:T(8,128)S(1)}, u32[]{:S(2)}, u32[]{:S(2)}) collective-permute-start(f32[8,128]{1,0:T(8,128)S(1)} %add_add_fusion.1), channel_id=1, source_target_pairs={{0,192},{4,196},{8,200},{12,204},{16,208},{20,212},{24,216},{28,22... | collective-permute-start | bytes 12296 | tf_op jit(solution)/shard_map/ppermute | solution.py:244
  165.8 2.1 %collective-permute-start.10 = (f32[8,128]{1,0:T(8,128)S(1)}, f32[8,128]{1,0:T(8,128)S(1)}, u32[]{:S(2)}, u32[]{:S(2)}) collective-permute-start(f32[8,128]{1,0:T(8,128)S(1)} %add_add_fusion.1), channel_id=1, source_target_pairs={{0,128},{4,132},{8,136},{12,140},{16,144},{20,148},{24,152},{28,15... | collective-permute-start | bytes 12296 | tf_op jit(solution)/shard_map/ppermute | solution.py:244
  168.0 0.8 collective-permute-start.9
  168.8 4.5 %collective-permute-done.10 = f32[8,128]{1,0:T(8,128)S(1)} collective-permute-done((f32[8,128]{1,0:T(8,128)S(1)}, f32[8,128]{1,0:T(8,128)S(1)}, u32[]{:S(2)}, u32[]{:S(2)}) %collective-permute-start.10) | collective-permute-done | bytes 4128 | tf_op jit(solution)/shard_map/ppermute | solution.py:244
  173.4 1.9 %shard_map.118 = (f32[3,256,128]{2,1,0:T(8,128)}, f32[3,256,128]{2,1,0:T(8,128)}) custom-call(bf16[512,768]{1,0:T(8,128)(2,1)S(1)} %bitcast.25, f32[4,256,128]{2,1,0:T(8,128)S(1)} %bitcast.36, bf16[512,512]{1,0:T(8,128)(2,1)S(1)} %copy-done.4, bf16[256,256]{1,0:T(8,128)(2,1)S(1)} %copy-done.9, f32[3,256,128]{2,1,0:T(8,128)S(1)} %get-tuple-element.23.b, ...), custom_call_target="tpu_custom_call" | custom-call | flops 805306368 | bytes 3543040 | tf_op jit(solution)/shard_map/pallas_call | solution.py:222
  (32 shorter events, 0.6 us)
Async XLA Ops:
  0.6 1.1 copy-start
  1.8 0.9 copy-start.2
  2.7 1.0 copy-start.5
  3.7 0.9 copy-start.11
  4.6 37.0 %copy-start.9 = (bf16[256,256]{1,0:T(8,128)(2,1)S(1)}, bf16[256,256]{1,0:T(8,128)(2,1)}, u32[]{:S(2)}) copy-start(bf16[256,256]{1,0:T(8,128)(2,1)} %constant.15.clone.zi) | copy-start | bytes 393220
  4.6 37.0 %copy-start.10 = (bf16[256,256]{1,0:T(8,128)(2,1)S(1)}, bf16[256,256]{1,0:T(8,128)(2,1)}, u32[]{:S(2)}) copy-start(bf16[256,256]{1,0:T(8,128)(2,1)} %constant.14.clone.zf) | copy-start | bytes 393220
  6.5 35.2 %copy-start.1 = (f32[4,2,16384]{2,1,0:T(2,128)S(1)}, f32[4,2,16384]{2,1,0:T(2,128)}, u32[]{:S(2)}) copy-start(f32[4,2,16384]{2,1,0:T(2,128)} %param.11) | copy-start | bytes 1572868
  6.5 35.2 %copy-start.4 = (bf16[512,512]{1,0:T(8,128)(2,1)S(1)}, bf16[512,512]{1,0:T(8,128)(2,1)}, u32[]{:S(2)}) copy-start(bf16[512,512]{1,0:T(8,128)(2,1)} %constant.17.clone.yi) | copy-start | bytes 1572868
  6.5 35.2 %copy-start.8 = (bf16[512,512]{1,0:T(8,128)(2,1)S(1)}, bf16[512,512]{1,0:T(8,128)(2,1)}, u32[]{:S(2)}) copy-start(bf16[512,512]{1,0:T(8,128)(2,1)} %constant.16.clone.yf) | copy-start | bytes 1572868
  43.7 29.0 %copy-start.3 = (s32[3,128,128]{2,1,0:T(8,128)S(1)}, s32[3,128,128]{2,1,0:T(8,128)}, u32[]{:S(2)}) copy-start(s32[3,128,128]{2,1,0:T(8,128)} %sampling.3) | copy-start | bytes 589828
  43.7 28.9 %copy-start.6 = (bf16[512,512]{1,0:T(8,128)(2,1)S(1)}, bf16[512,512]{1,0:T(8,128)(2,1)}, u32[]{:S(2)}) copy-start(bf16[512,512]{1,0:T(8,128)(2,1)} %constant.19.clone.xi_at.xi) | copy-start | bytes 1572868
  43.8 28.9 %copy-start.7 = (bf16[512,512]{1,0:T(8,128)(2,1)S(1)}, bf16[512,512]{1,0:T(8,128)(2,1)}, u32[]{:S(2)}) copy-start(bf16[512,512]{1,0:T(8,128)(2,1)} %constant.18.clone.xf) | copy-start | bytes 1572868
  135.4 38.0 %all-to-all-start.4 = ((bf16[64,8,768]{2,1,0:T(8,128)(2,1)}), bf16[64,8,768]{2,1,0:T(8,128)(2,1)S(1)}, u32[]{:S(2)}, u32[]{:S(2)}) async-start(bf16[64,8,768]{2,1,0:T(8,128)(2,1)} %bitcast.11), calls=%async_computation.4 | async-start | bytes 1572864 | tf_op jit(solution)/shard_map/all_to_all | solution.py:234
  141.2 4.9 %collective-permute-start.2 = (f32[8,128]{1,0:T(8,128)S(1)}, f32[8,128]{1,0:T(8,128)S(1)}, u32[]{:S(2)}, u32[]{:S(2)}) collective-permute-start(f32[8,128]{1,0:T(8,128)S(1)} %get-tuple-element.25), channel_id=1, source_target_pairs={{0,3},{1,2},{2,1},{3,0},{4,7},{5,6},{6,5},{7,4},{8,11},{9,10},{10,... | collective-permute-start | bytes 12296 | tf_op jit(solution)/shard_map/ppermute | solution.py:244
  144.3 5.1 %collective-permute-start.1 = (f32[8,128]{1,0:T(8,128)S(1)}, f32[8,128]{1,0:T(8,128)S(1)}, u32[]{:S(2)}, u32[]{:S(2)}) collective-permute-start(f32[8,128]{1,0:T(8,128)S(1)} %get-tuple-element.25), channel_id=1, source_target_pairs={{0,2},{1,3},{2,0},{3,1},{4,6},{5,7},{6,4},{7,5},{8,10},{9,11},{10,... | collective-permute-start | bytes 12296 | tf_op jit(solution)/shard_map/ppermute | solution.py:244
  144.9 4.5 %collective-permute-start = (f32[8,128]{1,0:T(8,128)S(1)}, f32[8,128]{1,0:T(8,128)S(1)}, u32[]{:S(2)}, u32[]{:S(2)}) collective-permute-start(f32[8,128]{1,0:T(8,128)S(1)} %get-tuple-element.25), channel_id=1, source_target_pairs={{0,1},{1,0},{2,3},{3,2},{4,5},{5,4},{6,7},{7,6},{8,9},{9,8},{10,11... | collective-permute-start | bytes 12296 | tf_op jit(solution)/shard_map/ppermute | solution.py:244
  149.4 3.2 %collective-permute-start.5 = (f32[8,128]{1,0:T(8,128)S(1)}, f32[8,128]{1,0:T(8,128)S(1)}, u32[]{:S(2)}, u32[]{:S(2)}) collective-permute-start(f32[8,128]{1,0:T(8,128)S(1)} %add_add_fusion.3), channel_id=1, source_target_pairs={{0,12},{4,8},{8,4},{12,0},{16,28},{20,24},{24,20},{28,16},{32,44},... | collective-permute-start | bytes 12296 | tf_op jit(solution)/shard_map/ppermute | solution.py:244
  149.5 3.7 %collective-permute-start.4 = (f32[8,128]{1,0:T(8,128)S(1)}, f32[8,128]{1,0:T(8,128)S(1)}, u32[]{:S(2)}, u32[]{:S(2)}) collective-permute-start(f32[8,128]{1,0:T(8,128)S(1)} %add_add_fusion.3), channel_id=1, source_target_pairs={{0,8},{4,12},{8,0},{12,4},{16,24},{20,28},{24,16},{28,20},{32,40},... | collective-permute-start | bytes 12296 | tf_op jit(solution)/shard_map/ppermute | solution.py:244
  150.1 3.1 %collective-permute-start.3 = (f32[8,128]{1,0:T(8,128)S(1)}, f32[8,128]{1,0:T(8,128)S(1)}, u32[]{:S(2)}, u32[]{:S(2)}) collective-permute-start(f32[8,128]{1,0:T(8,128)S(1)} %add_add_fusion.3), channel_id=1, source_target_pairs={{0,4},{4,0},{8,12},{12,8},{16,20},{20,16},{24,28},{28,24},{32,36},... | collective-permute-start | bytes 12296 | tf_op jit(solution)/shard_map/ppermute | solution.py:244
  153.2 8.6 %collective-permute-start.8 = (f32[8,128]{1,0:T(8,128)S(1)}, f32[8,128]{1,0:T(8,128)S(1)}, u32[]{:S(2)}, u32[]{:S(2)}) collective-permute-start(f32[8,128]{1,0:T(8,128)S(1)} %add_add_fusion.2), channel_id=1, source_target_pairs={{0,48},{4,52},{8,56},{12,60},{16,32},{20,36},{24,40},{28,44},{32,1... | collective-permute-start | bytes 12296 | tf_op jit(solution)/shard_map/ppermute | solution.py:244
  156.3 5.6 %collective-permute-start.7 = (f32[8,128]{1,0:T(8,128)S(1)}, f32[8,128]{1,0:T(8,128)S(1)}, u32[]{:S(2)}, u32[]{:S(2)}) collective-permute-start(f32[8,128]{1,0:T(8,128)S(1)} %add_add_fusion.2), channel_id=1, source_target_pairs={{0,32},{4,36},{8,40},{12,44},{16,48},{20,52},{24,56},{28,60},{32,0... | collective-permute-start | bytes 12296 | tf_op jit(solution)/shard_map/ppermute | solution.py:244
  157.2 5.1 %collective-permute-start.6 = (f32[8,128]{1,0:T(8,128)S(1)}, f32[8,128]{1,0:T(8,128)S(1)}, u32[]{:S(2)}, u32[]{:S(2)}) collective-permute-start(f32[8,128]{1,0:T(8,128)S(1)} %add_add_fusion.2), channel_id=1, source_target_pairs={{0,16},{4,20},{8,24},{12,28},{16,0},{20,4},{24,8},{28,12},{32,48},... | collective-permute-start | bytes 12296 | tf_op jit(solution)/shard_map/ppermute | solution.py:244
  162.3 6.5 %collective-permute-start.11 = (f32[8,128]{1,0:T(8,128)S(1)}, f32[8,128]{1,0:T(8,128)S(1)}, u32[]{:S(2)}, u32[]{:S(2)}) collective-permute-start(f32[8,128]{1,0:T(8,128)S(1)} %add_add_fusion.1), channel_id=1, source_target_pairs={{0,192},{4,196},{8,200},{12,204},{16,208},{20,212},{24,216},{28,22... | collective-permute-start | bytes 12296 | tf_op jit(solution)/shard_map/ppermute | solution.py:244
  165.8 7.5 %collective-permute-start.10 = (f32[8,128]{1,0:T(8,128)S(1)}, f32[8,128]{1,0:T(8,128)S(1)}, u32[]{:S(2)}, u32[]{:S(2)}) collective-permute-start(f32[8,128]{1,0:T(8,128)S(1)} %add_add_fusion.1), channel_id=1, source_target_pairs={{0,128},{4,132},{8,136},{12,140},{16,144},{20,148},{24,152},{28,15... | collective-permute-start | bytes 12296 | tf_op jit(solution)/shard_map/ppermute | solution.py:244
  168.0 5.4 %collective-permute-start.9 = (f32[8,128]{1,0:T(8,128)S(1)}, f32[8,128]{1,0:T(8,128)S(1)}, u32[]{:S(2)}, u32[]{:S(2)}) collective-permute-start(f32[8,128]{1,0:T(8,128)S(1)} %add_add_fusion.1), channel_id=1, source_target_pairs={{0,64},{4,68},{8,72},{12,76},{16,80},{20,84},{24,88},{28,92},{32,9... | collective-permute-start | bytes 12296 | tf_op jit(solution)/shard_map/ppermute | solution.py:244

commit v3 on v2

--- a/solution.py
+++ b/solution.py
@@ -14,6 +14,7 @@
 COILS = 4
 PAIRS = COILS // 2
 LANES = 2 * NZ
+STEPS = (("comp", 1, 4), ("slab", 1, 4), ("slab", 4, 4), ("slab", 16, 4))
 
 
 def fourier_blocks(length, orientation):
@@ -78,14 +79,23 @@
 
 def first_masked(kspace, sampling, order):
     masks = masks_of(sampling)
+    stacked = [
+        jnp.concatenate(
+            [kspace[coil][:, place * LANES : (place + 1) * LANES] for coil in (2 * pair, 2 * pair + 1)], 1
+        )
+        for pair in range(PAIRS)
+        for place in range(2)
+    ]
+    ordered = product(jnp.concatenate(stacked, 0), order)
     columns = []
     for pair in range(PAIRS):
         rows = []
         for place in range(2):
-            lanes = slice(place * LANES, (place + 1) * LANES)
-            both = jnp.concatenate([kspace[2 * pair][:, lanes], kspace[2 * pair + 1][:, lanes]], 1)
-            ordered = product(both, order)
-            rows += [ordered[:, :LANES] * masks[place], ordered[:, LANES:] * masks[place]]
+            at = (2 * pair + place) * NX
+            rows += [
+                ordered[at : at + NX, part * LANES : (part + 1) * LANES] * masks[place]
+                for part in range(2)
+            ]
         columns.append(jnp.concatenate(rows, 0).astype(jnp.bfloat16))
     return jnp.concatenate(columns, 1)
 
@@ -107,38 +117,41 @@
 
 def combine_coils(arrived, factors, yi, zi):
     rows = product(yi, arrived).astype(jnp.bfloat16)
+    half = 2 * NY
+    places = range(0, arrived.shape[1], LANES)
+    stacked = [
+        jnp.concatenate([rows[:half, at : at + LANES], rows[half:, at : at + LANES]], 1)
+        for at in places
+    ]
+    depth = product(jnp.concatenate(stacked, 0), zi)
     images = []
-    for comp in range(arrived.shape[1] // (PAIRS * LANES)):
+    for comp in range(len(places) // PAIRS):
         total = None
-        for pair in range(PAIRS):
-            at = (comp * PAIRS + pair) * LANES
-            both = jnp.concatenate(
-                [rows[: 2 * NY, at : at + LANES], rows[2 * NY :, at : at + LANES]], 1
-            )
-            depth = product(both, zi)
-            for coil in range(2):
-                real_map, turn_map = factors[2 * pair + coil]
-                image = depth[:, coil * LANES : (coil + 1) * LANES]
-                term = real_map * image - turn_map * swap_halves(image)
-                total = term if total is None else total + term
+        for coil in range(COILS):
+            at = (comp * PAIRS + coil // 2) * half
+            image = depth[at : at + half, coil % 2 * LANES : (coil % 2 + 1) * LANES]
+            real_map, turn_map = factors[coil]
+            term = real_map * image - turn_map * swap_halves(image)
+            total = term if total is None else total + term
         images.append(total)
     return images
 
 
 def spread_out(images, factors, zf, yf):
-    columns = []
+    half = 2 * NY
+    stacked = []
     for image in images:
         turned = swap_halves(image)
-        for pair in range(PAIRS):
-            both = jnp.concatenate(
-                [
-                    (real_map * image + turn_map * turned).astype(jnp.bfloat16)
-                    for real_map, turn_map in factors[2 * pair : 2 * pair + 2]
-                ],
-                1,
-            )
-            depth = product(both, zf).astype(jnp.bfloat16)
-            columns.append(jnp.concatenate([depth[:, :LANES], depth[:, LANES:]], 0))
+        spread = [
+            (real_map * image + turn_map * turned).astype(jnp.bfloat16)
+            for real_map, turn_map in factors
+        ]
+        stacked += [jnp.concatenate(spread[2 * pair : 2 * pair + 2], 1) for pair in range(PAIRS)]
+    depth = product(jnp.concatenate(stacked, 0), zf).astype(jnp.bfloat16)
+    columns = [
+        jnp.concatenate([depth[at : at + half, :LANES], depth[at : at + half, LANES:]], 0)
+        for at in range(0, depth.shape[0], half)
+    ]
     return product(yf, jnp.concatenate(columns, 1)).astype(jnp.bfloat16)
 
 
@@ -216,7 +229,7 @@
         residual[comp] = b[comp] - along_b * q[comp] + along_q * image
 
 
-def call(body, operands, shapes, flops, space=pltpu.VMEM, scratch=()):
+def call(body, operands, shapes, flops, space=pltpu.VMEM, scratch=(), mebibytes=32):
     held = sum(math.prod(o.shape) * o.dtype.itemsize for o in operands)
     held += sum(math.prod(s.shape) * s.dtype.itemsize for s in shapes)
     return pl.pallas_call(
@@ -225,7 +238,7 @@
         in_specs=[pl.BlockSpec(memory_space=space)] * len(operands),
         out_specs=[pl.BlockSpec(memory_space=pltpu.VMEM)] * len(shapes),
         scratch_shapes=scratch,
-        compiler_params=pltpu.CompilerParams(vmem_limit_bytes=32 * 1024 * 1024),
+        compiler_params=pltpu.CompilerParams(vmem_limit_bytes=mebibytes * 1024 * 1024),
         cost_estimate=pl.CostEstimate(flops=flops, bytes_accessed=held, transcendentals=0),
     )(*operands)
 
@@ -238,12 +251,17 @@
     return [(place, place ^ flips) for place in range(lax.axis_size(axis))]
 
 
+def sum_over(values, axis, low, count):
+    terms = [values]
+    terms += [lax.ppermute(values, axis, exclusive(axis, flips * low)) for flips in range(1, count)]
+    while len(terms) > 1:
+        terms = [one + other for one, other in zip(terms[::2], terms[1::2])]
+    return terms[0]
+
+
 def total_of(values):
-    for axis, low in (("comp", 1), ("slab", 1), ("slab", 4), ("slab", 16)):
-        one, two, three = (
-            lax.ppermute(values, axis, exclusive(axis, flips * low)) for flips in (1, 2, 3)
-        )
-        values = (values + one) + (two + three)
+    for axis, low, count in STEPS:
+        values = sum_over(values, axis, low, count)
     return values
 
 
@@ -266,7 +284,7 @@
     first = [kspace, sampling, tables["order"], tables["xi"]]
     scratch = [pltpu.VMEM(array.shape, array.dtype) for array in first]
     scratch.append(pltpu.SemaphoreType.DMA((3 + comps,)))
-    (sent,) = call(first_kernel, first, [sent_shape], 2 * square, pltpu.HBM, scratch)
+    (sent,) = call(first_kernel, first, [sent_shape], 2 * square, pltpu.HBM, scratch, 58)
     b, bb, sent = image_step(exchange(sent))
     operands = [exchange(sent), sampling, tables["xf"], tables["xi"]]
     sent, masked_b, bq = call(

time: 176 us -> 173 us (0.983)
  local copies, waits for them, and re-layouts: 4.04 us -> 0.05 us
    unnamed x24 -> x16, local copies, waits for them, and re-layouts: 4.04 us -> 0.05 us
where the time goes in v3:
time: 173 us
  blocking collectives  122 us (71%)
  starting transfers between devices  23.6 us (14%)
  waiting for transfers between devices  14.4 us (8%)
  Pallas kernels  12.3 us (7%)
    all_to_all x4, blocking collectives, exchange(): lax.all_to_all(values, 'slab', split_axis=0, concat_axis=0, tiled=True)  122 us
    ppermute x12, starting transfers between devices, sum_over(): lax.ppermute(values, axis, exclusive(axis, flips * low))  17.8 us
    ppermute x12, waiting for transfers between devices, sum_over(): lax.ppermute(values, axis, exclusive(axis, flips * low))  14.4 us
    pallas_call x6, Pallas kernels, call(): pl.pallas_call(body, out_shape=shapes, in_specs=[pl.BlockSpec(memory_spac...  12.3 us
    all_to_all x1, starting transfers between devices, exchange(): lax.all_to_all(values, 'slab', split_axis=0, concat_axis=0, tiled=True)  5.81 us
  transfers between devices with their start and end apart: 13, of which 7 were waited for; matrix products, arithmetic and copies ran while one was open for 0% of the time, Pallas kernels for 0%

profile of v3, /device:TPU:2, one launch (start us, length us, event | category | flops | bytes accessed | tf_op | source)
XLA Modules:
  0.0 172.9 jit_solution(10816949766851950318)
XLA Ops:
  0.6 0.0 copy-start.6
  0.6 0.0 copy-start.7
  0.7 3.6 %shard_map.113 = bf16[512,768]{1,0:T(8,128)(2,1)} custom-call(bf16[3,4,128,256]{3,2,1,0:T(8,128)(2,1)} %kspace_at.1, s32[3,128,128]{2,1,0:T(8,128)} %sampling.3, bf16[256,256]{1,0:T(8,128)(2,1)} %constant.20.clone.order_at, bf16[512,512]{1,0:T(8,128)(2,1)} %constant.19.clone.xi_at.xi), custom_call_target="tpu_custom_call" | custom-call | flops 805306368 | bytes 2424832 | tf_op jit(solution)/shard_map/pallas_call | solution.py:235
  4.3 35.3 %all_to_all.55 = bf16[64,8,768]{2,1,0:T(8,128)(2,1)S(1)} all-to-all(bf16[64,8,768]{2,1,0:T(8,128)(2,1)} %bitcast.36), channel_id=1, replica_groups=mesh['slab'=64,'comp'=4] {'slab'}, dimensions={0} | all-to-all | bytes 1572864 | tf_op jit(solution)/shard_map/all_to_all | solution.py:247
  39.7 1.8 %shard_map.114 = (f32[3,256,128]{2,1,0:T(8,128)S(1)}, f32[1,128]{1,0:T(1,128)S(1)}, bf16[512,768]{1,0:T(8,128)(2,1)S(1)}) custom-call(bf16[512,768]{1,0:T(8,128)(2,1)S(1)} %bitcast.29, f32[4,256,128]{2,1,0:T(8,128)S(1)} %bitcast.33, bf16[512,512]{1,0:T(8,128)(2,1)S(1)} %copy-done.2, bf16[256,256]{1,0:T(8,128)(2,1)S(1)} %copy-done.6, ...), custom_call_target="tpu_custom_call" | custom-call | flops 1207959552 | bytes 3801600 | tf_op jit(solution)/shard_map/pallas_call | solution.py:235
  41.6 28.9 %all_to_all.56 = bf16[64,8,768]{2,1,0:T(8,128)(2,1)S(1)} all-to-all(bf16[64,8,768]{2,1,0:T(8,128)(2,1)S(1)} %bitcast.30), channel_id=1, replica_groups=mesh['slab'=64,'comp'=4] {'slab'}, dimensions={0} | all-to-all | bytes 1572864 | tf_op jit(solution)/shard_map/all_to_all | solution.py:247
  70.5 1.0 shard_map.115
  71.5 28.8 %all_to_all.57 = bf16[64,8,768]{2,1,0:T(8,128)(2,1)S(1)} all-to-all(bf16[64,8,768]{2,1,0:T(8,128)(2,1)S(1)} %bitcast.32), channel_id=1, replica_groups=mesh['slab'=64,'comp'=4] {'slab'}, dimensions={0} | all-to-all | bytes 1572864 | tf_op jit(solution)/shard_map/all_to_all | solution.py:247
  100.3 1.8 %shard_map.116 = (f32[3,256,128]{2,1,0:T(8,128)S(1)}, f32[1,128]{1,0:T(1,128)S(1)}, bf16[512,768]{1,0:T(8,128)(2,1)S(1)}) custom-call(bf16[512,768]{1,0:T(8,128)(2,1)S(1)} %bitcast.27, f32[4,256,128]{2,1,0:T(8,128)S(1)} %bitcast.34, bf16[512,512]{1,0:T(8,128)(2,1)S(1)} %copy-done.2, bf16[256,256]{1,0:T(8,128)(2,1)S(1)} %copy-done.6, ...), custom_call_target="tpu_custom_call" | custom-call | flops 1207959552 | bytes 3801600 | tf_op jit(solution)/shard_map/pallas_call | solution.py:235
  102.2 28.8 %all_to_all.58 = bf16[64,8,768]{2,1,0:T(8,128)(2,1)S(1)} all-to-all(bf16[64,8,768]{2,1,0:T(8,128)(2,1)S(1)} %bitcast.28), channel_id=1, replica_groups=mesh['slab'=64,'comp'=4] {'slab'}, dimensions={0} | all-to-all | bytes 1572864 | tf_op jit(solution)/shard_map/all_to_all | solution.py:247
  131.0 2.0 %shard_map.117 = (bf16[512,768]{1,0:T(8,128)(2,1)}, f32[8,128]{1,0:T(8,128)S(1)}) custom-call(bf16[512,768]{1,0:T(8,128)(2,1)S(1)} %bitcast.26, s32[3,128,128]{2,1,0:T(8,128)S(1)} %copy-done.1, bf16[512,512]{1,0:T(8,128)(2,1)S(1)} %copy-done.4, bf16[512,512]{1,0:T(8,128)(2,1)S(1)} %copy-done.3, bf16[512,768]{1,0:T(8,128)(2,1)S(1)} %get-tuple-element.18.masked_b, ...), custom_call_target="tpu_custom_call" | custom-call | flops 805306368 | bytes 3610112 | tf_op jit(solution)/shard_map/pallas_call | solution.py:235
  132.9 5.8 %all-to-all-start.4 = ((bf16[64,8,768]{2,1,0:T(8,128)(2,1)}), bf16[64,8,768]{2,1,0:T(8,128)(2,1)S(1)}, u32[]{:S(2)}, u32[]{:S(2)}) async-start(bf16[64,8,768]{2,1,0:T(8,128)(2,1)} %bitcast.11), calls=%async_computation.4 | async-start | bytes 1572864 | tf_op jit(solution)/shard_map/all_to_all | solution.py:247
  138.7 3.1 %collective-permute-start.2 = (f32[8,128]{1,0:T(8,128)S(1)}, f32[8,128]{1,0:T(8,128)S(1)}, u32[]{:S(2)}, u32[]{:S(2)}) collective-permute-start(f32[8,128]{1,0:T(8,128)S(1)} %get-tuple-element.25), channel_id=1, source_target_pairs={{0,3},{1,2},{2,1},{3,0},{4,7},{5,6},{6,5},{7,4},{8,11},{9,10},{10,... | collective-permute-start | bytes 12296 | tf_op jit(solution)/shard_map/ppermute | solution.py:256
  141.9 0.6 collective-permute-start.1
  142.5 0.5 collective-permute-start
  143.0 0.7 collective-permute-done.2
  143.7 3.3 %collective-permute-done.1 = f32[8,128]{1,0:T(8,128)S(1)} collective-permute-done((f32[8,128]{1,0:T(8,128)S(1)}, f32[8,128]{1,0:T(8,128)S(1)}, u32[]{:S(2)}, u32[]{:S(2)}) %collective-permute-start.1) | collective-permute-done | bytes 4128 | tf_op jit(solution)/shard_map/ppermute | solution.py:256
  147.0 0.1 collective-permute-start.5
  147.1 0.6 collective-permute-start.4
  147.7 1.2 collective-permute-start.3
  148.9 1.2 collective-permute-done.5
  150.1 0.7 collective-permute-done.4
  150.8 3.1 %collective-permute-start.8 = (f32[8,128]{1,0:T(8,128)S(1)}, f32[8,128]{1,0:T(8,128)S(1)}, u32[]{:S(2)}, u32[]{:S(2)}) collective-permute-start(f32[8,128]{1,0:T(8,128)S(1)} %add_add_fusion.2), channel_id=1, source_target_pairs={{0,48},{4,52},{8,56},{12,60},{16,32},{20,36},{24,40},{28,44},{32,1... | collective-permute-start | bytes 12296 | tf_op jit(solution)/shard_map/ppermute | solution.py:256
  153.9 0.9 collective-permute-start.7
  154.7 1.1 collective-permute-start.6
  155.9 3.5 %collective-permute-done.8 = f32[8,128]{1,0:T(8,128)S(1)} collective-permute-done((f32[8,128]{1,0:T(8,128)S(1)}, f32[8,128]{1,0:T(8,128)S(1)}, u32[]{:S(2)}, u32[]{:S(2)}) %collective-permute-start.8) | collective-permute-done | bytes 4128 | tf_op jit(solution)/shard_map/ppermute | solution.py:256
  159.4 0.4 collective-permute-done.6
  159.9 3.5 %collective-permute-start.11 = (f32[8,128]{1,0:T(8,128)S(1)}, f32[8,128]{1,0:T(8,128)S(1)}, u32[]{:S(2)}, u32[]{:S(2)}) collective-permute-start(f32[8,128]{1,0:T(8,128)S(1)} %add_add_fusion.1), channel_id=1, source_target_pairs={{0,192},{4,196},{8,200},{12,204},{16,208},{20,212},{24,216},{28,22... | collective-permute-start | bytes 12296 | tf_op jit(solution)/shard_map/ppermute | solution.py:256
  163.4 2.1 %collective-permute-start.10 = (f32[8,128]{1,0:T(8,128)S(1)}, f32[8,128]{1,0:T(8,128)S(1)}, u32[]{:S(2)}, u32[]{:S(2)}) collective-permute-start(f32[8,128]{1,0:T(8,128)S(1)} %add_add_fusion.1), channel_id=1, source_target_pairs={{0,128},{4,132},{8,136},{12,140},{16,144},{20,148},{24,152},{28,15... | collective-permute-start | bytes 12296 | tf_op jit(solution)/shard_map/ppermute | solution.py:256
  165.5 0.8 collective-permute-start.9
  166.4 4.5 %collective-permute-done.10 = f32[8,128]{1,0:T(8,128)S(1)} collective-permute-done((f32[8,128]{1,0:T(8,128)S(1)}, f32[8,128]{1,0:T(8,128)S(1)}, u32[]{:S(2)}, u32[]{:S(2)}) %collective-permute-start.10) | collective-permute-done | bytes 4128 | tf_op jit(solution)/shard_map/ppermute | solution.py:256
  170.9 2.0 %shard_map.118 = (f32[3,256,128]{2,1,0:T(8,128)}, f32[3,256,128]{2,1,0:T(8,128)}) custom-call(bf16[512,768]{1,0:T(8,128)(2,1)S(1)} %bitcast.25, f32[4,256,128]{2,1,0:T(8,128)S(1)} %bitcast.35, bf16[512,512]{1,0:T(8,128)(2,1)S(1)} %copy-done.2, bf16[256,256]{1,0:T(8,128)(2,1)S(1)} %copy-done.6, f32[3,256,128]{2,1,0:T(8,128)S(1)} %get-tuple-element.23.b, ...), custom_call_target="tpu_custom_call" | custom-call | flops 805306368 | bytes 3543040 | tf_op jit(solution)/shard_map/pallas_call | solution.py:235
  (24 shorter events, 0.1 us)
Async XLA Ops:
  0.6 39.0 %copy-start.6 = (bf16[256,256]{1,0:T(8,128)(2,1)S(1)}, bf16[256,256]{1,0:T(8,128)(2,1)}, u32[]{:S(2)}) copy-start(bf16[256,256]{1,0:T(8,128)(2,1)} %constant.15.clone.zi) | copy-start | bytes 393220
  0.6 39.0 %copy-start.7 = (bf16[256,256]{1,0:T(8,128)(2,1)S(1)}, bf16[256,256]{1,0:T(8,128)(2,1)}, u32[]{:S(2)}) copy-start(bf16[256,256]{1,0:T(8,128)(2,1)} %constant.14.clone.zf) | copy-start | bytes 393220
  4.3 35.4 %copy-start = (f32[4,2,16384]{2,1,0:T(2,128)S(1)}, f32[4,2,16384]{2,1,0:T(2,128)}, u32[]{:S(2)}) copy-start(f32[4,2,16384]{2,1,0:T(2,128)} %param.11) | copy-start | bytes 1572868
  4.3 35.4 %copy-start.2 = (bf16[512,512]{1,0:T(8,128)(2,1)S(1)}, bf16[512,512]{1,0:T(8,128)(2,1)}, u32[]{:S(2)}) copy-start(bf16[512,512]{1,0:T(8,128)(2,1)} %constant.17.clone.yi) | copy-start | bytes 1572868
  4.3 35.4 %copy-start.5 = (bf16[512,512]{1,0:T(8,128)(2,1)S(1)}, bf16[512,512]{1,0:T(8,128)(2,1)}, u32[]{:S(2)}) copy-start(bf16[512,512]{1,0:T(8,128)(2,1)} %constant.16.clone.yf) | copy-start | bytes 1572868
  41.5 29.0 %copy-start.1 = (s32[3,128,128]{2,1,0:T(8,128)S(1)}, s32[3,128,128]{2,1,0:T(8,128)}, u32[]{:S(2)}) copy-start(s32[3,128,128]{2,1,0:T(8,128)} %sampling.3) | copy-start | bytes 589828
  41.5 29.0 %copy-start.3 = (bf16[512,512]{1,0:T(8,128)(2,1)S(1)}, bf16[512,512]{1,0:T(8,128)(2,1)}, u32[]{:S(2)}) copy-start(bf16[512,512]{1,0:T(8,128)(2,1)} %constant.19.clone.xi_at.xi) | copy-start | bytes 1572868
  41.5 28.9 %copy-start.4 = (bf16[512,512]{1,0:T(8,128)(2,1)S(1)}, bf16[512,512]{1,0:T(8,128)(2,1)}, u32[]{:S(2)}) copy-start(bf16[512,512]{1,0:T(8,128)(2,1)} %constant.18.clone.xf) | copy-start | bytes 1572868
  132.9 38.0 %all-to-all-start.4 = ((bf16[64,8,768]{2,1,0:T(8,128)(2,1)}), bf16[64,8,768]{2,1,0:T(8,128)(2,1)S(1)}, u32[]{:S(2)}, u32[]{:S(2)}) async-start(bf16[64,8,768]{2,1,0:T(8,128)(2,1)} %bitcast.11), calls=%async_computation.4 | async-start | bytes 1572864 | tf_op jit(solution)/shard_map/all_to_all | solution.py:247
  138.7 4.9 %collective-permute-start.2 = (f32[8,128]{1,0:T(8,128)S(1)}, f32[8,128]{1,0:T(8,128)S(1)}, u32[]{:S(2)}, u32[]{:S(2)}) collective-permute-start(f32[8,128]{1,0:T(8,128)S(1)} %get-tuple-element.25), channel_id=1, source_target_pairs={{0,3},{1,2},{2,1},{3,0},{4,7},{5,6},{6,5},{7,4},{8,11},{9,10},{10,... | collective-permute-start | bytes 12296 | tf_op jit(solution)/shard_map/ppermute | solution.py:256
  141.9 5.1 %collective-permute-start.1 = (f32[8,128]{1,0:T(8,128)S(1)}, f32[8,128]{1,0:T(8,128)S(1)}, u32[]{:S(2)}, u32[]{:S(2)}) collective-permute-start(f32[8,128]{1,0:T(8,128)S(1)} %get-tuple-element.25), channel_id=1, source_target_pairs={{0,2},{1,3},{2,0},{3,1},{4,6},{5,7},{6,4},{7,5},{8,10},{9,11},{10,... | collective-permute-start | bytes 12296 | tf_op jit(solution)/shard_map/ppermute | solution.py:256
  142.5 4.5 %collective-permute-start = (f32[8,128]{1,0:T(8,128)S(1)}, f32[8,128]{1,0:T(8,128)S(1)}, u32[]{:S(2)}, u32[]{:S(2)}) collective-permute-start(f32[8,128]{1,0:T(8,128)S(1)} %get-tuple-element.25), channel_id=1, source_target_pairs={{0,1},{1,0},{2,3},{3,2},{4,5},{5,4},{6,7},{7,6},{8,9},{9,8},{10,11... | collective-permute-start | bytes 12296 | tf_op jit(solution)/shard_map/ppermute | solution.py:256
  147.0 3.1 %collective-permute-start.5 = (f32[8,128]{1,0:T(8,128)S(1)}, f32[8,128]{1,0:T(8,128)S(1)}, u32[]{:S(2)}, u32[]{:S(2)}) collective-permute-start(f32[8,128]{1,0:T(8,128)S(1)} %add_add_fusion.3), channel_id=1, source_target_pairs={{0,12},{4,8},{8,4},{12,0},{16,28},{20,24},{24,20},{28,16},{32,44},... | collective-permute-start | bytes 12296 | tf_op jit(solution)/shard_map/ppermute | solution.py:256
  147.1 3.7 %collective-permute-start.4 = (f32[8,128]{1,0:T(8,128)S(1)}, f32[8,128]{1,0:T(8,128)S(1)}, u32[]{:S(2)}, u32[]{:S(2)}) collective-permute-start(f32[8,128]{1,0:T(8,128)S(1)} %add_add_fusion.3), channel_id=1, source_target_pairs={{0,8},{4,12},{8,0},{12,4},{16,24},{20,28},{24,16},{28,20},{32,40},... | collective-permute-start | bytes 12296 | tf_op jit(solution)/shard_map/ppermute | solution.py:256
  147.7 3.1 %collective-permute-start.3 = (f32[8,128]{1,0:T(8,128)S(1)}, f32[8,128]{1,0:T(8,128)S(1)}, u32[]{:S(2)}, u32[]{:S(2)}) collective-permute-start(f32[8,128]{1,0:T(8,128)S(1)} %add_add_fusion.3), channel_id=1, source_target_pairs={{0,4},{4,0},{8,12},{12,8},{16,20},{20,16},{24,28},{28,24},{32,36},... | collective-permute-start | bytes 12296 | tf_op jit(solution)/shard_map/ppermute | solution.py:256
  150.8 8.6 %collective-permute-start.8 = (f32[8,128]{1,0:T(8,128)S(1)}, f32[8,128]{1,0:T(8,128)S(1)}, u32[]{:S(2)}, u32[]{:S(2)}) collective-permute-start(f32[8,128]{1,0:T(8,128)S(1)} %add_add_fusion.2), channel_id=1, source_target_pairs={{0,48},{4,52},{8,56},{12,60},{16,32},{20,36},{24,40},{28,44},{32,1... | collective-permute-start | bytes 12296 | tf_op jit(solution)/shard_map/ppermute | solution.py:256
  153.9 5.6 %collective-permute-start.7 = (f32[8,128]{1,0:T(8,128)S(1)}, f32[8,128]{1,0:T(8,128)S(1)}, u32[]{:S(2)}, u32[]{:S(2)}) collective-permute-start(f32[8,128]{1,0:T(8,128)S(1)} %add_add_fusion.2), channel_id=1, source_target_pairs={{0,32},{4,36},{8,40},{12,44},{16,48},{20,52},{24,56},{28,60},{32,0... | collective-permute-start | bytes 12296 | tf_op jit(solution)/shard_map/ppermute | solution.py:256
  154.7 5.1 %collective-permute-start.6 = (f32[8,128]{1,0:T(8,128)S(1)}, f32[8,128]{1,0:T(8,128)S(1)}, u32[]{:S(2)}, u32[]{:S(2)}) collective-permute-start(f32[8,128]{1,0:T(8,128)S(1)} %add_add_fusion.2), channel_id=1, source_target_pairs={{0,16},{4,20},{8,24},{12,28},{16,0},{20,4},{24,8},{28,12},{32,48},... | collective-permute-start | bytes 12296 | tf_op jit(solution)/shard_map/ppermute | solution.py:256
  159.9 6.5 %collective-permute-start.11 = (f32[8,128]{1,0:T(8,128)S(1)}, f32[8,128]{1,0:T(8,128)S(1)}, u32[]{:S(2)}, u32[]{:S(2)}) collective-permute-start(f32[8,128]{1,0:T(8,128)S(1)} %add_add_fusion.1), channel_id=1, source_target_pairs={{0,192},{4,196},{8,200},{12,204},{16,208},{20,212},{24,216},{28,22... | collective-permute-start | bytes 12296 | tf_op jit(solution)/shard_map/ppermute | solution.py:256
  163.4 7.5 %collective-permute-start.10 = (f32[8,128]{1,0:T(8,128)S(1)}, f32[8,128]{1,0:T(8,128)S(1)}, u32[]{:S(2)}, u32[]{:S(2)}) collective-permute-start(f32[8,128]{1,0:T(8,128)S(1)} %add_add_fusion.1), channel_id=1, source_target_pairs={{0,128},{4,132},{8,136},{12,140},{16,144},{20,148},{24,152},{28,15... | collective-permute-start | bytes 12296 | tf_op jit(solution)/shard_map/ppermute | solution.py:256
  165.5 5.4 %collective-permute-start.9 = (f32[8,128]{1,0:T(8,128)S(1)}, f32[8,128]{1,0:T(8,128)S(1)}, u32[]{:S(2)}, u32[]{:S(2)}) collective-permute-start(f32[8,128]{1,0:T(8,128)S(1)} %add_add_fusion.1), channel_id=1, source_target_pairs={{0,64},{4,68},{8,72},{12,76},{16,80},{20,84},{24,88},{28,92},{32,9... | collective-permute-start | bytes 12296 | tf_op jit(solution)/shard_map/ppermute | solution.py:256

commit v4 on v3

--- a/solution.py
+++ b/solution.py
@@ -14,7 +14,8 @@
 COILS = 4
 PAIRS = COILS // 2
 LANES = 2 * NZ
-STEPS = (("comp", 1, 4), ("slab", 1, 4), ("slab", 4, 4), ("slab", 16, 4))
+GROUP_STEPS = (("slab", 1, 4), ("slab", 4, 4), ("slab", 16, 4))
+STEPS = (("comp", 1, 4),) + GROUP_STEPS
 
 
 def fourier_blocks(length, orientation):
@@ -126,14 +127,14 @@
     depth = product(jnp.concatenate(stacked, 0), zi)
     images = []
     for comp in range(len(places) // PAIRS):
-        total = None
+        straight = turned = None
         for coil in range(COILS):
             at = (comp * PAIRS + coil // 2) * half
             image = depth[at : at + half, coil % 2 * LANES : (coil % 2 + 1) * LANES]
             real_map, turn_map = factors[coil]
-            term = real_map * image - turn_map * swap_halves(image)
-            total = term if total is None else total + term
-        images.append(total)
+            straight = real_map * image if coil == 0 else straight + real_map * image
+            turned = turn_map * image if coil == 0 else turned + turn_map * image
+        images.append(straight + swap_halves(turned))
     return images
 
 
@@ -164,13 +165,20 @@
     return fold_rows(one.astype(jnp.float32) * other.astype(jnp.float32))
 
 
+def group_step(sums):
+    totals = sums[0:2].sum(1, keepdims=True)
+    bb, bq = totals[0:1], totals[1:2]
+    usable = jnp.logical_and(bb > 0.0, bq > 0.0)
+    return jnp.where(usable, bb, 1.0) / jnp.where(usable, bq, 1.0)
+
+
 def final_scales(sums):
     totals = sums.sum(1, keepdims=True)
-    bb, bq, qq, bt, qt = (totals[place : place + 1] for place in range(5))
+    bb, bq, qq, mixed, square = (totals[place : place + 1] for place in range(5))
     step_one = bb / bq
     norm_next = bb - 2.0 * step_one * bq + step_one * step_one * qq
     more = 1.0 + norm_next / bb
-    curve = more * more * bq - more * step_one * (bt + qq) + step_one * step_one * qt
+    curve = more * more * bq + 2.0 * more * step_one * mixed + step_one * step_one * square
     step_two = norm_next / curve
     return step_one + step_two * more, step_two * step_one
 
@@ -193,40 +201,50 @@
     out[...] = product(xi[...], jnp.concatenate(columns, 1)).astype(jnp.bfloat16)
 
 
-def kspace_kernel(portion, sampling, xf, xi, out, masked_out, sum_out):
+def kspace_kernel(portion, sampling, xf, xi, bb, out, masked_out, sums_out):
     masked = masked_spectrum(portion[...], sampling[...], xf[...])
     masked_out[...] = masked
-    sum_out[...] = row_of(masked, masked)
+    sums_out[0:1] = bb[...]
+    sums_out[1:2] = row_of(masked, masked)
+    sums_out[2:8] = jnp.zeros((6, LANES), jnp.float32)
     out[...] = product(xi[...], masked).astype(jnp.bfloat16)
 
 
-def kspace_last_kernel(portion, sampling, xf, xi, masked_b, bb, bq, qq, out, sums_out):
+def kspace_last_kernel(portion, sampling, xf, xi, masked_b, here, group, qq, out, sums_out):
     masked = masked_spectrum(portion[...], sampling[...], xf[...])
     out[...] = product(xi[...], masked).astype(jnp.bfloat16)
-    sums_out[0:1] = bb[...]
-    sums_out[1:2] = bq[...]
+    inverse_step = 1.0 / group_step(group[...])
+    earlier = masked_b[...].astype(jnp.float32)
+    change = (masked.astype(jnp.float32) - earlier) * inverse_step
+    sums_out[0:2] = here[0:2]
     sums_out[2:3] = qq[...]
-    sums_out[3:4] = row_of(masked_b[...], masked)
-    sums_out[4:5] = row_of(masked, masked)
+    sums_out[3:4] = row_of(earlier, change)
+    sums_out[4:5] = row_of(change, change)
     sums_out[5:8] = jnp.zeros((3, LANES), jnp.float32)
 
 
-def image_kernel(arrived, coils, yi, zi, zf, yf, image_out, sum_out, out):
+def image_kernel(arrived, coils, yi, zi, zf, yf, *refs):
+    image_out, sum_out, out = refs[-3:]
     factors = [coil_factors(coils[coil]) for coil in range(COILS)]
     images = combine_coils(arrived[...], factors, yi[...], zi[...])
-    out[...] = spread_out(images, factors, zf[...], yf[...])
     for comp, image in enumerate(images):
         image_out[comp] = image
     sum_out[...] = sum(row_of(image, image) for image in images)
-
-
-def last_kernel(arrived, coils, yi, zi, b, q, sums, coefficients, residual):
+    if len(refs) > 3:
+        b, group = refs[:2]
+        step = group_step(group[...])
+        images = [b[comp] - step * image for comp, image in enumerate(images)]
+    out[...] = spread_out(images, factors, zf[...], yf[...])
+
+
+def last_kernel(arrived, coils, yi, zi, b, q, group, sums, coefficients, residual):
     factors = [coil_factors(coils[coil]) for coil in range(COILS)]
     images = combine_coils(arrived[...], factors, yi[...], zi[...])
     along_b, along_q = final_scales(sums[...])
+    along_t = along_q / group_step(group[...])
     for comp, image in enumerate(images):
         coefficients[comp] = along_b * b[comp] - along_q * q[comp]
-        residual[comp] = b[comp] - along_b * q[comp] + along_q * image
+        residual[comp] = b[comp] - along_b * q[comp] + along_t * (q[comp] - image)
 
 
 def call(body, operands, shapes, flops, space=pltpu.VMEM, scratch=(), mebibytes=32):
@@ -259,8 +277,8 @@
     return terms[0]
 
 
-def total_of(values):
-    for axis, low, count in STEPS:
+def total_of(values, steps):
+    for axis, low, count in steps:
         values = sum_over(values, axis, low, count)
     return values
 
@@ -277,8 +295,9 @@
     sums_shape = jax.ShapeDtypeStruct((8, LANES), jnp.float32)
     square = 2 * (4 * NX) * (4 * NX) * width
 
-    def image_step(arrived):
+    def image_step(arrived, *earlier):
         operands = [arrived, coils] + [tables[name] for name in ("yi", "zi", "zf", "yf")]
+        operands += earlier
         return call(image_kernel, operands, [image_shape, sum_shape, sent_shape], 3 * square)
 
     first = [kspace, sampling, tables["order"], tables["xi"]]
@@ -286,15 +305,16 @@
     scratch.append(pltpu.SemaphoreType.DMA((3 + comps,)))
     (sent,) = call(first_kernel, first, [sent_shape], 2 * square, pltpu.HBM, scratch, 58)
     b, bb, sent = image_step(exchange(sent))
-    operands = [exchange(sent), sampling, tables["xf"], tables["xi"]]
-    sent, masked_b, bq = call(
-        kspace_kernel, operands, [sent_shape, sent_shape, sum_shape], 2 * square
+    operands = [exchange(sent), sampling, tables["xf"], tables["xi"], bb]
+    sent, masked_b, here = call(
+        kspace_kernel, operands, [sent_shape, sent_shape, sums_shape], 2 * square
     )
-    q, qq, sent = image_step(exchange(sent))
-    operands = [exchange(sent), sampling, tables["xf"], tables["xi"], masked_b, bb, bq, qq]
+    group = total_of(here, GROUP_STEPS)
+    q, qq, sent = image_step(exchange(sent), b, group)
+    operands = [exchange(sent), sampling, tables["xf"], tables["xi"], masked_b, here, group, qq]
     sent, sums = call(kspace_last_kernel, operands, [sent_shape, sums_shape], 2 * square)
     arrived = exchange(sent)
-    operands = [arrived, coils, tables["yi"], tables["zi"], b, q, total_of(sums)]
+    operands = [arrived, coils, tables["yi"], tables["zi"], b, q, group, total_of(sums, STEPS)]
     outputs = call(last_kernel, operands, [image_shape] * 2, 2 * square)
     return tuple(
         output.reshape(comps, NY, 2, LANES).transpose(0, 2, 1, 3).reshape(comps, 2, -1)

time: 173 us -> 188 us (1.087)
  blocking collectives: 122 us -> 95 us
  starting transfers between devices: 23.6 us -> 43.1 us
  waiting for transfers between devices: 14.4 us -> 31.5 us
  local copies, waits for them, and re-layouts: 0.05 us -> 3.73 us
    all_to_all x4 -> x3, blocking collectives: 122 us -> 95 us  [exchange(): lax.all_to_all(values, 'slab', split_axis=0, concat_axis=0, tiled=True)]
    ppermute x12 -> x21, waiting for transfers between devices: 14.4 us -> 31.5 us  [sum_over(): lax.ppermute(values, axis, exclusive(axis, flips * low))]
    ppermute x12 -> x21, starting transfers between devices: 17.8 us -> 31.3 us  [sum_over(): lax.ppermute(values, axis, exclusive(axis, flips * low))]
    all_to_all x1 -> x2, starting transfers between devices: 5.81 us -> 11.8 us  [exchange(): lax.all_to_all(values, 'slab', split_axis=0, concat_axis=0, tiled=True)]
    unnamed x16 -> x32, local copies, waits for them, and re-layouts: 0.05 us -> 3.73 us
  transfers between devices with their start and end apart: 13 -> 23, of which waited for: 7 -> 11; matrix products, arithmetic and copies ran while one was open for 0% -> 0% of each run, Pallas kernels for 0% -> 0%
where the time goes in v4:
time: 188 us; the launch traced here: 187 us
  blocking collectives  95 us (51%)
  starting transfers between devices  43.1 us (23%)
  waiting for transfers between devices  31.5 us (17%)
  Pallas kernels  13.3 us (7%)
  local copies, waits for them, and re-layouts  3.73 us (2%)
    all_to_all x3, blocking collectives, exchange(): lax.all_to_all(values, 'slab', split_axis=0, concat_axis=0, tiled=True)  95 us
    ppermute x21, waiting for transfers between devices, sum_over(): lax.ppermute(values, axis, exclusive(axis, flips * low))  31.5 us
    ppermute x21, starting transfers between devices, sum_over(): lax.ppermute(values, axis, exclusive(axis, flips * low))  31.3 us
    pallas_call x6, Pallas kernels, call(): pl.pallas_call(body, out_shape=shapes, in_specs=[pl.BlockSpec(memory_spac...  13.3 us
    all_to_all x2, starting transfers between devices, exchange(): lax.all_to_all(values, 'slab', split_axis=0, concat_axis=0, tiled=True)  11.8 us
  transfers between devices with their start and end apart: 23, of which 11 were waited for; matrix products, arithmetic and copies ran while one was open for 0% of the time, Pallas kernels for 0%

profile of v4, /device:TPU:2, one launch (start us, length us, event | category | flops | bytes accessed | tf_op | source)
XLA Modules:
  0.0 187.5 jit_solution(15417417843496350118)
XLA Ops:
  0.7 3.6 %shard_map.113 = bf16[512,768]{1,0:T(8,128)(2,1)} custom-call(bf16[3,4,128,256]{3,2,1,0:T(8,128)(2,1)} %kspace_at.1, s32[3,128,128]{2,1,0:T(8,128)} %sampling.3, bf16[256,256]{1,0:T(8,128)(2,1)} %constant.20.clone.order_at, bf16[512,512]{1,0:T(8,128)(2,1)} %constant.19.clone.xi_at.xi), custom_call_target="tpu_custom_call" | custom-call | flops 805306368 | bytes 2424832 | tf_op jit(solution)/shard_map/pallas_call | solution.py:253
  4.3 35.3 %all_to_all.55 = bf16[64,8,768]{2,1,0:T(8,128)(2,1)S(1)} all-to-all(bf16[64,8,768]{2,1,0:T(8,128)(2,1)} %bitcast.35), channel_id=1, replica_groups=mesh['slab'=64,'comp'=4] {'slab'}, dimensions={0} | all-to-all | bytes 1572864 | tf_op jit(solution)/shard_map/all_to_all | solution.py:265
  39.7 1.8 shard_map.114
  41.5 28.9 %all_to_all.56 = bf16[64,8,768]{2,1,0:T(8,128)(2,1)S(1)} all-to-all(bf16[64,8,768]{2,1,0:T(8,128)(2,1)S(1)} %bitcast.31), channel_id=1, replica_groups=mesh['slab'=64,'comp'=4] {'slab'}, dimensions={0} | all-to-all | bytes 1572864 | tf_op jit(solution)/shard_map/all_to_all | solution.py:265
  70.5 2.0 %shard_map.115 = (bf16[512,768]{1,0:T(8,128)(2,1)}, bf16[512,768]{1,0:T(8,128)(2,1)S(1)}, f32[8,128]{1,0:T(8,128)S(1)}) custom-call(bf16[512,768]{1,0:T(8,128)(2,1)S(1)} %bitcast.29, s32[3,128,128]{2,1,0:T(8,128)S(1)} %copy-done.1, bf16[512,512]{1,0:T(8,128)(2,1)S(1)} %copy-done.4, bf16[512,512]{1,0:T(8,128)(2,1)S(1)} %copy-done.3, ...), custom_call_target="tpu_custom_call" | custom-call | flops 805306368 | bytes 3609088 | tf_op jit(solution)/shard_map/pallas_call | solution.py:253
  73.3 5.8 %all-to-all-start.2 = ((bf16[64,8,768]{2,1,0:T(8,128)(2,1)}), bf16[64,8,768]{2,1,0:T(8,128)(2,1)S(1)}, u32[]{:S(2)}, u32[]{:S(2)}) async-start(bf16[64,8,768]{2,1,0:T(8,128)(2,1)} %bitcast.7), calls=%async_computation.2 | async-start | bytes 1572864 | tf_op jit(solution)/shard_map/all_to_all | solution.py:265
  79.3 1.7 collective-permute-start.1
  81.1 1.3 collective-permute-done.2
  83.0 3.6 %collective-permute-start.5 = (f32[8,128]{1,0:T(8,128)S(1)}, f32[8,128]{1,0:T(8,128)S(1)}, u32[]{:S(2)}, u32[]{:S(2)}) collective-permute-start(f32[8,128]{1,0:T(8,128)S(1)} %add_add_fusion.6), channel_id=1, source_target_pairs={{0,48},{4,52},{8,56},{12,60},{16,32},{20,36},{24,40},{28,44},{32,1... | collective-permute-start | bytes 12296 | tf_op jit(solution)/shard_map/ppermute | solution.py:274
  87.1 1.0 collective-permute-start.3
  88.0 11.8 %collective-permute-done.5 = f32[8,128]{1,0:T(8,128)S(1)} collective-permute-done((f32[8,128]{1,0:T(8,128)S(1)}, f32[8,128]{1,0:T(8,128)S(1)}, u32[]{:S(2)}, u32[]{:S(2)}) %collective-permute-start.5) | collective-permute-done | bytes 4128 | tf_op jit(solution)/shard_map/ppermute | solution.py:274
  99.8 2.5 %collective-permute-start.8 = (f32[8,128]{1,0:T(8,128)S(1)}, f32[8,128]{1,0:T(8,128)S(1)}, u32[]{:S(2)}, u32[]{:S(2)}) collective-permute-start(f32[8,128]{1,0:T(8,128)S(1)} %add_add_fusion.5), channel_id=1, source_target_pairs={{0,192},{4,196},{8,200},{12,204},{16,208},{20,212},{24,216},{28,22... | collective-permute-start | bytes 12296 | tf_op jit(solution)/shard_map/ppermute | solution.py:274
  102.3 2.5 %collective-permute-start.7 = (f32[8,128]{1,0:T(8,128)S(1)}, f32[8,128]{1,0:T(8,128)S(1)}, u32[]{:S(2)}, u32[]{:S(2)}) collective-permute-start(f32[8,128]{1,0:T(8,128)S(1)} %add_add_fusion.5), channel_id=1, source_target_pairs={{0,128},{4,132},{8,136},{12,140},{16,144},{20,148},{24,152},{28,15... | collective-permute-start | bytes 12296 | tf_op jit(solution)/shard_map/ppermute | solution.py:274
  104.8 1.6 collective-permute-start.6
  106.4 3.4 %collective-permute-done.7 = f32[8,128]{1,0:T(8,128)S(1)} collective-permute-done((f32[8,128]{1,0:T(8,128)S(1)}, f32[8,128]{1,0:T(8,128)S(1)}, u32[]{:S(2)}, u32[]{:S(2)}) %collective-permute-start.7) | collective-permute-done | bytes 4128 | tf_op jit(solution)/shard_map/ppermute | solution.py:274
  109.9 1.0 copy-done.6
  110.9 1.0 copy-done.12
  111.9 1.8 shard_map.116
  114.5 30.7 %all_to_all.57 = bf16[64,8,768]{2,1,0:T(8,128)(2,1)S(1)} all-to-all(bf16[64,8,768]{2,1,0:T(8,128)(2,1)S(1)} %bitcast.28), channel_id=1, replica_groups=mesh['slab'=64,'comp'=4] {'slab'}, dimensions={0} | all-to-all | bytes 1572864 | tf_op jit(solution)/shard_map/all_to_all | solution.py:265
  145.2 2.1 %shard_map.117 = (bf16[512,768]{1,0:T(8,128)(2,1)}, f32[8,128]{1,0:T(8,128)S(1)}) custom-call(bf16[512,768]{1,0:T(8,128)(2,1)S(1)} %bitcast.27, s32[3,128,128]{2,1,0:T(8,128)S(1)} %copy-done.1, bf16[512,512]{1,0:T(8,128)(2,1)S(1)} %copy-done.4, bf16[512,512]{1,0:T(8,128)(2,1)S(1)} %copy-done.3, bf16[512,768]{1,0:T(8,128)(2,1)S(1)} %copy-done.10, ...), custom_call_target="tpu_custom_call" | custom-call | flops 805306368 | bytes 3617280 | tf_op jit(solution)/shard_map/pallas_call | solution.py:253
  147.3 5.9 %all-to-all-start.4 = ((bf16[64,8,768]{2,1,0:T(8,128)(2,1)}), bf16[64,8,768]{2,1,0:T(8,128)(2,1)S(1)}, u32[]{:S(2)}, u32[]{:S(2)}) async-start(bf16[64,8,768]{2,1,0:T(8,128)(2,1)} %bitcast.11), calls=%async_computation.4 | async-start | bytes 1572864 | tf_op jit(solution)/shard_map/all_to_all | solution.py:265
  153.3 3.1 %collective-permute-start.11 = (f32[8,128]{1,0:T(8,128)S(1)}, f32[8,128]{1,0:T(8,128)S(1)}, u32[]{:S(2)}, u32[]{:S(2)}) collective-permute-start(f32[8,128]{1,0:T(8,128)S(1)} %get-tuple-element.25), channel_id=1, source_target_pairs={{0,3},{1,2},{2,1},{3,0},{4,7},{5,6},{6,5},{7,4},{8,11},{9,10},{10,... | collective-permute-start | bytes 12296 | tf_op jit(solution)/shard_map/ppermute | solution.py:274
  158.2 3.3 %collective-permute-done.10 = f32[8,128]{1,0:T(8,128)S(1)} collective-permute-done((f32[8,128]{1,0:T(8,128)S(1)}, f32[8,128]{1,0:T(8,128)S(1)}, u32[]{:S(2)}, u32[]{:S(2)}) %collective-permute-start.10) | collective-permute-done | bytes 4128 | tf_op jit(solution)/shard_map/ppermute | solution.py:274
  162.2 1.2 collective-permute-start.12
  163.5 1.2 collective-permute-done.14
  165.3 3.1 %collective-permute-start.17 = (f32[8,128]{1,0:T(8,128)S(1)}, f32[8,128]{1,0:T(8,128)S(1)}, u32[]{:S(2)}, u32[]{:S(2)}) collective-permute-start(f32[8,128]{1,0:T(8,128)S(1)} %add_add_fusion.2), channel_id=1, source_target_pairs={{0,48},{4,52},{8,56},{12,60},{16,32},{20,36},{24,40},{28,44},{32,1... | collective-permute-start | bytes 12296 | tf_op jit(solution)/shard_map/ppermute | solution.py:274
  169.3 1.1 collective-permute-start.15
  170.4 3.5 %collective-permute-done.17 = f32[8,128]{1,0:T(8,128)S(1)} collective-permute-done((f32[8,128]{1,0:T(8,128)S(1)}, f32[8,128]{1,0:T(8,128)S(1)}, u32[]{:S(2)}, u32[]{:S(2)}) %collective-permute-start.17) | collective-permute-done | bytes 4128 | tf_op jit(solution)/shard_map/ppermute | solution.py:274
  174.4 3.5 %collective-permute-start.20 = (f32[8,128]{1,0:T(8,128)S(1)}, f32[8,128]{1,0:T(8,128)S(1)}, u32[]{:S(2)}, u32[]{:S(2)}) collective-permute-start(f32[8,128]{1,0:T(8,128)S(1)} %add_add_fusion.1), channel_id=1, source_target_pairs={{0,192},{4,196},{8,200},{12,204},{16,208},{20,212},{24,216},{28,22... | collective-permute-start | bytes 12296 | tf_op jit(solution)/shard_map/ppermute | solution.py:274
  177.9 2.1 %collective-permute-start.19 = (f32[8,128]{1,0:T(8,128)S(1)}, f32[8,128]{1,0:T(8,128)S(1)}, u32[]{:S(2)}, u32[]{:S(2)}) collective-permute-start(f32[8,128]{1,0:T(8,128)S(1)} %add_add_fusion.1), channel_id=1, source_target_pairs={{0,128},{4,132},{8,136},{12,140},{16,144},{20,148},{24,152},{28,15... | collective-permute-start | bytes 12296 | tf_op jit(solution)/shard_map/ppermute | solution.py:274
  180.9 4.5 %collective-permute-done.19 = f32[8,128]{1,0:T(8,128)S(1)} collective-permute-done((f32[8,128]{1,0:T(8,128)S(1)}, f32[8,128]{1,0:T(8,128)S(1)}, u32[]{:S(2)}, u32[]{:S(2)}) %collective-permute-start.19) | collective-permute-done | bytes 4128 | tf_op jit(solution)/shard_map/ppermute | solution.py:274
  185.5 2.0 %shard_map.118 = (f32[3,256,128]{2,1,0:T(8,128)}, f32[3,256,128]{2,1,0:T(8,128)}) custom-call(bf16[512,768]{1,0:T(8,128)(2,1)S(1)} %bitcast.25, f32[4,256,128]{2,1,0:T(8,128)S(1)} %bitcast.34, bf16[512,512]{1,0:T(8,128)(2,1)S(1)} %copy-done.2, bf16[256,256]{1,0:T(8,128)(2,1)S(1)} %copy-done.7, f32[3,256,128]{2,1,0:T(8,128)S(1)} %copy-done.13, ...), custom_call_target="tpu_custom_call" | custom-call | flops 805306368 | bytes 3547136 | tf_op jit(solution)/shard_map/pallas_call | solution.py:253
  (62 shorter events, 8.5 us)
Async XLA Ops:
  0.6 39.0 %copy-start.7 = (bf16[256,256]{1,0:T(8,128)(2,1)S(1)}, bf16[256,256]{1,0:T(8,128)(2,1)}, u32[]{:S(2)}) copy-start(bf16[256,256]{1,0:T(8,128)(2,1)} %constant.15.clone.zi) | copy-start | bytes 393220
  0.6 39.0 %copy-start.8 = (bf16[256,256]{1,0:T(8,128)(2,1)S(1)}, bf16[256,256]{1,0:T(8,128)(2,1)}, u32[]{:S(2)}) copy-start(bf16[256,256]{1,0:T(8,128)(2,1)} %constant.14.clone.zf) | copy-start | bytes 393220
  4.3 35.4 %copy-start = (f32[4,2,16384]{2,1,0:T(2,128)S(1)}, f32[4,2,16384]{2,1,0:T(2,128)}, u32[]{:S(2)}) copy-start(f32[4,2,16384]{2,1,0:T(2,128)} %param.11) | copy-start | bytes 1572868
  4.3 35.4 %copy-start.2 = (bf16[512,512]{1,0:T(8,128)(2,1)S(1)}, bf16[512,512]{1,0:T(8,128)(2,1)}, u32[]{:S(2)}) copy-start(bf16[512,512]{1,0:T(8,128)(2,1)} %constant.17.clone.yi) | copy-start | bytes 1572868
  4.3 35.4 %copy-start.5 = (bf16[512,512]{1,0:T(8,128)(2,1)S(1)}, bf16[512,512]{1,0:T(8,128)(2,1)}, u32[]{:S(2)}) copy-start(bf16[512,512]{1,0:T(8,128)(2,1)} %constant.16.clone.yf) | copy-start | bytes 1572868
  41.5 29.0 %copy-start.11 = (f32[3,256,128]{2,1,0:T(8,128)}, f32[3,256,128]{2,1,0:T(8,128)S(1)}, u32[]{:S(2)}) copy-start(f32[3,256,128]{2,1,0:T(8,128)S(1)} %get-tuple-element.18.refs_0_.b) | copy-start | bytes 1179652
  73.3 36.5 %all-to-all-start.2 = ((bf16[64,8,768]{2,1,0:T(8,128)(2,1)}), bf16[64,8,768]{2,1,0:T(8,128)(2,1)S(1)}, u32[]{:S(2)}, u32[]{:S(2)}) async-start(bf16[64,8,768]{2,1,0:T(8,128)(2,1)} %bitcast.7), calls=%async_computation.2 | async-start | bytes 1572864 | tf_op jit(solution)/shard_map/all_to_all | solution.py:265
  79.1 3.2 %collective-permute-start.2 = (f32[8,128]{1,0:T(8,128)S(1)}, f32[8,128]{1,0:T(8,128)S(1)}, u32[]{:S(2)}, u32[]{:S(2)}) collective-permute-start(f32[8,128]{1,0:T(8,128)S(1)} %get-tuple-element.19.here), channel_id=1, source_target_pairs={{0,12},{4,8},{8,4},{12,0},{16,28},{20,24},{24,20},{28,16},{32,44},... | collective-permute-start | bytes 12296 | tf_op jit(solution)/shard_map/ppermute | solution.py:274
  79.3 3.6 %collective-permute-start.1 = (f32[8,128]{1,0:T(8,128)S(1)}, f32[8,128]{1,0:T(8,128)S(1)}, u32[]{:S(2)}, u32[]{:S(2)}) collective-permute-start(f32[8,128]{1,0:T(8,128)S(1)} %get-tuple-element.19.here), channel_id=1, source_target_pairs={{0,8},{4,12},{8,0},{12,4},{16,24},{20,28},{24,16},{28,20},{32,40},... | collective-permute-start | bytes 12296 | tf_op jit(solution)/shard_map/ppermute | solution.py:274
  81.0 1.9 %collective-permute-start = (f32[8,128]{1,0:T(8,128)S(1)}, f32[8,128]{1,0:T(8,128)S(1)}, u32[]{:S(2)}, u32[]{:S(2)}) collective-permute-start(f32[8,128]{1,0:T(8,128)S(1)} %get-tuple-element.19.here), channel_id=1, source_target_pairs={{0,4},{4,0},{8,12},{12,8},{16,20},{20,16},{24,28},{28,24},{32,36},... | collective-permute-start | bytes 12296 | tf_op jit(solution)/shard_map/ppermute | solution.py:274
  83.0 16.8 %collective-permute-start.5 = (f32[8,128]{1,0:T(8,128)S(1)}, f32[8,128]{1,0:T(8,128)S(1)}, u32[]{:S(2)}, u32[]{:S(2)}) collective-permute-start(f32[8,128]{1,0:T(8,128)S(1)} %add_add_fusion.6), channel_id=1, source_target_pairs={{0,48},{4,52},{8,56},{12,60},{16,32},{20,36},{24,40},{28,44},{32,1... | collective-permute-start | bytes 12296 | tf_op jit(solution)/shard_map/ppermute | solution.py:274
  86.5 13.3 %collective-permute-start.4 = (f32[8,128]{1,0:T(8,128)S(1)}, f32[8,128]{1,0:T(8,128)S(1)}, u32[]{:S(2)}, u32[]{:S(2)}) collective-permute-start(f32[8,128]{1,0:T(8,128)S(1)} %add_add_fusion.6), channel_id=1, source_target_pairs={{0,32},{4,36},{8,40},{12,44},{16,48},{20,52},{24,56},{28,60},{32,0... | collective-permute-start | bytes 12296 | tf_op jit(solution)/shard_map/ppermute | solution.py:274
  87.1 12.7 %collective-permute-start.3 = (f32[8,128]{1,0:T(8,128)S(1)}, f32[8,128]{1,0:T(8,128)S(1)}, u32[]{:S(2)}, u32[]{:S(2)}) collective-permute-start(f32[8,128]{1,0:T(8,128)S(1)} %add_add_fusion.6), channel_id=1, source_target_pairs={{0,16},{4,20},{8,24},{12,28},{16,0},{20,4},{24,8},{28,12},{32,48},... | collective-permute-start | bytes 12296 | tf_op jit(solution)/shard_map/ppermute | solution.py:274
  99.8 6.6 %collective-permute-start.8 = (f32[8,128]{1,0:T(8,128)S(1)}, f32[8,128]{1,0:T(8,128)S(1)}, u32[]{:S(2)}, u32[]{:S(2)}) collective-permute-start(f32[8,128]{1,0:T(8,128)S(1)} %add_add_fusion.5), channel_id=1, source_target_pairs={{0,192},{4,196},{8,200},{12,204},{16,208},{20,212},{24,216},{28,22... | collective-permute-start | bytes 12296 | tf_op jit(solution)/shard_map/ppermute | solution.py:274
  102.3 7.5 %collective-permute-start.7 = (f32[8,128]{1,0:T(8,128)S(1)}, f32[8,128]{1,0:T(8,128)S(1)}, u32[]{:S(2)}, u32[]{:S(2)}) collective-permute-start(f32[8,128]{1,0:T(8,128)S(1)} %add_add_fusion.5), channel_id=1, source_target_pairs={{0,128},{4,132},{8,136},{12,140},{16,144},{20,148},{24,152},{28,15... | collective-permute-start | bytes 12296 | tf_op jit(solution)/shard_map/ppermute | solution.py:274
  104.8 5.0 %collective-permute-start.6 = (f32[8,128]{1,0:T(8,128)S(1)}, f32[8,128]{1,0:T(8,128)S(1)}, u32[]{:S(2)}, u32[]{:S(2)}) collective-permute-start(f32[8,128]{1,0:T(8,128)S(1)} %add_add_fusion.5), channel_id=1, source_target_pairs={{0,64},{4,68},{8,72},{12,76},{16,80},{20,84},{24,88},{28,92},{32,9... | collective-permute-start | bytes 12296 | tf_op jit(solution)/shard_map/ppermute | solution.py:274
  114.5 30.7 %copy-start.10 = (bf16[512,768]{1,0:T(8,128)(2,1)S(1)}, bf16[512,768]{1,0:T(8,128)(2,1)}, u32[]{:S(2)}) copy-start(bf16[512,768]{1,0:T(8,128)(2,1)} %copy-done.9) | copy-start | bytes 2359300
  147.3 38.1 %copy-start.13 = (f32[3,256,128]{2,1,0:T(8,128)S(1)}, f32[3,256,128]{2,1,0:T(8,128)}, u32[]{:S(2)}) copy-start(f32[3,256,128]{2,1,0:T(8,128)} %copy-done.11) | copy-start | bytes 1179652
  147.3 38.1 %copy-start.15 = (f32[3,256,128]{2,1,0:T(8,128)S(1)}, f32[3,256,128]{2,1,0:T(8,128)}, u32[]{:S(2)}) copy-start(f32[3,256,128]{2,1,0:T(8,128)} %copy-done.14) | copy-start | bytes 1179652
  147.3 38.1 %all-to-all-start.4 = ((bf16[64,8,768]{2,1,0:T(8,128)(2,1)}), bf16[64,8,768]{2,1,0:T(8,128)(2,1)S(1)}, u32[]{:S(2)}, u32[]{:S(2)}) async-start(bf16[64,8,768]{2,1,0:T(8,128)(2,1)} %bitcast.11), calls=%async_computation.4 | async-start | bytes 1572864 | tf_op jit(solution)/shard_map/all_to_all | solution.py:265
  153.3 4.9 %collective-permute-start.11 = (f32[8,128]{1,0:T(8,128)S(1)}, f32[8,128]{1,0:T(8,128)S(1)}, u32[]{:S(2)}, u32[]{:S(2)}) collective-permute-start(f32[8,128]{1,0:T(8,128)S(1)} %get-tuple-element.25), channel_id=1, source_target_pairs={{0,3},{1,2},{2,1},{3,0},{4,7},{5,6},{6,5},{7,4},{8,11},{9,10},{10,... | collective-permute-start | bytes 12296 | tf_op jit(solution)/shard_map/ppermute | solution.py:274
  156.4 5.1 %collective-permute-start.10 = (f32[8,128]{1,0:T(8,128)S(1)}, f32[8,128]{1,0:T(8,128)S(1)}, u32[]{:S(2)}, u32[]{:S(2)}) collective-permute-start(f32[8,128]{1,0:T(8,128)S(1)} %get-tuple-element.25), channel_id=1, source_target_pairs={{0,2},{1,3},{2,0},{3,1},{4,6},{5,7},{6,4},{7,5},{8,10},{9,11},{10,... | collective-permute-start | bytes 12296 | tf_op jit(solution)/shard_map/ppermute | solution.py:274
  157.0 4.5 %collective-permute-start.9 = (f32[8,128]{1,0:T(8,128)S(1)}, f32[8,128]{1,0:T(8,128)S(1)}, u32[]{:S(2)}, u32[]{:S(2)}) collective-permute-start(f32[8,128]{1,0:T(8,128)S(1)} %get-tuple-element.25), channel_id=1, source_target_pairs={{0,1},{1,0},{2,3},{3,2},{4,5},{5,4},{6,7},{7,6},{8,9},{9,8},{10,11... | collective-permute-start | bytes 12296 | tf_op jit(solution)/shard_map/ppermute | solution.py:274
  161.5 3.1 %collective-permute-start.14 = (f32[8,128]{1,0:T(8,128)S(1)}, f32[8,128]{1,0:T(8,128)S(1)}, u32[]{:S(2)}, u32[]{:S(2)}) collective-permute-start(f32[8,128]{1,0:T(8,128)S(1)} %add_add_fusion.3), channel_id=1, source_target_pairs={{0,12},{4,8},{8,4},{12,0},{16,28},{20,24},{24,20},{28,16},{32,44},... | collective-permute-start | bytes 12296 | tf_op jit(solution)/shard_map/ppermute | solution.py:274
  161.6 3.7 %collective-permute-start.13 = (f32[8,128]{1,0:T(8,128)S(1)}, f32[8,128]{1,0:T(8,128)S(1)}, u32[]{:S(2)}, u32[]{:S(2)}) collective-permute-start(f32[8,128]{1,0:T(8,128)S(1)} %add_add_fusion.3), channel_id=1, source_target_pairs={{0,8},{4,12},{8,0},{12,4},{16,24},{20,28},{24,16},{28,20},{32,40},... | collective-permute-start | bytes 12296 | tf_op jit(solution)/shard_map/ppermute | solution.py:274
  162.2 3.1 %collective-permute-start.12 = (f32[8,128]{1,0:T(8,128)S(1)}, f32[8,128]{1,0:T(8,128)S(1)}, u32[]{:S(2)}, u32[]{:S(2)}) collective-permute-start(f32[8,128]{1,0:T(8,128)S(1)} %add_add_fusion.3), channel_id=1, source_target_pairs={{0,4},{4,0},{8,12},{12,8},{16,20},{20,16},{24,28},{28,24},{32,36},... | collective-permute-start | bytes 12296 | tf_op jit(solution)/shard_map/ppermute | solution.py:274
  165.3 8.6 %collective-permute-start.17 = (f32[8,128]{1,0:T(8,128)S(1)}, f32[8,128]{1,0:T(8,128)S(1)}, u32[]{:S(2)}, u32[]{:S(2)}) collective-permute-start(f32[8,128]{1,0:T(8,128)S(1)} %add_add_fusion.2), channel_id=1, source_target_pairs={{0,48},{4,52},{8,56},{12,60},{16,32},{20,36},{24,40},{28,44},{32,1... | collective-permute-start | bytes 12296 | tf_op jit(solution)/shard_map/ppermute | solution.py:274
  168.4 5.6 %collective-permute-start.16 = (f32[8,128]{1,0:T(8,128)S(1)}, f32[8,128]{1,0:T(8,128)S(1)}, u32[]{:S(2)}, u32[]{:S(2)}) collective-permute-start(f32[8,128]{1,0:T(8,128)S(1)} %add_add_fusion.2), channel_id=1, source_target_pairs={{0,32},{4,36},{8,40},{12,44},{16,48},{20,52},{24,56},{28,60},{32,0... | collective-permute-start | bytes 12296 | tf_op jit(solution)/shard_map/ppermute | solution.py:274
  169.3 5.1 %collective-permute-start.15 = (f32[8,128]{1,0:T(8,128)S(1)}, f32[8,128]{1,0:T(8,128)S(1)}, u32[]{:S(2)}, u32[]{:S(2)}) collective-permute-start(f32[8,128]{1,0:T(8,128)S(1)} %add_add_fusion.2), channel_id=1, source_target_pairs={{0,16},{4,20},{8,24},{12,28},{16,0},{20,4},{24,8},{28,12},{32,48},... | collective-permute-start | bytes 12296 | tf_op jit(solution)/shard_map/ppermute | solution.py:274
  174.4 6.5 %collective-permute-start.20 = (f32[8,128]{1,0:T(8,128)S(1)}, f32[8,128]{1,0:T(8,128)S(1)}, u32[]{:S(2)}, u32[]{:S(2)}) collective-permute-start(f32[8,128]{1,0:T(8,128)S(1)} %add_add_fusion.1), channel_id=1, source_target_pairs={{0,192},{4,196},{8,200},{12,204},{16,208},{20,212},{24,216},{28,22... | collective-permute-start | bytes 12296 | tf_op jit(solution)/shard_map/ppermute | solution.py:274
  177.9 7.5 %collective-permute-start.19 = (f32[8,128]{1,0:T(8,128)S(1)}, f32[8,128]{1,0:T(8,128)S(1)}, u32[]{:S(2)}, u32[]{:S(2)}) collective-permute-start(f32[8,128]{1,0:T(8,128)S(1)} %add_add_fusion.1), channel_id=1, source_target_pairs={{0,128},{4,132},{8,136},{12,140},{16,144},{20,148},{24,152},{28,15... | collective-permute-start | bytes 12296 | tf_op jit(solution)/shard_map/ppermute | solution.py:274
  180.0 5.4 %collective-permute-start.18 = (f32[8,128]{1,0:T(8,128)S(1)}, f32[8,128]{1,0:T(8,128)S(1)}, u32[]{:S(2)}, u32[]{:S(2)}) collective-permute-start(f32[8,128]{1,0:T(8,128)S(1)} %add_add_fusion.1), channel_id=1, source_target_pairs={{0,64},{4,68},{8,72},{12,76},{16,80},{20,84},{24,88},{28,92},{32,9... | collective-permute-start | bytes 12296 | tf_op jit(solution)/shard_map/ppermute | solution.py:274
  (7 other events, 90.5 us)

commit v5 on v4

--- a/solution.py
+++ b/solution.py
@@ -167,9 +167,9 @@
 
 def group_step(sums):
     totals = sums[0:2].sum(1, keepdims=True)
-    bb, bq = totals[0:1], totals[1:2]
-    usable = jnp.logical_and(bb > 0.0, bq > 0.0)
-    return jnp.where(usable, bb, 1.0) / jnp.where(usable, bq, 1.0)
+    bb, data = totals[0:1], totals[1:2]
+    usable = jnp.logical_and(bb > 0.0, data > 0.0)
+    return jnp.where(usable, 0.5 * data, 1.0) / jnp.where(usable, bb, 1.0)
 
 
 def final_scales(sums):
@@ -183,7 +183,9 @@
     return step_one + step_two * more, step_two * step_one
 
 
-def first_kernel(kspace_at, sampling_at, order_at, xi_at, out, kspace, sampling, order, xi, sems):
+def first_kernel(
+    kspace_at, sampling_at, order_at, xi_at, out, sum_out, kspace, sampling, order, xi, sems
+):
     copies = [pltpu.make_async_copy(order_at, order, sems.at[0])]
     copies.append(pltpu.make_async_copy(sampling_at, sampling, sems.at[1]))
     for comp in range(kspace.shape[0]):
@@ -198,42 +200,51 @@
         copies[2 + comp].wait()
         columns.append(first_masked(kspace[comp], sampling[comp], order[...]))
     copies[-1].wait()
-    out[...] = product(xi[...], jnp.concatenate(columns, 1)).astype(jnp.bfloat16)
-
-
-def kspace_kernel(portion, sampling, xf, xi, bb, out, masked_out, sums_out):
+    masked = jnp.concatenate(columns, 1)
+    out[...] = product(xi[...], masked).astype(jnp.bfloat16)
+    sum_out[...] = row_of(masked, masked)
+
+
+def kspace_kernel(portion, sampling, xf, xi, out, masked_out, sum_out):
     masked = masked_spectrum(portion[...], sampling[...], xf[...])
     masked_out[...] = masked
-    sums_out[0:1] = bb[...]
-    sums_out[1:2] = row_of(masked, masked)
-    sums_out[2:8] = jnp.zeros((6, LANES), jnp.float32)
+    sum_out[...] = row_of(masked, masked)
     out[...] = product(xi[...], masked).astype(jnp.bfloat16)
 
 
-def kspace_last_kernel(portion, sampling, xf, xi, masked_b, here, group, qq, out, sums_out):
+def kspace_last_kernel(portion, sampling, xf, xi, masked_b, group, here, bq, qq, out, sums_out):
     masked = masked_spectrum(portion[...], sampling[...], xf[...])
     out[...] = product(xi[...], masked).astype(jnp.bfloat16)
     inverse_step = 1.0 / group_step(group[...])
     earlier = masked_b[...].astype(jnp.float32)
     change = (masked.astype(jnp.float32) - earlier) * inverse_step
-    sums_out[0:2] = here[0:2]
+    sums_out[0:1] = here[0:1]
+    sums_out[1:2] = bq[...]
     sums_out[2:3] = qq[...]
     sums_out[3:4] = row_of(earlier, change)
     sums_out[4:5] = row_of(change, change)
     sums_out[5:8] = jnp.zeros((3, LANES), jnp.float32)
 
 
-def image_kernel(arrived, coils, yi, zi, zf, yf, *refs):
-    image_out, sum_out, out = refs[-3:]
+def image_kernel(arrived, coils, yi, zi, zf, yf, data, image_out, sums_out, out):
+    factors = [coil_factors(coils[coil]) for coil in range(COILS)]
+    images = combine_coils(arrived[...], factors, yi[...], zi[...])
+    for comp, image in enumerate(images):
+        image_out[comp] = image
+    sums_out[0:1] = sum(row_of(image, image) for image in images)
+    sums_out[1:2] = data[...]
+    sums_out[2:8] = jnp.zeros((6, LANES), jnp.float32)
+    out[...] = spread_out(images, factors, zf[...], yf[...])
+
+
+def image_next_kernel(arrived, coils, yi, zi, zf, yf, b, group, image_out, sum_out, out):
     factors = [coil_factors(coils[coil]) for coil in range(COILS)]
     images = combine_coils(arrived[...], factors, yi[...], zi[...])
     for comp, image in enumerate(images):
         image_out[comp] = image
     sum_out[...] = sum(row_of(image, image) for image in images)
-    if len(refs) > 3:
-        b, group = refs[:2]
-        step = group_step(group[...])
-        images = [b[comp] - step * image for comp, image in enumerate(images)]
+    step = group_step(group[...])
+    images = [b[comp] - step * image for comp, image in enumerate(images)]
     out[...] = spread_out(images, factors, zf[...], yf[...])
 
 
@@ -295,23 +306,25 @@
     sums_shape = jax.ShapeDtypeStruct((8, LANES), jnp.float32)
     square = 2 * (4 * NX) * (4 * NX) * width
 
-    def image_step(arrived, *earlier):
+    def image_step(body, arrived, earlier, sums):
         operands = [arrived, coils] + [tables[name] for name in ("yi", "zi", "zf", "yf")]
-        operands += earlier
-        return call(image_kernel, operands, [image_shape, sum_shape, sent_shape], 3 * square)
+        return call(body, operands + earlier, [image_shape, sums, sent_shape], 3 * square)
 
     first = [kspace, sampling, tables["order"], tables["xi"]]
     scratch = [pltpu.VMEM(array.shape, array.dtype) for array in first]
     scratch.append(pltpu.SemaphoreType.DMA((3 + comps,)))
-    (sent,) = call(first_kernel, first, [sent_shape], 2 * square, pltpu.HBM, scratch, 58)
-    b, bb, sent = image_step(exchange(sent))
-    operands = [exchange(sent), sampling, tables["xf"], tables["xi"], bb]
-    sent, masked_b, here = call(
-        kspace_kernel, operands, [sent_shape, sent_shape, sums_shape], 2 * square
+    sent, data = call(first_kernel, first, [sent_shape, sum_shape], 2 * square, pltpu.HBM, scratch, 58)
+    b, here, sent = image_step(image_kernel, exchange(sent), [data], sums_shape)
+    arrived, group = exchange(sent), total_of(here, GROUP_STEPS[:2])
+    arrived, group = lax.optimization_barrier((arrived, group))
+    operands = [arrived, sampling, tables["xf"], tables["xi"]]
+    sent, masked_b, bq = call(
+        kspace_kernel, operands, [sent_shape, sent_shape, sum_shape], 2 * square
     )
-    group = total_of(here, GROUP_STEPS)
-    q, qq, sent = image_step(exchange(sent), b, group)
-    operands = [exchange(sent), sampling, tables["xf"], tables["xi"], masked_b, here, group, qq]
+    sent, group = lax.optimization_barrier((sent, group))
+    group = total_of(group, GROUP_STEPS[2:])
+    q, qq, sent = image_step(image_next_kernel, exchange(sent), [b, group], sum_shape)
+    operands = [exchange(sent), sampling, tables["xf"], tables["xi"], masked_b, group, here, bq, qq]
     sent, sums = call(kspace_last_kernel, operands, [sent_shape, sums_shape], 2 * square)
     arrived = exchange(sent)
     operands = [arrived, coils, tables["yi"], tables["zi"], b, q, group, total_of(sums, STEPS)]

time: 188 us -> 182 us (0.968)
  blocking collectives: 95 us -> 64.1 us
  waiting for transfers between devices: 31.5 us -> 47.5 us
  starting transfers between devices: 43.1 us -> 49.3 us
    all_to_all x3 -> x2, blocking collectives: 95 us -> 64.1 us  [exchange(): lax.all_to_all(values, 'slab', split_axis=0, concat_axis=0, tiled=True)]
    ppermute x21, waiting for transfers between devices: 31.5 us -> 45 us  [sum_over(): lax.ppermute(values, axis, exclusive(axis, flips * low))]
    all_to_all x2 -> x3, starting transfers between devices: 11.8 us -> 18 us  [exchange(): lax.all_to_all(values, 'slab', split_axis=0, concat_axis=0, tiled=True)]
    all_to_all x2 -> x3, waiting for transfers between devices: 0.01 us -> 2.59 us  [exchange(): lax.all_to_all(values, 'slab', split_axis=0, concat_axis=0, tiled=True)]
    unnamed x32 -> x34, local copies, waits for them, and re-layouts: 3.73 us -> 5.1 us
  transfers between devices with their start and end apart: 23 -> 24, of which waited for: 11 -> 13; matrix products, arithmetic and copies ran while one was open for 0% -> 0% of each run, Pallas kernels for 0% -> 0%
where the time goes in v5:
time: 182 us; the launch traced here: 181 us
  blocking collectives  64.1 us (35%)
  starting transfers between devices  49.3 us (27%)
  waiting for transfers between devices  47.5 us (26%)
  Pallas kernels  14.2 us (8%)
  local copies, waits for them, and re-layouts  5.1 us (3%)
    all_to_all x2, blocking collectives, exchange(): lax.all_to_all(values, 'slab', split_axis=0, concat_axis=0, tiled=True)  64.1 us
    ppermute x21, waiting for transfers between devices, sum_over(): lax.ppermute(values, axis, exclusive(axis, flips * low))  45 us
    ppermute x21, starting transfers between devices, sum_over(): lax.ppermute(values, axis, exclusive(axis, flips * low))  31.3 us
    all_to_all x3, starting transfers between devices, exchange(): lax.all_to_all(values, 'slab', split_axis=0, concat_axis=0, tiled=True)  18 us
    pallas_call x6, Pallas kernels, call(): pl.pallas_call(body, out_shape=shapes, in_specs=[pl.BlockSpec(memory_spac...  14.2 us
    unnamed x34, local copies, waits for them, and re-layouts  5.1 us
  transfers between devices with their start and end apart: 24, of which 13 were waited for; matrix products, arithmetic and copies ran while one was open for 0% of the time, Pallas kernels for 0%

profile of v5, /device:TPU:2, one launch (start us, length us, event | category | flops | bytes accessed | tf_op | source)
XLA Modules:
  0.0 181.1 jit_solution(5145399390170682018)
XLA Ops:
  0.7 3.6 %shard_map.113 = (bf16[512,768]{1,0:T(8,128)(2,1)}, f32[1,128]{1,0:T(1,128)}) custom-call(bf16[3,4,128,256]{3,2,1,0:T(8,128)(2,1)} %kspace_at.1, s32[3,128,128]{2,1,0:T(8,128)} %sampling.3, bf16[256,256]{1,0:T(8,128)(2,1)} %constant.20.clone.order_at, bf16[512,512]{1,0:T(8,128)(2,1)} %constant.19.clone.xi_at.xi), custom_call_target="tpu_custom_call" | custom-call | flops 805306368 | bytes 2425344 | tf_op jit(solution)/shard_map/pallas_call | solution.py:264
  4.3 35.3 %all_to_all.56 = bf16[64,8,768]{2,1,0:T(8,128)(2,1)S(1)} all-to-all(bf16[64,8,768]{2,1,0:T(8,128)(2,1)} %bitcast.34), channel_id=1, replica_groups=mesh['slab'=64,'comp'=4] {'slab'}, dimensions={0} | all-to-all | bytes 1572864 | tf_op jit(solution)/shard_map/all_to_all | solution.py:276
  40.3 2.7 %shard_map.114 = (f32[3,256,128]{2,1,0:T(8,128)S(1)}, f32[8,128]{1,0:T(8,128)S(1)}, bf16[512,768]{1,0:T(8,128)(2,1)}) custom-call(bf16[512,768]{1,0:T(8,128)(2,1)S(1)} %bitcast.29, f32[4,256,128]{2,1,0:T(8,128)S(1)} %bitcast.31, bf16[512,512]{1,0:T(8,128)(2,1)S(1)} %copy-done.2, bf16[256,256]{1,0:T(8,128)(2,1)S(1)} %copy-done.7, ...), custom_call_target="tpu_custom_call" | custom-call | flops 1207959552 | bytes 3805696 | tf_op jit(solution)/shard_map/pallas_call | solution.py:264
  43.8 5.9 %all-to-all-start.1 = ((bf16[64,8,768]{2,1,0:T(8,128)(2,1)}), bf16[64,8,768]{2,1,0:T(8,128)(2,1)S(1)}, u32[]{:S(2)}, u32[]{:S(2)}) async-start(bf16[64,8,768]{2,1,0:T(8,128)(2,1)} %bitcast.5), calls=%async_computation.1 | async-start | bytes 1572864 | tf_op jit(solution)/shard_map/all_to_all | solution.py:276
  50.0 1.7 collective-permute-start.1
  51.7 1.3 collective-permute-done.2
  53.6 3.6 %collective-permute-start.5 = (f32[8,128]{1,0:T(8,128)S(1)}, f32[8,128]{1,0:T(8,128)S(1)}, u32[]{:S(2)}, u32[]{:S(2)}) collective-permute-start(f32[8,128]{1,0:T(8,128)S(1)} %add_add_fusion.6), channel_id=1, source_target_pairs={{0,48},{4,52},{8,56},{12,60},{16,32},{20,36},{24,40},{28,44},{32,1... | collective-permute-start | bytes 12296 | tf_op jit(solution)/shard_map/ppermute | solution.py:285
  58.7 11.8 %collective-permute-done.5 = f32[8,128]{1,0:T(8,128)S(1)} collective-permute-done((f32[8,128]{1,0:T(8,128)S(1)}, f32[8,128]{1,0:T(8,128)S(1)}, u32[]{:S(2)}, u32[]{:S(2)}) %collective-permute-start.5) | collective-permute-done | bytes 4128 | tf_op jit(solution)/shard_map/ppermute | solution.py:285
  70.5 2.6 %all-to-all-done.1 = bf16[64,8,768]{2,1,0:T(8,128)(2,1)S(1)} async-done(((bf16[64,8,768]{2,1,0:T(8,128)(2,1)}), bf16[64,8,768]{2,1,0:T(8,128)(2,1)S(1)}, u32[]{:S(2)}, u32[]{:S(2)}) %all-to-all-start.1) | async-done | bytes 786464 | tf_op jit(solution)/shard_map/all_to_all | solution.py:276
  73.0 1.9 %shard_map.115 = (bf16[512,768]{1,0:T(8,128)(2,1)}, bf16[512,768]{1,0:T(8,128)(2,1)S(1)}, f32[1,128]{1,0:T(1,128)S(1)}) custom-call(bf16[512,768]{1,0:T(8,128)(2,1)S(1)} %bitcast.26, s32[3,128,128]{2,1,0:T(8,128)S(1)} %copy-done.1, bf16[512,512]{1,0:T(8,128)(2,1)S(1)} %copy-done.4, bf16[512,512]{1,0:T(8,128)(2,1)S(1)} %copy-done.3), custom_call_target="tpu_custom_call" | custom-call | flops 805306368 | bytes 3604992 | tf_op jit(solution)/shard_map/pallas_call | solution.py:264
  75.9 6.1 %all-to-all-start.2 = ((bf16[64,8,768]{2,1,0:T(8,128)(2,1)}), bf16[64,8,768]{2,1,0:T(8,128)(2,1)S(1)}, u32[]{:S(2)}, u32[]{:S(2)}) async-start(bf16[64,8,768]{2,1,0:T(8,128)(2,1)} %bitcast.7), calls=%async_computation.2 | async-start | bytes 1572864 | tf_op jit(solution)/shard_map/all_to_all | solution.py:276
  82.0 3.9 %collective-permute-start.8 = (f32[8,128]{1,0:T(8,128)S(1)}, f32[8,128]{1,0:T(8,128)S(1)}, u32[]{:S(2)}, u32[]{:S(2)}) collective-permute-start(f32[8,128]{1,0:T(8,128)S(1)} %add_add_fusion.5), channel_id=1, source_target_pairs={{0,192},{4,196},{8,200},{12,204},{16,208},{20,212},{24,216},{28,22... | collective-permute-start | bytes 12296 | tf_op jit(solution)/shard_map/ppermute | solution.py:285
  85.9 2.1 %collective-permute-start.7 = (f32[8,128]{1,0:T(8,128)S(1)}, f32[8,128]{1,0:T(8,128)S(1)}, u32[]{:S(2)}, u32[]{:S(2)}) collective-permute-start(f32[8,128]{1,0:T(8,128)S(1)} %add_add_fusion.5), channel_id=1, source_target_pairs={{0,128},{4,132},{8,136},{12,140},{16,144},{20,148},{24,152},{28,15... | collective-permute-start | bytes 12296 | tf_op jit(solution)/shard_map/ppermute | solution.py:285
  88.6 14.7 %collective-permute-done.8 = f32[8,128]{1,0:T(8,128)S(1)} collective-permute-done((f32[8,128]{1,0:T(8,128)S(1)}, f32[8,128]{1,0:T(8,128)S(1)}, u32[]{:S(2)}, u32[]{:S(2)}) %collective-permute-start.8) | collective-permute-done | bytes 4128 | tf_op jit(solution)/shard_map/ppermute | solution.py:285
  103.3 2.2 %collective-permute-done.7 = f32[8,128]{1,0:T(8,128)S(1)} collective-permute-done((f32[8,128]{1,0:T(8,128)S(1)}, f32[8,128]{1,0:T(8,128)S(1)}, u32[]{:S(2)}, u32[]{:S(2)}) %collective-permute-start.7) | collective-permute-done | bytes 4128 | tf_op jit(solution)/shard_map/ppermute | solution.py:285
  105.5 1.0 copy-done.6
  106.6 1.0 copy-done.12
  107.6 1.8 %shard_map.116 = (f32[3,256,128]{2,1,0:T(8,128)S(1)}, f32[1,128]{1,0:T(1,128)S(1)}, bf16[512,768]{1,0:T(8,128)(2,1)S(1)}) custom-call(bf16[512,768]{1,0:T(8,128)(2,1)S(1)} %bitcast.27, f32[4,256,128]{2,1,0:T(8,128)S(1)} %bitcast.32, bf16[512,512]{1,0:T(8,128)(2,1)S(1)} %copy-done.2, bf16[256,256]{1,0:T(8,128)(2,1)S(1)} %copy-done.7, ...), custom_call_target="tpu_custom_call" | custom-call | flops 1207959552 | bytes 4198912 | tf_op jit(solution)/shard_map/pallas_call | solution.py:264
  110.1 28.8 %all_to_all.57 = bf16[64,8,768]{2,1,0:T(8,128)(2,1)S(1)} all-to-all(bf16[64,8,768]{2,1,0:T(8,128)(2,1)S(1)} %bitcast.30), channel_id=1, replica_groups=mesh['slab'=64,'comp'=4] {'slab'}, dimensions={0} | all-to-all | bytes 1572864 | tf_op jit(solution)/shard_map/all_to_all | solution.py:276
  138.9 2.1 %shard_map.117 = (bf16[512,768]{1,0:T(8,128)(2,1)}, f32[8,128]{1,0:T(8,128)S(1)}) custom-call(bf16[512,768]{1,0:T(8,128)(2,1)S(1)} %bitcast.28, s32[3,128,128]{2,1,0:T(8,128)S(1)} %copy-done.1, bf16[512,512]{1,0:T(8,128)(2,1)S(1)} %copy-done.4, bf16[512,512]{1,0:T(8,128)(2,1)S(1)} %copy-done.3, bf16[512,768]{1,0:T(8,128)(2,1)S(1)} %copy-done.10, ...), custom_call_target="tpu_custom_call" | custom-call | flops 805306368 | bytes 3617792 | tf_op jit(solution)/shard_map/pallas_call | solution.py:264
  141.0 5.9 %all-to-all-start.4 = ((bf16[64,8,768]{2,1,0:T(8,128)(2,1)}), bf16[64,8,768]{2,1,0:T(8,128)(2,1)S(1)}, u32[]{:S(2)}, u32[]{:S(2)}) async-start(bf16[64,8,768]{2,1,0:T(8,128)(2,1)} %bitcast.11), calls=%async_computation.4 | async-start | bytes 1572864 | tf_op jit(solution)/shard_map/all_to_all | solution.py:276
  147.0 3.1 %collective-permute-start.11 = (f32[8,128]{1,0:T(8,128)S(1)}, f32[8,128]{1,0:T(8,128)S(1)}, u32[]{:S(2)}, u32[]{:S(2)}) collective-permute-start(f32[8,128]{1,0:T(8,128)S(1)} %get-tuple-element.37), channel_id=1, source_target_pairs={{0,3},{1,2},{2,1},{3,0},{4,7},{5,6},{6,5},{7,4},{8,11},{9,10},{10,... | collective-permute-start | bytes 12296 | tf_op jit(solution)/shard_map/ppermute | solution.py:285
  151.9 3.3 %collective-permute-done.10 = f32[8,128]{1,0:T(8,128)S(1)} collective-permute-done((f32[8,128]{1,0:T(8,128)S(1)}, f32[8,128]{1,0:T(8,128)S(1)}, u32[]{:S(2)}, u32[]{:S(2)}) %collective-permute-start.10) | collective-permute-done | bytes 4128 | tf_op jit(solution)/shard_map/ppermute | solution.py:285
  155.9 1.2 collective-permute-start.12
  157.1 1.2 collective-permute-done.14
  159.0 3.1 %collective-permute-start.17 = (f32[8,128]{1,0:T(8,128)S(1)}, f32[8,128]{1,0:T(8,128)S(1)}, u32[]{:S(2)}, u32[]{:S(2)}) collective-permute-start(f32[8,128]{1,0:T(8,128)S(1)} %add_add_fusion.2), channel_id=1, source_target_pairs={{0,48},{4,52},{8,56},{12,60},{16,32},{20,36},{24,40},{28,44},{32,1... | collective-permute-start | bytes 12296 | tf_op jit(solution)/shard_map/ppermute | solution.py:285
  162.9 1.1 collective-permute-start.15
  164.1 3.5 %collective-permute-done.17 = f32[8,128]{1,0:T(8,128)S(1)} collective-permute-done((f32[8,128]{1,0:T(8,128)S(1)}, f32[8,128]{1,0:T(8,128)S(1)}, u32[]{:S(2)}, u32[]{:S(2)}) %collective-permute-start.17) | collective-permute-done | bytes 4128 | tf_op jit(solution)/shard_map/ppermute | solution.py:285
  168.1 3.5 %collective-permute-start.20 = (f32[8,128]{1,0:T(8,128)S(1)}, f32[8,128]{1,0:T(8,128)S(1)}, u32[]{:S(2)}, u32[]{:S(2)}) collective-permute-start(f32[8,128]{1,0:T(8,128)S(1)} %add_add_fusion.1), channel_id=1, source_target_pairs={{0,192},{4,196},{8,200},{12,204},{16,208},{20,212},{24,216},{28,22... | collective-permute-start | bytes 12296 | tf_op jit(solution)/shard_map/ppermute | solution.py:285
  171.6 2.1 %collective-permute-start.19 = (f32[8,128]{1,0:T(8,128)S(1)}, f32[8,128]{1,0:T(8,128)S(1)}, u32[]{:S(2)}, u32[]{:S(2)}) collective-permute-start(f32[8,128]{1,0:T(8,128)S(1)} %add_add_fusion.1), channel_id=1, source_target_pairs={{0,128},{4,132},{8,136},{12,140},{16,144},{20,148},{24,152},{28,15... | collective-permute-start | bytes 12296 | tf_op jit(solution)/shard_map/ppermute | solution.py:285
  174.6 4.5 %collective-permute-done.19 = f32[8,128]{1,0:T(8,128)S(1)} collective-permute-done((f32[8,128]{1,0:T(8,128)S(1)}, f32[8,128]{1,0:T(8,128)S(1)}, u32[]{:S(2)}, u32[]{:S(2)}) %collective-permute-start.19) | collective-permute-done | bytes 4128 | tf_op jit(solution)/shard_map/ppermute | solution.py:285
  179.2 2.0 %shard_map.118 = (f32[3,256,128]{2,1,0:T(8,128)}, f32[3,256,128]{2,1,0:T(8,128)}) custom-call(bf16[512,768]{1,0:T(8,128)(2,1)S(1)} %bitcast.25, f32[4,256,128]{2,1,0:T(8,128)S(1)} %bitcast.33, bf16[512,512]{1,0:T(8,128)(2,1)S(1)} %copy-done.2, bf16[256,256]{1,0:T(8,128)(2,1)S(1)} %copy-done.7, f32[3,256,128]{2,1,0:T(8,128)S(1)} %copy-done.13, ...), custom_call_target="tpu_custom_call" | custom-call | flops 805306368 | bytes 3547136 | tf_op jit(solution)/shard_map/pallas_call | solution.py:264
  (65 shorter events, 11.4 us)
Async XLA Ops:
  0.6 39.1 %copy-start.7 = (bf16[256,256]{1,0:T(8,128)(2,1)S(1)}, bf16[256,256]{1,0:T(8,128)(2,1)}, u32[]{:S(2)}) copy-start(bf16[256,256]{1,0:T(8,128)(2,1)} %constant.15.clone.zi) | copy-start | bytes 393220
  0.6 39.1 %copy-start.8 = (bf16[256,256]{1,0:T(8,128)(2,1)S(1)}, bf16[256,256]{1,0:T(8,128)(2,1)}, u32[]{:S(2)}) copy-start(bf16[256,256]{1,0:T(8,128)(2,1)} %constant.14.clone.zf) | copy-start | bytes 393220
  4.3 35.4 %copy-start = (f32[4,2,16384]{2,1,0:T(2,128)S(1)}, f32[4,2,16384]{2,1,0:T(2,128)}, u32[]{:S(2)}) copy-start(f32[4,2,16384]{2,1,0:T(2,128)} %param.11) | copy-start | bytes 1572868
  4.3 35.4 %copy-start.2 = (bf16[512,512]{1,0:T(8,128)(2,1)S(1)}, bf16[512,512]{1,0:T(8,128)(2,1)}, u32[]{:S(2)}) copy-start(bf16[512,512]{1,0:T(8,128)(2,1)} %constant.17.clone.yi) | copy-start | bytes 1572868
  4.3 35.4 %copy-start.5 = (bf16[512,512]{1,0:T(8,128)(2,1)S(1)}, bf16[512,512]{1,0:T(8,128)(2,1)}, u32[]{:S(2)}) copy-start(bf16[512,512]{1,0:T(8,128)(2,1)} %constant.16.clone.yf) | copy-start | bytes 1572868
  43.8 29.2 %copy-start.4 = (bf16[512,512]{1,0:T(8,128)(2,1)S(1)}, bf16[512,512]{1,0:T(8,128)(2,1)}, u32[]{:S(2)}) copy-start(bf16[512,512]{1,0:T(8,128)(2,1)} %constant.18.clone.xf) | copy-start | bytes 1572868
  43.8 29.2 %all-to-all-start.1 = ((bf16[64,8,768]{2,1,0:T(8,128)(2,1)}), bf16[64,8,768]{2,1,0:T(8,128)(2,1)S(1)}, u32[]{:S(2)}, u32[]{:S(2)}) async-start(bf16[64,8,768]{2,1,0:T(8,128)(2,1)} %bitcast.5), calls=%async_computation.1 | async-start | bytes 1572864 | tf_op jit(solution)/shard_map/all_to_all | solution.py:276
  49.8 3.2 %collective-permute-start.2 = (f32[8,128]{1,0:T(8,128)S(1)}, f32[8,128]{1,0:T(8,128)S(1)}, u32[]{:S(2)}, u32[]{:S(2)}) collective-permute-start(f32[8,128]{1,0:T(8,128)S(1)} %get-tuple-element.24.here), channel_id=1, source_target_pairs={{0,12},{4,8},{8,4},{12,0},{16,28},{20,24},{24,20},{28,16},{32,44},... | collective-permute-start | bytes 12296 | tf_op jit(solution)/shard_map/ppermute | solution.py:285
  50.0 3.6 %collective-permute-start.1 = (f32[8,128]{1,0:T(8,128)S(1)}, f32[8,128]{1,0:T(8,128)S(1)}, u32[]{:S(2)}, u32[]{:S(2)}) collective-permute-start(f32[8,128]{1,0:T(8,128)S(1)} %get-tuple-element.24.here), channel_id=1, source_target_pairs={{0,8},{4,12},{8,0},{12,4},{16,24},{20,28},{24,16},{28,20},{32,40},... | collective-permute-start | bytes 12296 | tf_op jit(solution)/shard_map/ppermute | solution.py:285
  51.7 1.9 %collective-permute-start = (f32[8,128]{1,0:T(8,128)S(1)}, f32[8,128]{1,0:T(8,128)S(1)}, u32[]{:S(2)}, u32[]{:S(2)}) collective-permute-start(f32[8,128]{1,0:T(8,128)S(1)} %get-tuple-element.24.here), channel_id=1, source_target_pairs={{0,4},{4,0},{8,12},{12,8},{16,20},{20,16},{24,28},{28,24},{32,36},... | collective-permute-start | bytes 12296 | tf_op jit(solution)/shard_map/ppermute | solution.py:285
  53.6 16.8 %collective-permute-start.5 = (f32[8,128]{1,0:T(8,128)S(1)}, f32[8,128]{1,0:T(8,128)S(1)}, u32[]{:S(2)}, u32[]{:S(2)}) collective-permute-start(f32[8,128]{1,0:T(8,128)S(1)} %add_add_fusion.6), channel_id=1, source_target_pairs={{0,48},{4,52},{8,56},{12,60},{16,32},{20,36},{24,40},{28,44},{32,1... | collective-permute-start | bytes 12296 | tf_op jit(solution)/shard_map/ppermute | solution.py:285
  57.2 13.3 %collective-permute-start.4 = (f32[8,128]{1,0:T(8,128)S(1)}, f32[8,128]{1,0:T(8,128)S(1)}, u32[]{:S(2)}, u32[]{:S(2)}) collective-permute-start(f32[8,128]{1,0:T(8,128)S(1)} %add_add_fusion.6), channel_id=1, source_target_pairs={{0,32},{4,36},{8,40},{12,44},{16,48},{20,52},{24,56},{28,60},{32,0... | collective-permute-start | bytes 12296 | tf_op jit(solution)/shard_map/ppermute | solution.py:285
  57.7 12.7 %collective-permute-start.3 = (f32[8,128]{1,0:T(8,128)S(1)}, f32[8,128]{1,0:T(8,128)S(1)}, u32[]{:S(2)}, u32[]{:S(2)}) collective-permute-start(f32[8,128]{1,0:T(8,128)S(1)} %add_add_fusion.6), channel_id=1, source_target_pairs={{0,16},{4,20},{8,24},{12,28},{16,0},{20,4},{24,8},{28,12},{32,48},... | collective-permute-start | bytes 12296 | tf_op jit(solution)/shard_map/ppermute | solution.py:285
  75.9 29.6 %all-to-all-start.2 = ((bf16[64,8,768]{2,1,0:T(8,128)(2,1)}), bf16[64,8,768]{2,1,0:T(8,128)(2,1)S(1)}, u32[]{:S(2)}, u32[]{:S(2)}) async-start(bf16[64,8,768]{2,1,0:T(8,128)(2,1)} %bitcast.7), calls=%async_computation.2 | async-start | bytes 1572864 | tf_op jit(solution)/shard_map/all_to_all | solution.py:276
  82.0 21.3 %collective-permute-start.8 = (f32[8,128]{1,0:T(8,128)S(1)}, f32[8,128]{1,0:T(8,128)S(1)}, u32[]{:S(2)}, u32[]{:S(2)}) collective-permute-start(f32[8,128]{1,0:T(8,128)S(1)} %add_add_fusion.5), channel_id=1, source_target_pairs={{0,192},{4,196},{8,200},{12,204},{16,208},{20,212},{24,216},{28,22... | collective-permute-start | bytes 12296 | tf_op jit(solution)/shard_map/ppermute | solution.py:285
  85.9 19.6 %collective-permute-start.7 = (f32[8,128]{1,0:T(8,128)S(1)}, f32[8,128]{1,0:T(8,128)S(1)}, u32[]{:S(2)}, u32[]{:S(2)}) collective-permute-start(f32[8,128]{1,0:T(8,128)S(1)} %add_add_fusion.5), channel_id=1, source_target_pairs={{0,128},{4,132},{8,136},{12,140},{16,144},{20,148},{24,152},{28,15... | collective-permute-start | bytes 12296 | tf_op jit(solution)/shard_map/ppermute | solution.py:285
  88.0 17.5 %collective-permute-start.6 = (f32[8,128]{1,0:T(8,128)S(1)}, f32[8,128]{1,0:T(8,128)S(1)}, u32[]{:S(2)}, u32[]{:S(2)}) collective-permute-start(f32[8,128]{1,0:T(8,128)S(1)} %add_add_fusion.5), channel_id=1, source_target_pairs={{0,64},{4,68},{8,72},{12,76},{16,80},{20,84},{24,88},{28,92},{32,9... | collective-permute-start | bytes 12296 | tf_op jit(solution)/shard_map/ppermute | solution.py:285
  141.0 38.1 %copy-start.13 = (f32[3,256,128]{2,1,0:T(8,128)S(1)}, f32[3,256,128]{2,1,0:T(8,128)}, u32[]{:S(2)}) copy-start(f32[3,256,128]{2,1,0:T(8,128)} %copy-done.11) | copy-start | bytes 1179652
  141.0 38.1 %copy-start.15 = (f32[3,256,128]{2,1,0:T(8,128)S(1)}, f32[3,256,128]{2,1,0:T(8,128)}, u32[]{:S(2)}) copy-start(f32[3,256,128]{2,1,0:T(8,128)} %copy-done.14) | copy-start | bytes 1179652
  141.0 38.1 %all-to-all-start.4 = ((bf16[64,8,768]{2,1,0:T(8,128)(2,1)}), bf16[64,8,768]{2,1,0:T(8,128)(2,1)S(1)}, u32[]{:S(2)}, u32[]{:S(2)}) async-start(bf16[64,8,768]{2,1,0:T(8,128)(2,1)} %bitcast.11), calls=%async_computation.4 | async-start | bytes 1572864 | tf_op jit(solution)/shard_map/all_to_all | solution.py:276
  147.0 4.9 %collective-permute-start.11 = (f32[8,128]{1,0:T(8,128)S(1)}, f32[8,128]{1,0:T(8,128)S(1)}, u32[]{:S(2)}, u32[]{:S(2)}) collective-permute-start(f32[8,128]{1,0:T(8,128)S(1)} %get-tuple-element.37), channel_id=1, source_target_pairs={{0,3},{1,2},{2,1},{3,0},{4,7},{5,6},{6,5},{7,4},{8,11},{9,10},{10,... | collective-permute-start | bytes 12296 | tf_op jit(solution)/shard_map/ppermute | solution.py:285
  150.1 5.1 %collective-permute-start.10 = (f32[8,128]{1,0:T(8,128)S(1)}, f32[8,128]{1,0:T(8,128)S(1)}, u32[]{:S(2)}, u32[]{:S(2)}) collective-permute-start(f32[8,128]{1,0:T(8,128)S(1)} %get-tuple-element.37), channel_id=1, source_target_pairs={{0,2},{1,3},{2,0},{3,1},{4,6},{5,7},{6,4},{7,5},{8,10},{9,11},{10,... | collective-permute-start | bytes 12296 | tf_op jit(solution)/shard_map/ppermute | solution.py:285
  150.7 4.5 %collective-permute-start.9 = (f32[8,128]{1,0:T(8,128)S(1)}, f32[8,128]{1,0:T(8,128)S(1)}, u32[]{:S(2)}, u32[]{:S(2)}) collective-permute-start(f32[8,128]{1,0:T(8,128)S(1)} %get-tuple-element.37), channel_id=1, source_target_pairs={{0,1},{1,0},{2,3},{3,2},{4,5},{5,4},{6,7},{7,6},{8,9},{9,8},{10,11... | collective-permute-start | bytes 12296 | tf_op jit(solution)/shard_map/ppermute | solution.py:285
  155.2 3.2 %collective-permute-start.14 = (f32[8,128]{1,0:T(8,128)S(1)}, f32[8,128]{1,0:T(8,128)S(1)}, u32[]{:S(2)}, u32[]{:S(2)}) collective-permute-start(f32[8,128]{1,0:T(8,128)S(1)} %add_add_fusion.3), channel_id=1, source_target_pairs={{0,12},{4,8},{8,4},{12,0},{16,28},{20,24},{24,20},{28,16},{32,44},... | collective-permute-start | bytes 12296 | tf_op jit(solution)/shard_map/ppermute | solution.py:285
  155.3 3.7 %collective-permute-start.13 = (f32[8,128]{1,0:T(8,128)S(1)}, f32[8,128]{1,0:T(8,128)S(1)}, u32[]{:S(2)}, u32[]{:S(2)}) collective-permute-start(f32[8,128]{1,0:T(8,128)S(1)} %add_add_fusion.3), channel_id=1, source_target_pairs={{0,8},{4,12},{8,0},{12,4},{16,24},{20,28},{24,16},{28,20},{32,40},... | collective-permute-start | bytes 12296 | tf_op jit(solution)/shard_map/ppermute | solution.py:285
  155.9 3.1 %collective-permute-start.12 = (f32[8,128]{1,0:T(8,128)S(1)}, f32[8,128]{1,0:T(8,128)S(1)}, u32[]{:S(2)}, u32[]{:S(2)}) collective-permute-start(f32[8,128]{1,0:T(8,128)S(1)} %add_add_fusion.3), channel_id=1, source_target_pairs={{0,4},{4,0},{8,12},{12,8},{16,20},{20,16},{24,28},{28,24},{32,36},... | collective-permute-start | bytes 12296 | tf_op jit(solution)/shard_map/ppermute | solution.py:285
  159.0 8.6 %collective-permute-start.17 = (f32[8,128]{1,0:T(8,128)S(1)}, f32[8,128]{1,0:T(8,128)S(1)}, u32[]{:S(2)}, u32[]{:S(2)}) collective-permute-start(f32[8,128]{1,0:T(8,128)S(1)} %add_add_fusion.2), channel_id=1, source_target_pairs={{0,48},{4,52},{8,56},{12,60},{16,32},{20,36},{24,40},{28,44},{32,1... | collective-permute-start | bytes 12296 | tf_op jit(solution)/shard_map/ppermute | solution.py:285
  162.1 5.6 %collective-permute-start.16 = (f32[8,128]{1,0:T(8,128)S(1)}, f32[8,128]{1,0:T(8,128)S(1)}, u32[]{:S(2)}, u32[]{:S(2)}) collective-permute-start(f32[8,128]{1,0:T(8,128)S(1)} %add_add_fusion.2), channel_id=1, source_target_pairs={{0,32},{4,36},{8,40},{12,44},{16,48},{20,52},{24,56},{28,60},{32,0... | collective-permute-start | bytes 12296 | tf_op jit(solution)/shard_map/ppermute | solution.py:285
  162.9 5.1 %collective-permute-start.15 = (f32[8,128]{1,0:T(8,128)S(1)}, f32[8,128]{1,0:T(8,128)S(1)}, u32[]{:S(2)}, u32[]{:S(2)}) collective-permute-start(f32[8,128]{1,0:T(8,128)S(1)} %add_add_fusion.2), channel_id=1, source_target_pairs={{0,16},{4,20},{8,24},{12,28},{16,0},{20,4},{24,8},{28,12},{32,48},... | collective-permute-start | bytes 12296 | tf_op jit(solution)/shard_map/ppermute | solution.py:285
  168.1 6.5 %collective-permute-start.20 = (f32[8,128]{1,0:T(8,128)S(1)}, f32[8,128]{1,0:T(8,128)S(1)}, u32[]{:S(2)}, u32[]{:S(2)}) collective-permute-start(f32[8,128]{1,0:T(8,128)S(1)} %add_add_fusion.1), channel_id=1, source_target_pairs={{0,192},{4,196},{8,200},{12,204},{16,208},{20,212},{24,216},{28,22... | collective-permute-start | bytes 12296 | tf_op jit(solution)/shard_map/ppermute | solution.py:285
  171.6 7.5 %collective-permute-start.19 = (f32[8,128]{1,0:T(8,128)S(1)}, f32[8,128]{1,0:T(8,128)S(1)}, u32[]{:S(2)}, u32[]{:S(2)}) collective-permute-start(f32[8,128]{1,0:T(8,128)S(1)} %add_add_fusion.1), channel_id=1, source_target_pairs={{0,128},{4,132},{8,136},{12,140},{16,144},{20,148},{24,152},{28,15... | collective-permute-start | bytes 12296 | tf_op jit(solution)/shard_map/ppermute | solution.py:285
  173.7 5.4 %collective-permute-start.18 = (f32[8,128]{1,0:T(8,128)S(1)}, f32[8,128]{1,0:T(8,128)S(1)}, u32[]{:S(2)}, u32[]{:S(2)}) collective-permute-start(f32[8,128]{1,0:T(8,128)S(1)} %add_add_fusion.1), channel_id=1, source_target_pairs={{0,64},{4,68},{8,72},{12,76},{16,80},{20,84},{24,88},{28,92},{32,9... | collective-permute-start | bytes 12296 | tf_op jit(solution)/shard_map/ppermute | solution.py:285
  (9 other events, 92.3 us)

commit v6 on v5

--- a/solution.py
+++ b/solution.py
@@ -205,17 +205,25 @@
     sum_out[...] = row_of(masked, masked)
 
 
-def kspace_kernel(portion, sampling, xf, xi, out, masked_out, sum_out):
+def kspace_kernel(portion, sampling, xf, xi, out, masked_at, sum_out, kept, sem):
     masked = masked_spectrum(portion[...], sampling[...], xf[...])
-    masked_out[...] = masked
+    kept[...] = masked
+    copy = pltpu.make_async_copy(kept, masked_at, sem)
+    copy.start()
+    out[...] = product(xi[...], masked).astype(jnp.bfloat16)
     sum_out[...] = row_of(masked, masked)
-    out[...] = product(xi[...], masked).astype(jnp.bfloat16)
-
-
-def kspace_last_kernel(portion, sampling, xf, xi, masked_b, group, here, bq, qq, out, sums_out):
+    copy.wait()
+
+
+def kspace_last_kernel(
+    portion, sampling, xf, xi, masked_at, group, here, bq, qq, out, sums_out, masked_b, sem
+):
+    copy = pltpu.make_async_copy(masked_at, masked_b, sem)
+    copy.start()
     masked = masked_spectrum(portion[...], sampling[...], xf[...])
     out[...] = product(xi[...], masked).astype(jnp.bfloat16)
     inverse_step = 1.0 / group_step(group[...])
+    copy.wait()
     earlier = masked_b[...].astype(jnp.float32)
     change = (masked.astype(jnp.float32) - earlier) * inverse_step
     sums_out[0:1] = here[0:1]
@@ -226,46 +234,77 @@
     sums_out[5:8] = jnp.zeros((3, LANES), jnp.float32)
 
 
-def image_kernel(arrived, coils, yi, zi, zf, yf, data, image_out, sums_out, out):
+def image_kernel(arrived, coils, yi, zi, zf, yf, data, image_at, sums_out, out, kept, sem):
     factors = [coil_factors(coils[coil]) for coil in range(COILS)]
     images = combine_coils(arrived[...], factors, yi[...], zi[...])
     for comp, image in enumerate(images):
-        image_out[comp] = image
+        kept[comp] = image
+    copy = pltpu.make_async_copy(kept, image_at, sem)
+    copy.start()
     sums_out[0:1] = sum(row_of(image, image) for image in images)
     sums_out[1:2] = data[...]
     sums_out[2:8] = jnp.zeros((6, LANES), jnp.float32)
     out[...] = spread_out(images, factors, zf[...], yf[...])
-
-
-def image_next_kernel(arrived, coils, yi, zi, zf, yf, b, group, image_out, sum_out, out):
+    copy.wait()
+
+
+def image_next_kernel(
+    arrived, coils, yi, zi, zf, yf, b_at, group, image_at, sum_out, out, kept, sem, b, b_sem
+):
+    b_copy = pltpu.make_async_copy(b_at, b, b_sem)
+    b_copy.start()
     factors = [coil_factors(coils[coil]) for coil in range(COILS)]
     images = combine_coils(arrived[...], factors, yi[...], zi[...])
     for comp, image in enumerate(images):
-        image_out[comp] = image
+        kept[comp] = image
+    copy = pltpu.make_async_copy(kept, image_at, sem)
+    copy.start()
     sum_out[...] = sum(row_of(image, image) for image in images)
+    b_copy.wait()
     step = group_step(group[...])
     images = [b[comp] - step * image for comp, image in enumerate(images)]
     out[...] = spread_out(images, factors, zf[...], yf[...])
-
-
-def last_kernel(arrived, coils, yi, zi, b, q, group, sums, coefficients, residual):
+    copy.wait()
+
+
+def last_kernel(
+    arrived, coils, yi, zi, b_at, q_at, group, sums, coefficients, residual, b, q, b_sem, q_sem
+):
+    copies = [pltpu.make_async_copy(b_at, b, b_sem), pltpu.make_async_copy(q_at, q, q_sem)]
+    for copy in copies:
+        copy.start()
     factors = [coil_factors(coils[coil]) for coil in range(COILS)]
     images = combine_coils(arrived[...], factors, yi[...], zi[...])
     along_b, along_q = final_scales(sums[...])
     along_t = along_q / group_step(group[...])
+    for copy in copies:
+        copy.wait()
     for comp, image in enumerate(images):
         coefficients[comp] = along_b * b[comp] - along_q * q[comp]
         residual[comp] = b[comp] - along_b * q[comp] + along_t * (q[comp] - image)
 
 
-def call(body, operands, shapes, flops, space=pltpu.VMEM, scratch=(), mebibytes=32):
+def call(body, operands, shapes, flops, far=(), far_out=(), scratch=(), mebibytes=32):
     held = sum(math.prod(o.shape) * o.dtype.itemsize for o in operands)
     held += sum(math.prod(s.shape) * s.dtype.itemsize for s in shapes)
+    operands = [
+        pltpu.with_memory_space_constraint(operand, pltpu.HBM) if place in far else operand
+        for place, operand in enumerate(operands)
+    ]
     return pl.pallas_call(
         body,
-        out_shape=shapes,
-        in_specs=[pl.BlockSpec(memory_space=space)] * len(operands),
-        out_specs=[pl.BlockSpec(memory_space=pltpu.VMEM)] * len(shapes),
+        out_shape=[
+            pltpu.HBM(shape.shape, shape.dtype) if place in far_out else shape
+            for place, shape in enumerate(shapes)
+        ],
+        in_specs=[
+            pl.BlockSpec(memory_space=pltpu.HBM if place in far else pltpu.VMEM)
+            for place in range(len(operands))
+        ],
+        out_specs=[
+            pl.BlockSpec(memory_space=pltpu.HBM if place in far_out else pltpu.VMEM)
+            for place in range(len(shapes))
+        ],
         scratch_shapes=scratch,
         compiler_params=pltpu.CompilerParams(vmem_limit_bytes=mebibytes * 1024 * 1024),
         cost_estimate=pl.CostEstimate(flops=flops, bytes_accessed=held, transcendentals=0),
@@ -306,29 +345,39 @@
     sums_shape = jax.ShapeDtypeStruct((8, LANES), jnp.float32)
     square = 2 * (4 * NX) * (4 * NX) * width
 
-    def image_step(body, arrived, earlier, sums):
+    sem = pltpu.SemaphoreType.DMA
+    image_kept = pltpu.VMEM(image_shape.shape, jnp.float32)
+    sent_kept = pltpu.VMEM(sent_shape.shape, jnp.bfloat16)
+
+    def image_step(body, arrived, earlier, sums, far, scratch):
         operands = [arrived, coils] + [tables[name] for name in ("yi", "zi", "zf", "yf")]
-        return call(body, operands + earlier, [image_shape, sums, sent_shape], 3 * square)
+        shapes = [image_shape, sums, sent_shape]
+        return call(body, operands + earlier, shapes, 3 * square, far, (0,), scratch)
 
     first = [kspace, sampling, tables["order"], tables["xi"]]
     scratch = [pltpu.VMEM(array.shape, array.dtype) for array in first]
     scratch.append(pltpu.SemaphoreType.DMA((3 + comps,)))
-    sent, data = call(first_kernel, first, [sent_shape, sum_shape], 2 * square, pltpu.HBM, scratch, 58)
-    b, here, sent = image_step(image_kernel, exchange(sent), [data], sums_shape)
+    sent, data = call(
+        first_kernel, first, [sent_shape, sum_shape], 2 * square, range(4), (), scratch, 58
+    )
+    b, here, sent = image_step(image_kernel, exchange(sent), [data], sums_shape, (), [image_kept, sem])
     arrived, group = exchange(sent), total_of(here, GROUP_STEPS[:2])
     arrived, group = lax.optimization_barrier((arrived, group))
     operands = [arrived, sampling, tables["xf"], tables["xi"]]
+    shapes = [sent_shape, sent_shape, sum_shape]
     sent, masked_b, bq = call(
-        kspace_kernel, operands, [sent_shape, sent_shape, sum_shape], 2 * square
+        kspace_kernel, operands, shapes, 2 * square, (), (1,), [sent_kept, sem]
     )
     sent, group = lax.optimization_barrier((sent, group))
     group = total_of(group, GROUP_STEPS[2:])
-    q, qq, sent = image_step(image_next_kernel, exchange(sent), [b, group], sum_shape)
+    scratch = [image_kept, sem, image_kept, sem]
+    q, qq, sent = image_step(image_next_kernel, exchange(sent), [b, group], sum_shape, (6,), scratch)
     operands = [exchange(sent), sampling, tables["xf"], tables["xi"], masked_b, group, here, bq, qq]
-    sent, sums = call(kspace_last_kernel, operands, [sent_shape, sums_shape], 2 * square)
+    sent, sums = call(kspace_last_kernel, operands, [sent_shape, sums_shape], 2 * square, (4,), (), [sent_kept, sem])
     arrived = exchange(sent)
     operands = [arrived, coils, tables["yi"], tables["zi"], b, q, group, total_of(sums, STEPS)]
-    outputs = call(last_kernel, operands, [image_shape] * 2, 2 * square)
+    scratch = [image_kept, image_kept, sem, sem]
+    outputs = call(last_kernel, operands, [image_shape] * 2, 2 * square, (4, 5), (), scratch)
     return tuple(
         output.reshape(comps, NY, 2, LANES).transpose(0, 2, 1, 3).reshape(comps, 2, -1)
         for output in outputs

time: 182 us -> 182 us (level)
  Pallas kernels: 14.2 us -> 18.1 us
  local copies, waits for them, and re-layouts: 5.1 us -> 1.72 us
    pallas_call x6, Pallas kernels: 14.2 us -> 18.1 us  [call(): pl.pallas_call(body, out_shape=[pltpu.HBM(shape.shape, shape.dtype) if pl...]
    unnamed x34 -> x20, local copies, waits for them, and re-layouts: 5.1 us -> 1.72 us
where the time goes in v6:
time: 182 us
  blocking collectives  64 us (35%)
  starting transfers between devices  49.2 us (27%)
  waiting for transfers between devices  47.5 us (26%)
  Pallas kernels  18.1 us (10%)
    all_to_all x2, blocking collectives, exchange(): lax.all_to_all(values, 'slab', split_axis=0, concat_axis=0, tiled=True)  64 us
    ppermute x21, waiting for transfers between devices, sum_over(): lax.ppermute(values, axis, exclusive(axis, flips * low))  45 us
    ppermute x21, starting transfers between devices, sum_over(): lax.ppermute(values, axis, exclusive(axis, flips * low))  31.3 us
    pallas_call x6, Pallas kernels, call(): pl.pallas_call(body, out_shape=[pltpu.HBM(shape.shape, shape.dtype) if pl...  18.1 us
    all_to_all x3, starting transfers between devices, exchange(): lax.all_to_all(values, 'slab', split_axis=0, concat_axis=0, tiled=True)  17.9 us
  transfers between devices with their start and end apart: 24, of which 13 were waited for; matrix products, arithmetic and copies ran while one was open for 0% of the time, Pallas kernels for 0%

profile of v6, /device:TPU:2, one launch (start us, length us, event | category | flops | bytes accessed | tf_op | source)
XLA Modules:
  0.0 181.6 jit_solution(4386778529299052300)
XLA Ops:
  0.7 3.7 %shard_map.113 = (bf16[512,768]{1,0:T(8,128)(2,1)}, f32[1,128]{1,0:T(1,128)}) custom-call(bf16[3,4,128,256]{3,2,1,0:T(8,128)(2,1)} %kspace_at.1, s32[3,128,128]{2,1,0:T(8,128)} %sampling.3, bf16[256,256]{1,0:T(8,128)(2,1)} %constant.20.clone.order_at, bf16[512,512]{1,0:T(8,128)(2,1)} %constant.19.clone.xi_at.xi), custom_call_target="tpu_custom_call" | custom-call | flops 805306368 | bytes 2425344 | tf_op jit(solution)/shard_map/pallas_call | solution.py:294
  4.4 35.3 %all_to_all.56 = bf16[64,8,768]{2,1,0:T(8,128)(2,1)S(1)} all-to-all(bf16[64,8,768]{2,1,0:T(8,128)(2,1)} %bitcast.34), channel_id=1, replica_groups=mesh['slab'=64,'comp'=4] {'slab'}, dimensions={0} | all-to-all | bytes 1572864 | tf_op jit(solution)/shard_map/all_to_all | solution.py:315
  40.4 3.3 %shard_map.114 = (f32[3,256,128]{2,1,0:T(8,128)}, f32[8,128]{1,0:T(8,128)S(1)}, bf16[512,768]{1,0:T(8,128)(2,1)}) custom-call(bf16[512,768]{1,0:T(8,128)(2,1)S(1)} %bitcast.29, f32[4,256,128]{2,1,0:T(8,128)S(1)} %bitcast.31, bf16[512,512]{1,0:T(8,128)(2,1)S(1)} %copy-done.2, bf16[256,256]{1,0:T(8,128)(2,1)S(1)} %copy-done.7, bf16[256,256]{1,0:T(8,128)(2,1)S(1)} %copy-done.8, ...), custom_call_target="tpu_custom_call" | custom-call | flops 1207959552 | bytes 3805696 | tf_op jit(solution)/shard_map/pallas_call | solution.py:294
  43.7 6.0 %all-to-all-start.1 = ((bf16[64,8,768]{2,1,0:T(8,128)(2,1)}), bf16[64,8,768]{2,1,0:T(8,128)(2,1)S(1)}, u32[]{:S(2)}, u32[]{:S(2)}) async-start(bf16[64,8,768]{2,1,0:T(8,128)(2,1)} %bitcast.5), calls=%async_computation.1 | async-start | bytes 1572864 | tf_op jit(solution)/shard_map/all_to_all | solution.py:315
  49.8 1.7 collective-permute-start.1
  51.6 1.3 collective-permute-done.2
  53.5 3.6 %collective-permute-start.5 = (f32[8,128]{1,0:T(8,128)S(1)}, f32[8,128]{1,0:T(8,128)S(1)}, u32[]{:S(2)}, u32[]{:S(2)}) collective-permute-start(f32[8,128]{1,0:T(8,128)S(1)} %add_add_fusion.6), channel_id=1, source_target_pairs={{0,48},{4,52},{8,56},{12,60},{16,32},{20,36},{24,40},{28,44},{32,1... | collective-permute-start | bytes 12296 | tf_op jit(solution)/shard_map/ppermute | solution.py:324
  57.6 1.0 collective-permute-start.3
  58.5 11.8 %collective-permute-done.5 = f32[8,128]{1,0:T(8,128)S(1)} collective-permute-done((f32[8,128]{1,0:T(8,128)S(1)}, f32[8,128]{1,0:T(8,128)S(1)}, u32[]{:S(2)}, u32[]{:S(2)}) %collective-permute-start.5) | collective-permute-done | bytes 4128 | tf_op jit(solution)/shard_map/ppermute | solution.py:324
  70.3 2.6 %all-to-all-done.1 = bf16[64,8,768]{2,1,0:T(8,128)(2,1)S(1)} async-done(((bf16[64,8,768]{2,1,0:T(8,128)(2,1)}), bf16[64,8,768]{2,1,0:T(8,128)(2,1)S(1)}, u32[]{:S(2)}, u32[]{:S(2)}) %all-to-all-start.1) | async-done | bytes 786464 | tf_op jit(solution)/shard_map/all_to_all | solution.py:315
  72.9 2.7 %shard_map.115 = (bf16[512,768]{1,0:T(8,128)(2,1)}, bf16[512,768]{1,0:T(8,128)(2,1)}, f32[1,128]{1,0:T(1,128)S(1)}) custom-call(bf16[512,768]{1,0:T(8,128)(2,1)S(1)} %bitcast.26, s32[3,128,128]{2,1,0:T(8,128)S(1)} %copy-done.1, bf16[512,512]{1,0:T(8,128)(2,1)S(1)} %copy-done.4, bf16[512,512]{1,0:T(8,128)(2,1)S(1)} %copy-done.3), custom_call_target="tpu_custom_call" | custom-call | flops 805306368 | bytes 3604992 | tf_op jit(solution)/shard_map/pallas_call | solution.py:294
  75.6 6.1 %all-to-all-start.2 = ((bf16[64,8,768]{2,1,0:T(8,128)(2,1)}), bf16[64,8,768]{2,1,0:T(8,128)(2,1)S(1)}, u32[]{:S(2)}, u32[]{:S(2)}) async-start(bf16[64,8,768]{2,1,0:T(8,128)(2,1)} %bitcast.7), calls=%async_computation.2 | async-start | bytes 1572864 | tf_op jit(solution)/shard_map/all_to_all | solution.py:315
  81.7 3.9 %collective-permute-start.8 = (f32[8,128]{1,0:T(8,128)S(1)}, f32[8,128]{1,0:T(8,128)S(1)}, u32[]{:S(2)}, u32[]{:S(2)}) collective-permute-start(f32[8,128]{1,0:T(8,128)S(1)} %add_add_fusion.5), channel_id=1, source_target_pairs={{0,192},{4,196},{8,200},{12,204},{16,208},{20,212},{24,216},{28,22... | collective-permute-start | bytes 12296 | tf_op jit(solution)/shard_map/ppermute | solution.py:324
  85.6 2.1 %collective-permute-start.7 = (f32[8,128]{1,0:T(8,128)S(1)}, f32[8,128]{1,0:T(8,128)S(1)}, u32[]{:S(2)}, u32[]{:S(2)}) collective-permute-start(f32[8,128]{1,0:T(8,128)S(1)} %add_add_fusion.5), channel_id=1, source_target_pairs={{0,128},{4,132},{8,136},{12,140},{16,144},{20,148},{24,152},{28,15... | collective-permute-start | bytes 12296 | tf_op jit(solution)/shard_map/ppermute | solution.py:324
  88.3 14.7 %collective-permute-done.8 = f32[8,128]{1,0:T(8,128)S(1)} collective-permute-done((f32[8,128]{1,0:T(8,128)S(1)}, f32[8,128]{1,0:T(8,128)S(1)}, u32[]{:S(2)}, u32[]{:S(2)}) %collective-permute-start.8) | collective-permute-done | bytes 4128 | tf_op jit(solution)/shard_map/ppermute | solution.py:324
  103.0 2.2 %collective-permute-done.7 = f32[8,128]{1,0:T(8,128)S(1)} collective-permute-done((f32[8,128]{1,0:T(8,128)S(1)}, f32[8,128]{1,0:T(8,128)S(1)}, u32[]{:S(2)}, u32[]{:S(2)}) %collective-permute-start.7) | collective-permute-done | bytes 4128 | tf_op jit(solution)/shard_map/ppermute | solution.py:324
  105.2 1.0 copy-done.6
  106.3 2.8 %shard_map.116 = (f32[3,256,128]{2,1,0:T(8,128)}, f32[1,128]{1,0:T(1,128)S(1)}, bf16[512,768]{1,0:T(8,128)(2,1)S(1)}) custom-call(bf16[512,768]{1,0:T(8,128)(2,1)S(1)} %bitcast.27, f32[4,256,128]{2,1,0:T(8,128)S(1)} %bitcast.32, bf16[512,512]{1,0:T(8,128)(2,1)S(1)} %copy-done.2, bf16[256,256]{1,0:T(8,128)(2,1)S(1)} %copy-done.7, ...), custom_call_target="tpu_custom_call" | custom-call | flops 1207959552 | bytes 4198912 | tf_op jit(solution)/shard_map/pallas_call | solution.py:294
  109.1 28.6 %all_to_all.57 = bf16[64,8,768]{2,1,0:T(8,128)(2,1)S(1)} all-to-all(bf16[64,8,768]{2,1,0:T(8,128)(2,1)S(1)} %bitcast.30), channel_id=1, replica_groups=mesh['slab'=64,'comp'=4] {'slab'}, dimensions={0} | all-to-all | bytes 1572864 | tf_op jit(solution)/shard_map/all_to_all | solution.py:315
  137.7 2.9 %shard_map.117 = (bf16[512,768]{1,0:T(8,128)(2,1)}, f32[8,128]{1,0:T(8,128)S(1)}) custom-call(bf16[512,768]{1,0:T(8,128)(2,1)S(1)} %bitcast.28, s32[3,128,128]{2,1,0:T(8,128)S(1)} %copy-done.1, bf16[512,512]{1,0:T(8,128)(2,1)S(1)} %copy-done.4, bf16[512,512]{1,0:T(8,128)(2,1)S(1)} %copy-done.3, bf16[512,768]{1,0:T(8,128)(2,1)} %get-tuple-element.32.masked_at, ...), custom_call_target="tpu_custom_call" | custom-call | flops 805306368 | bytes 3617792 | tf_op jit(solution)/shard_map/pallas_call | solution.py:294
  140.6 5.8 %all-to-all-start.4 = ((bf16[64,8,768]{2,1,0:T(8,128)(2,1)}), bf16[64,8,768]{2,1,0:T(8,128)(2,1)S(1)}, u32[]{:S(2)}, u32[]{:S(2)}) async-start(bf16[64,8,768]{2,1,0:T(8,128)(2,1)} %bitcast.11), calls=%async_computation.4 | async-start | bytes 1572864 | tf_op jit(solution)/shard_map/all_to_all | solution.py:315
  146.5 3.1 %collective-permute-start.11 = (f32[8,128]{1,0:T(8,128)S(1)}, f32[8,128]{1,0:T(8,128)S(1)}, u32[]{:S(2)}, u32[]{:S(2)}) collective-permute-start(f32[8,128]{1,0:T(8,128)S(1)} %get-tuple-element.37), channel_id=1, source_target_pairs={{0,3},{1,2},{2,1},{3,0},{4,7},{5,6},{6,5},{7,4},{8,11},{9,10},{10,... | collective-permute-start | bytes 12296 | tf_op jit(solution)/shard_map/ppermute | solution.py:324
  151.4 3.3 %collective-permute-done.10 = f32[8,128]{1,0:T(8,128)S(1)} collective-permute-done((f32[8,128]{1,0:T(8,128)S(1)}, f32[8,128]{1,0:T(8,128)S(1)}, u32[]{:S(2)}, u32[]{:S(2)}) %collective-permute-start.10) | collective-permute-done | bytes 4128 | tf_op jit(solution)/shard_map/ppermute | solution.py:324
  155.4 1.2 collective-permute-start.12
  156.6 1.2 collective-permute-done.14
  158.5 3.1 %collective-permute-start.17 = (f32[8,128]{1,0:T(8,128)S(1)}, f32[8,128]{1,0:T(8,128)S(1)}, u32[]{:S(2)}, u32[]{:S(2)}) collective-permute-start(f32[8,128]{1,0:T(8,128)S(1)} %add_add_fusion.2), channel_id=1, source_target_pairs={{0,48},{4,52},{8,56},{12,60},{16,32},{20,36},{24,40},{28,44},{32,1... | collective-permute-start | bytes 12296 | tf_op jit(solution)/shard_map/ppermute | solution.py:324
  162.5 1.1 collective-permute-start.15
  163.6 3.5 %collective-permute-done.17 = f32[8,128]{1,0:T(8,128)S(1)} collective-permute-done((f32[8,128]{1,0:T(8,128)S(1)}, f32[8,128]{1,0:T(8,128)S(1)}, u32[]{:S(2)}, u32[]{:S(2)}) %collective-permute-start.17) | collective-permute-done | bytes 4128 | tf_op jit(solution)/shard_map/ppermute | solution.py:324
  167.6 3.5 %collective-permute-start.20 = (f32[8,128]{1,0:T(8,128)S(1)}, f32[8,128]{1,0:T(8,128)S(1)}, u32[]{:S(2)}, u32[]{:S(2)}) collective-permute-start(f32[8,128]{1,0:T(8,128)S(1)} %add_add_fusion.1), channel_id=1, source_target_pairs={{0,192},{4,196},{8,200},{12,204},{16,208},{20,212},{24,216},{28,22... | collective-permute-start | bytes 12296 | tf_op jit(solution)/shard_map/ppermute | solution.py:324
  171.1 2.1 %collective-permute-start.19 = (f32[8,128]{1,0:T(8,128)S(1)}, f32[8,128]{1,0:T(8,128)S(1)}, u32[]{:S(2)}, u32[]{:S(2)}) collective-permute-start(f32[8,128]{1,0:T(8,128)S(1)} %add_add_fusion.1), channel_id=1, source_target_pairs={{0,128},{4,132},{8,136},{12,140},{16,144},{20,148},{24,152},{28,15... | collective-permute-start | bytes 12296 | tf_op jit(solution)/shard_map/ppermute | solution.py:324
  174.1 4.5 %collective-permute-done.19 = f32[8,128]{1,0:T(8,128)S(1)} collective-permute-done((f32[8,128]{1,0:T(8,128)S(1)}, f32[8,128]{1,0:T(8,128)S(1)}, u32[]{:S(2)}, u32[]{:S(2)}) %collective-permute-start.19) | collective-permute-done | bytes 4128 | tf_op jit(solution)/shard_map/ppermute | solution.py:324
  178.7 2.8 %shard_map.118 = (f32[3,256,128]{2,1,0:T(8,128)}, f32[3,256,128]{2,1,0:T(8,128)}) custom-call(bf16[512,768]{1,0:T(8,128)(2,1)S(1)} %bitcast.25, f32[4,256,128]{2,1,0:T(8,128)S(1)} %bitcast.33, bf16[512,512]{1,0:T(8,128)(2,1)S(1)} %copy-done.2, bf16[256,256]{1,0:T(8,128)(2,1)S(1)} %copy-done.7, f32[3,256,128]{2,1,0:T(8,128)} %get-tuple-element.29.b_at, ...), custom_call_target="tpu_custom_call" | custom-call | flops 805306368 | bytes 3547136 | tf_op jit(solution)/shard_map/pallas_call | solution.py:294
  (51 shorter events, 8.1 us)
Async XLA Ops:
  0.6 39.1 %copy-start.7 = (bf16[256,256]{1,0:T(8,128)(2,1)S(1)}, bf16[256,256]{1,0:T(8,128)(2,1)}, u32[]{:S(2)}) copy-start(bf16[256,256]{1,0:T(8,128)(2,1)} %constant.15.clone.zi) | copy-start | bytes 393220
  0.6 39.1 %copy-start.8 = (bf16[256,256]{1,0:T(8,128)(2,1)S(1)}, bf16[256,256]{1,0:T(8,128)(2,1)}, u32[]{:S(2)}) copy-start(bf16[256,256]{1,0:T(8,128)(2,1)} %constant.14.clone.zf) | copy-start | bytes 393220
  4.3 35.4 %copy-start = (f32[4,2,16384]{2,1,0:T(2,128)S(1)}, f32[4,2,16384]{2,1,0:T(2,128)}, u32[]{:S(2)}) copy-start(f32[4,2,16384]{2,1,0:T(2,128)} %param.11) | copy-start | bytes 1572868
  4.3 35.4 %copy-start.2 = (bf16[512,512]{1,0:T(8,128)(2,1)S(1)}, bf16[512,512]{1,0:T(8,128)(2,1)}, u32[]{:S(2)}) copy-start(bf16[512,512]{1,0:T(8,128)(2,1)} %constant.17.clone.yi) | copy-start | bytes 1572868
  4.3 35.4 %copy-start.5 = (bf16[512,512]{1,0:T(8,128)(2,1)S(1)}, bf16[512,512]{1,0:T(8,128)(2,1)}, u32[]{:S(2)}) copy-start(bf16[512,512]{1,0:T(8,128)(2,1)} %constant.16.clone.yf) | copy-start | bytes 1572868
  43.6 29.3 %copy-start.1 = (s32[3,128,128]{2,1,0:T(8,128)S(1)}, s32[3,128,128]{2,1,0:T(8,128)}, u32[]{:S(2)}) copy-start(s32[3,128,128]{2,1,0:T(8,128)} %sampling.3) | copy-start | bytes 589828
  43.6 29.3 %copy-start.3 = (bf16[512,512]{1,0:T(8,128)(2,1)S(1)}, bf16[512,512]{1,0:T(8,128)(2,1)}, u32[]{:S(2)}) copy-start(bf16[512,512]{1,0:T(8,128)(2,1)} %constant.19.clone.xi_at.xi) | copy-start | bytes 1572868
  43.6 29.3 %copy-start.4 = (bf16[512,512]{1,0:T(8,128)(2,1)S(1)}, bf16[512,512]{1,0:T(8,128)(2,1)}, u32[]{:S(2)}) copy-start(bf16[512,512]{1,0:T(8,128)(2,1)} %constant.18.clone.xf) | copy-start | bytes 1572868
  43.7 29.2 %all-to-all-start.1 = ((bf16[64,8,768]{2,1,0:T(8,128)(2,1)}), bf16[64,8,768]{2,1,0:T(8,128)(2,1)S(1)}, u32[]{:S(2)}, u32[]{:S(2)}) async-start(bf16[64,8,768]{2,1,0:T(8,128)(2,1)} %bitcast.5), calls=%async_computation.1 | async-start | bytes 1572864 | tf_op jit(solution)/shard_map/all_to_all | solution.py:315
  49.6 3.2 %collective-permute-start.2 = (f32[8,128]{1,0:T(8,128)S(1)}, f32[8,128]{1,0:T(8,128)S(1)}, u32[]{:S(2)}, u32[]{:S(2)}) collective-permute-start(f32[8,128]{1,0:T(8,128)S(1)} %get-tuple-element.24.here), channel_id=1, source_target_pairs={{0,12},{4,8},{8,4},{12,0},{16,28},{20,24},{24,20},{28,16},{32,44},... | collective-permute-start | bytes 12296 | tf_op jit(solution)/shard_map/ppermute | solution.py:324
  49.8 3.6 %collective-permute-start.1 = (f32[8,128]{1,0:T(8,128)S(1)}, f32[8,128]{1,0:T(8,128)S(1)}, u32[]{:S(2)}, u32[]{:S(2)}) collective-permute-start(f32[8,128]{1,0:T(8,128)S(1)} %get-tuple-element.24.here), channel_id=1, source_target_pairs={{0,8},{4,12},{8,0},{12,4},{16,24},{20,28},{24,16},{28,20},{32,40},... | collective-permute-start | bytes 12296 | tf_op jit(solution)/shard_map/ppermute | solution.py:324
  51.5 1.9 %collective-permute-start = (f32[8,128]{1,0:T(8,128)S(1)}, f32[8,128]{1,0:T(8,128)S(1)}, u32[]{:S(2)}, u32[]{:S(2)}) collective-permute-start(f32[8,128]{1,0:T(8,128)S(1)} %get-tuple-element.24.here), channel_id=1, source_target_pairs={{0,4},{4,0},{8,12},{12,8},{16,20},{20,16},{24,28},{28,24},{32,36},... | collective-permute-start | bytes 12296 | tf_op jit(solution)/shard_map/ppermute | solution.py:324
  53.5 16.8 %collective-permute-start.5 = (f32[8,128]{1,0:T(8,128)S(1)}, f32[8,128]{1,0:T(8,128)S(1)}, u32[]{:S(2)}, u32[]{:S(2)}) collective-permute-start(f32[8,128]{1,0:T(8,128)S(1)} %add_add_fusion.6), channel_id=1, source_target_pairs={{0,48},{4,52},{8,56},{12,60},{16,32},{20,36},{24,40},{28,44},{32,1... | collective-permute-start | bytes 12296 | tf_op jit(solution)/shard_map/ppermute | solution.py:324
  57.0 13.3 %collective-permute-start.4 = (f32[8,128]{1,0:T(8,128)S(1)}, f32[8,128]{1,0:T(8,128)S(1)}, u32[]{:S(2)}, u32[]{:S(2)}) collective-permute-start(f32[8,128]{1,0:T(8,128)S(1)} %add_add_fusion.6), channel_id=1, source_target_pairs={{0,32},{4,36},{8,40},{12,44},{16,48},{20,52},{24,56},{28,60},{32,0... | collective-permute-start | bytes 12296 | tf_op jit(solution)/shard_map/ppermute | solution.py:324
  57.6 12.7 %collective-permute-start.3 = (f32[8,128]{1,0:T(8,128)S(1)}, f32[8,128]{1,0:T(8,128)S(1)}, u32[]{:S(2)}, u32[]{:S(2)}) collective-permute-start(f32[8,128]{1,0:T(8,128)S(1)} %add_add_fusion.6), channel_id=1, source_target_pairs={{0,16},{4,20},{8,24},{12,28},{16,0},{20,4},{24,8},{28,12},{32,48},... | collective-permute-start | bytes 12296 | tf_op jit(solution)/shard_map/ppermute | solution.py:324
  75.6 29.6 %all-to-all-start.2 = ((bf16[64,8,768]{2,1,0:T(8,128)(2,1)}), bf16[64,8,768]{2,1,0:T(8,128)(2,1)S(1)}, u32[]{:S(2)}, u32[]{:S(2)}) async-start(bf16[64,8,768]{2,1,0:T(8,128)(2,1)} %bitcast.7), calls=%async_computation.2 | async-start | bytes 1572864 | tf_op jit(solution)/shard_map/all_to_all | solution.py:315
  81.7 21.3 %collective-permute-start.8 = (f32[8,128]{1,0:T(8,128)S(1)}, f32[8,128]{1,0:T(8,128)S(1)}, u32[]{:S(2)}, u32[]{:S(2)}) collective-permute-start(f32[8,128]{1,0:T(8,128)S(1)} %add_add_fusion.5), channel_id=1, source_target_pairs={{0,192},{4,196},{8,200},{12,204},{16,208},{20,212},{24,216},{28,22... | collective-permute-start | bytes 12296 | tf_op jit(solution)/shard_map/ppermute | solution.py:324
  85.6 19.6 %collective-permute-start.7 = (f32[8,128]{1,0:T(8,128)S(1)}, f32[8,128]{1,0:T(8,128)S(1)}, u32[]{:S(2)}, u32[]{:S(2)}) collective-permute-start(f32[8,128]{1,0:T(8,128)S(1)} %add_add_fusion.5), channel_id=1, source_target_pairs={{0,128},{4,132},{8,136},{12,140},{16,144},{20,148},{24,152},{28,15... | collective-permute-start | bytes 12296 | tf_op jit(solution)/shard_map/ppermute | solution.py:324
  87.7 17.5 %collective-permute-start.6 = (f32[8,128]{1,0:T(8,128)S(1)}, f32[8,128]{1,0:T(8,128)S(1)}, u32[]{:S(2)}, u32[]{:S(2)}) collective-permute-start(f32[8,128]{1,0:T(8,128)S(1)} %add_add_fusion.5), channel_id=1, source_target_pairs={{0,64},{4,68},{8,72},{12,76},{16,80},{20,84},{24,88},{28,92},{32,9... | collective-permute-start | bytes 12296 | tf_op jit(solution)/shard_map/ppermute | solution.py:324
  140.6 38.0 %all-to-all-start.4 = ((bf16[64,8,768]{2,1,0:T(8,128)(2,1)}), bf16[64,8,768]{2,1,0:T(8,128)(2,1)S(1)}, u32[]{:S(2)}, u32[]{:S(2)}) async-start(bf16[64,8,768]{2,1,0:T(8,128)(2,1)} %bitcast.11), calls=%async_computation.4 | async-start | bytes 1572864 | tf_op jit(solution)/shard_map/all_to_all | solution.py:315
  146.5 4.9 %collective-permute-start.11 = (f32[8,128]{1,0:T(8,128)S(1)}, f32[8,128]{1,0:T(8,128)S(1)}, u32[]{:S(2)}, u32[]{:S(2)}) collective-permute-start(f32[8,128]{1,0:T(8,128)S(1)} %get-tuple-element.37), channel_id=1, source_target_pairs={{0,3},{1,2},{2,1},{3,0},{4,7},{5,6},{6,5},{7,4},{8,11},{9,10},{10,... | collective-permute-start | bytes 12296 | tf_op jit(solution)/shard_map/ppermute | solution.py:324
  149.6 5.1 %collective-permute-start.10 = (f32[8,128]{1,0:T(8,128)S(1)}, f32[8,128]{1,0:T(8,128)S(1)}, u32[]{:S(2)}, u32[]{:S(2)}) collective-permute-start(f32[8,128]{1,0:T(8,128)S(1)} %get-tuple-element.37), channel_id=1, source_target_pairs={{0,2},{1,3},{2,0},{3,1},{4,6},{5,7},{6,4},{7,5},{8,10},{9,11},{10,... | collective-permute-start | bytes 12296 | tf_op jit(solution)/shard_map/ppermute | solution.py:324
  150.2 4.5 %collective-permute-start.9 = (f32[8,128]{1,0:T(8,128)S(1)}, f32[8,128]{1,0:T(8,128)S(1)}, u32[]{:S(2)}, u32[]{:S(2)}) collective-permute-start(f32[8,128]{1,0:T(8,128)S(1)} %get-tuple-element.37), channel_id=1, source_target_pairs={{0,1},{1,0},{2,3},{3,2},{4,5},{5,4},{6,7},{7,6},{8,9},{9,8},{10,11... | collective-permute-start | bytes 12296 | tf_op jit(solution)/shard_map/ppermute | solution.py:324
  154.7 3.2 %collective-permute-start.14 = (f32[8,128]{1,0:T(8,128)S(1)}, f32[8,128]{1,0:T(8,128)S(1)}, u32[]{:S(2)}, u32[]{:S(2)}) collective-permute-start(f32[8,128]{1,0:T(8,128)S(1)} %add_add_fusion.3), channel_id=1, source_target_pairs={{0,12},{4,8},{8,4},{12,0},{16,28},{20,24},{24,20},{28,16},{32,44},... | collective-permute-start | bytes 12296 | tf_op jit(solution)/shard_map/ppermute | solution.py:324
  154.8 3.7 %collective-permute-start.13 = (f32[8,128]{1,0:T(8,128)S(1)}, f32[8,128]{1,0:T(8,128)S(1)}, u32[]{:S(2)}, u32[]{:S(2)}) collective-permute-start(f32[8,128]{1,0:T(8,128)S(1)} %add_add_fusion.3), channel_id=1, source_target_pairs={{0,8},{4,12},{8,0},{12,4},{16,24},{20,28},{24,16},{28,20},{32,40},... | collective-permute-start | bytes 12296 | tf_op jit(solution)/shard_map/ppermute | solution.py:324
  155.4 3.1 %collective-permute-start.12 = (f32[8,128]{1,0:T(8,128)S(1)}, f32[8,128]{1,0:T(8,128)S(1)}, u32[]{:S(2)}, u32[]{:S(2)}) collective-permute-start(f32[8,128]{1,0:T(8,128)S(1)} %add_add_fusion.3), channel_id=1, source_target_pairs={{0,4},{4,0},{8,12},{12,8},{16,20},{20,16},{24,28},{28,24},{32,36},... | collective-permute-start | bytes 12296 | tf_op jit(solution)/shard_map/ppermute | solution.py:324
  158.5 8.6 %collective-permute-start.17 = (f32[8,128]{1,0:T(8,128)S(1)}, f32[8,128]{1,0:T(8,128)S(1)}, u32[]{:S(2)}, u32[]{:S(2)}) collective-permute-start(f32[8,128]{1,0:T(8,128)S(1)} %add_add_fusion.2), channel_id=1, source_target_pairs={{0,48},{4,52},{8,56},{12,60},{16,32},{20,36},{24,40},{28,44},{32,1... | collective-permute-start | bytes 12296 | tf_op jit(solution)/shard_map/ppermute | solution.py:324
  161.6 5.6 %collective-permute-start.16 = (f32[8,128]{1,0:T(8,128)S(1)}, f32[8,128]{1,0:T(8,128)S(1)}, u32[]{:S(2)}, u32[]{:S(2)}) collective-permute-start(f32[8,128]{1,0:T(8,128)S(1)} %add_add_fusion.2), channel_id=1, source_target_pairs={{0,32},{4,36},{8,40},{12,44},{16,48},{20,52},{24,56},{28,60},{32,0... | collective-permute-start | bytes 12296 | tf_op jit(solution)/shard_map/ppermute | solution.py:324
  162.5 5.1 %collective-permute-start.15 = (f32[8,128]{1,0:T(8,128)S(1)}, f32[8,128]{1,0:T(8,128)S(1)}, u32[]{:S(2)}, u32[]{:S(2)}) collective-permute-start(f32[8,128]{1,0:T(8,128)S(1)} %add_add_fusion.2), channel_id=1, source_target_pairs={{0,16},{4,20},{8,24},{12,28},{16,0},{20,4},{24,8},{28,12},{32,48},... | collective-permute-start | bytes 12296 | tf_op jit(solution)/shard_map/ppermute | solution.py:324
  167.6 6.5 %collective-permute-start.20 = (f32[8,128]{1,0:T(8,128)S(1)}, f32[8,128]{1,0:T(8,128)S(1)}, u32[]{:S(2)}, u32[]{:S(2)}) collective-permute-start(f32[8,128]{1,0:T(8,128)S(1)} %add_add_fusion.1), channel_id=1, source_target_pairs={{0,192},{4,196},{8,200},{12,204},{16,208},{20,212},{24,216},{28,22... | collective-permute-start | bytes 12296 | tf_op jit(solution)/shard_map/ppermute | solution.py:324
  171.1 7.5 %collective-permute-start.19 = (f32[8,128]{1,0:T(8,128)S(1)}, f32[8,128]{1,0:T(8,128)S(1)}, u32[]{:S(2)}, u32[]{:S(2)}) collective-permute-start(f32[8,128]{1,0:T(8,128)S(1)} %add_add_fusion.1), channel_id=1, source_target_pairs={{0,128},{4,132},{8,136},{12,140},{16,144},{20,148},{24,152},{28,15... | collective-permute-start | bytes 12296 | tf_op jit(solution)/shard_map/ppermute | solution.py:324
  173.2 5.4 %collective-permute-start.18 = (f32[8,128]{1,0:T(8,128)S(1)}, f32[8,128]{1,0:T(8,128)S(1)}, u32[]{:S(2)}, u32[]{:S(2)}) collective-permute-start(f32[8,128]{1,0:T(8,128)S(1)} %add_add_fusion.1), channel_id=1, source_target_pairs={{0,64},{4,68},{8,72},{12,76},{16,80},{20,84},{24,88},{28,92},{32,9... | collective-permute-start | bytes 12296 | tf_op jit(solution)/shard_map/ppermute | solution.py:324
  (2 other events, 1.7 us)

commit v7 on v5

--- a/solution.py
+++ b/solution.py
@@ -205,24 +205,22 @@
     sum_out[...] = row_of(masked, masked)
 
 
-def kspace_kernel(portion, sampling, xf, xi, out, masked_out, sum_out):
+def kspace_kernel(portion, sampling, xf, xi, out, sum_out):
     masked = masked_spectrum(portion[...], sampling[...], xf[...])
-    masked_out[...] = masked
     sum_out[...] = row_of(masked, masked)
     out[...] = product(xi[...], masked).astype(jnp.bfloat16)
 
 
-def kspace_last_kernel(portion, sampling, xf, xi, masked_b, group, here, bq, qq, out, sums_out):
+def kspace_last_kernel(portion, sampling, xf, xi, group, here, bq, image_sums, out, sums_out):
     masked = masked_spectrum(portion[...], sampling[...], xf[...])
     out[...] = product(xi[...], masked).astype(jnp.bfloat16)
     inverse_step = 1.0 / group_step(group[...])
-    earlier = masked_b[...].astype(jnp.float32)
-    change = (masked.astype(jnp.float32) - earlier) * inverse_step
+    qp = image_sums[1:2]
     sums_out[0:1] = here[0:1]
     sums_out[1:2] = bq[...]
-    sums_out[2:3] = qq[...]
-    sums_out[3:4] = row_of(earlier, change)
-    sums_out[4:5] = row_of(change, change)
+    sums_out[2:3] = image_sums[0:1]
+    sums_out[3:4] = (qp - bq[...]) * inverse_step
+    sums_out[4:5] = (bq[...] - 2.0 * qp + row_of(masked, masked)) * (inverse_step * inverse_step)
     sums_out[5:8] = jnp.zeros((3, LANES), jnp.float32)
 
 
@@ -237,15 +235,17 @@
     out[...] = spread_out(images, factors, zf[...], yf[...])
 
 
-def image_next_kernel(arrived, coils, yi, zi, zf, yf, b, group, image_out, sum_out, out):
+def image_next_kernel(arrived, coils, yi, zi, zf, yf, b, group, image_out, sums_out, out):
     factors = [coil_factors(coils[coil]) for coil in range(COILS)]
     images = combine_coils(arrived[...], factors, yi[...], zi[...])
     for comp, image in enumerate(images):
         image_out[comp] = image
-    sum_out[...] = sum(row_of(image, image) for image in images)
     step = group_step(group[...])
-    images = [b[comp] - step * image for comp, image in enumerate(images)]
-    out[...] = spread_out(images, factors, zf[...], yf[...])
+    moved = [b[comp] - step * image for comp, image in enumerate(images)]
+    sums_out[0:1] = sum(row_of(image, image) for image in images)
+    sums_out[1:2] = sum(row_of(image, other) for image, other in zip(images, moved))
+    sums_out[2:8] = jnp.zeros((6, LANES), jnp.float32)
+    out[...] = spread_out(moved, factors, zf[...], yf[...])
 
 
 def last_kernel(arrived, coils, yi, zi, b, q, group, sums, coefficients, residual):
@@ -318,13 +318,11 @@
     arrived, group = exchange(sent), total_of(here, GROUP_STEPS[:2])
     arrived, group = lax.optimization_barrier((arrived, group))
     operands = [arrived, sampling, tables["xf"], tables["xi"]]
-    sent, masked_b, bq = call(
-        kspace_kernel, operands, [sent_shape, sent_shape, sum_shape], 2 * square
-    )
+    sent, bq = call(kspace_kernel, operands, [sent_shape, sum_shape], 2 * square)
     sent, group = lax.optimization_barrier((sent, group))
     group = total_of(group, GROUP_STEPS[2:])
-    q, qq, sent = image_step(image_next_kernel, exchange(sent), [b, group], sum_shape)
-    operands = [exchange(sent), sampling, tables["xf"], tables["xi"], masked_b, group, here, bq, qq]
+    q, image_sums, sent = image_step(image_next_kernel, exchange(sent), [b, group], sums_shape)
+    operands = [exchange(sent), sampling, tables["xf"], tables["xi"], group, here, bq, image_sums]
     sent, sums = call(kspace_last_kernel, operands, [sent_shape, sums_shape], 2 * square)
     arrived = exchange(sent)
     operands = [arrived, coils, tables["yi"], tables["zi"], b, q, group, total_of(sums, STEPS)]

time: 182 us -> 180 us (0.989)
    unnamed x34 -> x30, local copies, waits for them, and re-layouts: 5.1 us -> 3.46 us
where the time goes in v7:
time: 180 us; the launch traced here: 179 us
  blocking collectives  64 us (36%)
  starting transfers between devices  49.3 us (27%)
  waiting for transfers between devices  47.5 us (26%)
  Pallas kernels  14.1 us (8%)
  local copies, waits for them, and re-layouts  3.46 us (2%)
    all_to_all x2, blocking collectives, exchange(): lax.all_to_all(values, 'slab', split_axis=0, concat_axis=0, tiled=True)  64 us
    ppermute x21, waiting for transfers between devices, sum_over(): lax.ppermute(values, axis, exclusive(axis, flips * low))  45 us
    ppermute x21, starting transfers between devices, sum_over(): lax.ppermute(values, axis, exclusive(axis, flips * low))  31.3 us
    all_to_all x3, starting transfers between devices, exchange(): lax.all_to_all(values, 'slab', split_axis=0, concat_axis=0, tiled=True)  18 us
    pallas_call x6, Pallas kernels, call(): pl.pallas_call(body, out_shape=shapes, in_specs=[pl.BlockSpec(memory_spac...  14.1 us
  transfers between devices with their start and end apart: 24, of which 13 were waited for; matrix products, arithmetic and copies ran while one was open for 0% of the time, Pallas kernels for 0%

profile of v7, /device:TPU:2, one launch (start us, length us, event | category | flops | bytes accessed | tf_op | source)
XLA Modules:
  0.0 179.3 jit_solution(11440730864722547793)
XLA Ops:
  0.7 3.7 %shard_map.113 = (bf16[512,768]{1,0:T(8,128)(2,1)}, f32[1,128]{1,0:T(1,128)}) custom-call(bf16[3,4,128,256]{3,2,1,0:T(8,128)(2,1)} %kspace_at.1, s32[3,128,128]{2,1,0:T(8,128)} %sampling.3, bf16[256,256]{1,0:T(8,128)(2,1)} %constant.20.clone.order_at, bf16[512,512]{1,0:T(8,128)(2,1)} %constant.19.clone.xi_at.xi), custom_call_target="tpu_custom_call" | custom-call | flops 805306368 | bytes 2425344 | tf_op jit(solution)/shard_map/pallas_call | solution.py:264
  4.4 35.3 %all_to_all.56 = bf16[64,8,768]{2,1,0:T(8,128)(2,1)S(1)} all-to-all(bf16[64,8,768]{2,1,0:T(8,128)(2,1)} %bitcast.34), channel_id=1, replica_groups=mesh['slab'=64,'comp'=4] {'slab'}, dimensions={0} | all-to-all | bytes 1572864 | tf_op jit(solution)/shard_map/all_to_all | solution.py:276
  40.4 2.7 %shard_map.114 = (f32[3,256,128]{2,1,0:T(8,128)S(1)}, f32[8,128]{1,0:T(8,128)S(1)}, bf16[512,768]{1,0:T(8,128)(2,1)}) custom-call(bf16[512,768]{1,0:T(8,128)(2,1)S(1)} %bitcast.29, f32[4,256,128]{2,1,0:T(8,128)S(1)} %bitcast.31, bf16[512,512]{1,0:T(8,128)(2,1)S(1)} %copy-done.2, bf16[256,256]{1,0:T(8,128)(2,1)S(1)} %copy-done.7, ...), custom_call_target="tpu_custom_call" | custom-call | flops 1207959552 | bytes 3805696 | tf_op jit(solution)/shard_map/pallas_call | solution.py:264
  43.8 5.9 %all-to-all-start.1 = ((bf16[64,8,768]{2,1,0:T(8,128)(2,1)}), bf16[64,8,768]{2,1,0:T(8,128)(2,1)S(1)}, u32[]{:S(2)}, u32[]{:S(2)}) async-start(bf16[64,8,768]{2,1,0:T(8,128)(2,1)} %bitcast.5), calls=%async_computation.1 | async-start | bytes 1572864 | tf_op jit(solution)/shard_map/all_to_all | solution.py:276
  50.0 1.7 collective-permute-start.1
  51.7 1.3 collective-permute-done.2
  53.6 3.6 %collective-permute-start.5 = (f32[8,128]{1,0:T(8,128)S(1)}, f32[8,128]{1,0:T(8,128)S(1)}, u32[]{:S(2)}, u32[]{:S(2)}) collective-permute-start(f32[8,128]{1,0:T(8,128)S(1)} %add_add_fusion.6), channel_id=1, source_target_pairs={{0,48},{4,52},{8,56},{12,60},{16,32},{20,36},{24,40},{28,44},{32,1... | collective-permute-start | bytes 12296 | tf_op jit(solution)/shard_map/ppermute | solution.py:285
  58.7 11.8 %collective-permute-done.5 = f32[8,128]{1,0:T(8,128)S(1)} collective-permute-done((f32[8,128]{1,0:T(8,128)S(1)}, f32[8,128]{1,0:T(8,128)S(1)}, u32[]{:S(2)}, u32[]{:S(2)}) %collective-permute-start.5) | collective-permute-done | bytes 4128 | tf_op jit(solution)/shard_map/ppermute | solution.py:285
  70.5 2.6 %all-to-all-done.1 = bf16[64,8,768]{2,1,0:T(8,128)(2,1)S(1)} async-done(((bf16[64,8,768]{2,1,0:T(8,128)(2,1)}), bf16[64,8,768]{2,1,0:T(8,128)(2,1)S(1)}, u32[]{:S(2)}, u32[]{:S(2)}) %all-to-all-start.1) | async-done | bytes 786464 | tf_op jit(solution)/shard_map/all_to_all | solution.py:276
  73.1 2.0 %shard_map.115 = (bf16[512,768]{1,0:T(8,128)(2,1)}, f32[1,128]{1,0:T(1,128)S(1)}) custom-call(bf16[512,768]{1,0:T(8,128)(2,1)S(1)} %bitcast.26, s32[3,128,128]{2,1,0:T(8,128)S(1)} %copy-done.1, bf16[512,512]{1,0:T(8,128)(2,1)S(1)} %copy-done.4, bf16[512,512]{1,0:T(8,128)(2,1)S(1)} %copy-done.3), custom_call_target="tpu_custom_call" | custom-call | flops 805306368 | bytes 2818560 | tf_op jit(solution)/shard_map/pallas_call | solution.py:264
  75.0 6.1 %all-to-all-start.2 = ((bf16[64,8,768]{2,1,0:T(8,128)(2,1)}), bf16[64,8,768]{2,1,0:T(8,128)(2,1)S(1)}, u32[]{:S(2)}, u32[]{:S(2)}) async-start(bf16[64,8,768]{2,1,0:T(8,128)(2,1)} %bitcast.7), calls=%async_computation.2 | async-start | bytes 1572864 | tf_op jit(solution)/shard_map/all_to_all | solution.py:276
  81.1 3.9 %collective-permute-start.8 = (f32[8,128]{1,0:T(8,128)S(1)}, f32[8,128]{1,0:T(8,128)S(1)}, u32[]{:S(2)}, u32[]{:S(2)}) collective-permute-start(f32[8,128]{1,0:T(8,128)S(1)} %add_add_fusion.5), channel_id=1, source_target_pairs={{0,192},{4,196},{8,200},{12,204},{16,208},{20,212},{24,216},{28,22... | collective-permute-start | bytes 12296 | tf_op jit(solution)/shard_map/ppermute | solution.py:285
  85.0 2.1 %collective-permute-start.7 = (f32[8,128]{1,0:T(8,128)S(1)}, f32[8,128]{1,0:T(8,128)S(1)}, u32[]{:S(2)}, u32[]{:S(2)}) collective-permute-start(f32[8,128]{1,0:T(8,128)S(1)} %add_add_fusion.5), channel_id=1, source_target_pairs={{0,128},{4,132},{8,136},{12,140},{16,144},{20,148},{24,152},{28,15... | collective-permute-start | bytes 12296 | tf_op jit(solution)/shard_map/ppermute | solution.py:285
  87.7 14.7 %collective-permute-done.8 = f32[8,128]{1,0:T(8,128)S(1)} collective-permute-done((f32[8,128]{1,0:T(8,128)S(1)}, f32[8,128]{1,0:T(8,128)S(1)}, u32[]{:S(2)}, u32[]{:S(2)}) %collective-permute-start.8) | collective-permute-done | bytes 4128 | tf_op jit(solution)/shard_map/ppermute | solution.py:285
  102.5 2.2 %collective-permute-done.7 = f32[8,128]{1,0:T(8,128)S(1)} collective-permute-done((f32[8,128]{1,0:T(8,128)S(1)}, f32[8,128]{1,0:T(8,128)S(1)}, u32[]{:S(2)}, u32[]{:S(2)}) %collective-permute-start.7) | collective-permute-done | bytes 4128 | tf_op jit(solution)/shard_map/ppermute | solution.py:285
  104.7 1.0 copy-done.6
  105.7 1.0 copy-done.10
  106.7 1.8 %shard_map.116 = (f32[3,256,128]{2,1,0:T(8,128)S(1)}, f32[8,128]{1,0:T(8,128)S(1)}, bf16[512,768]{1,0:T(8,128)(2,1)S(1)}) custom-call(bf16[512,768]{1,0:T(8,128)(2,1)S(1)} %bitcast.27, f32[4,256,128]{2,1,0:T(8,128)S(1)} %bitcast.32, bf16[512,512]{1,0:T(8,128)(2,1)S(1)} %copy-done.2, bf16[256,256]{1,0:T(8,128)(2,1)S(1)} %copy-done.7, ...), custom_call_target="tpu_custom_call" | custom-call | flops 1207959552 | bytes 4202496 | tf_op jit(solution)/shard_map/pallas_call | solution.py:264
  108.6 28.6 %all_to_all.57 = bf16[64,8,768]{2,1,0:T(8,128)(2,1)S(1)} all-to-all(bf16[64,8,768]{2,1,0:T(8,128)(2,1)S(1)} %bitcast.30), channel_id=1, replica_groups=mesh['slab'=64,'comp'=4] {'slab'}, dimensions={0} | all-to-all | bytes 1572864 | tf_op jit(solution)/shard_map/all_to_all | solution.py:276
  137.2 2.0 %shard_map.117 = (bf16[512,768]{1,0:T(8,128)(2,1)}, f32[8,128]{1,0:T(8,128)S(1)}) custom-call(bf16[512,768]{1,0:T(8,128)(2,1)S(1)} %bitcast.28, s32[3,128,128]{2,1,0:T(8,128)S(1)} %copy-done.1, bf16[512,512]{1,0:T(8,128)(2,1)S(1)} %copy-done.4, bf16[512,512]{1,0:T(8,128)(2,1)S(1)} %copy-done.3, f32[8,128]{1,0:T(8,128)S(1)} %add_add_fusion.4.group, ...), custom_call_target="tpu_custom_call" | custom-call | flops 805306368 | bytes 2834944 | tf_op jit(solution)/shard_map/pallas_call | solution.py:264
  139.2 5.9 %all-to-all-start.4 = ((bf16[64,8,768]{2,1,0:T(8,128)(2,1)}), bf16[64,8,768]{2,1,0:T(8,128)(2,1)S(1)}, u32[]{:S(2)}, u32[]{:S(2)}) async-start(bf16[64,8,768]{2,1,0:T(8,128)(2,1)} %bitcast.11), calls=%async_computation.4 | async-start | bytes 1572864 | tf_op jit(solution)/shard_map/all_to_all | solution.py:276
  145.1 3.1 %collective-permute-start.11 = (f32[8,128]{1,0:T(8,128)S(1)}, f32[8,128]{1,0:T(8,128)S(1)}, u32[]{:S(2)}, u32[]{:S(2)}) collective-permute-start(f32[8,128]{1,0:T(8,128)S(1)} %get-tuple-element.35), channel_id=1, source_target_pairs={{0,3},{1,2},{2,1},{3,0},{4,7},{5,6},{6,5},{7,4},{8,11},{9,10},{10,... | collective-permute-start | bytes 12296 | tf_op jit(solution)/shard_map/ppermute | solution.py:285
  150.0 3.3 %collective-permute-done.10 = f32[8,128]{1,0:T(8,128)S(1)} collective-permute-done((f32[8,128]{1,0:T(8,128)S(1)}, f32[8,128]{1,0:T(8,128)S(1)}, u32[]{:S(2)}, u32[]{:S(2)}) %collective-permute-start.10) | collective-permute-done | bytes 4128 | tf_op jit(solution)/shard_map/ppermute | solution.py:285
  154.1 1.2 collective-permute-start.12
  155.3 1.2 collective-permute-done.14
  157.2 3.1 %collective-permute-start.17 = (f32[8,128]{1,0:T(8,128)S(1)}, f32[8,128]{1,0:T(8,128)S(1)}, u32[]{:S(2)}, u32[]{:S(2)}) collective-permute-start(f32[8,128]{1,0:T(8,128)S(1)} %add_add_fusion.2), channel_id=1, source_target_pairs={{0,48},{4,52},{8,56},{12,60},{16,32},{20,36},{24,40},{28,44},{32,1... | collective-permute-start | bytes 12296 | tf_op jit(solution)/shard_map/ppermute | solution.py:285
  161.1 1.1 collective-permute-start.15
  162.2 3.5 %collective-permute-done.17 = f32[8,128]{1,0:T(8,128)S(1)} collective-permute-done((f32[8,128]{1,0:T(8,128)S(1)}, f32[8,128]{1,0:T(8,128)S(1)}, u32[]{:S(2)}, u32[]{:S(2)}) %collective-permute-start.17) | collective-permute-done | bytes 4128 | tf_op jit(solution)/shard_map/ppermute | solution.py:285
  166.2 3.5 %collective-permute-start.20 = (f32[8,128]{1,0:T(8,128)S(1)}, f32[8,128]{1,0:T(8,128)S(1)}, u32[]{:S(2)}, u32[]{:S(2)}) collective-permute-start(f32[8,128]{1,0:T(8,128)S(1)} %add_add_fusion.1), channel_id=1, source_target_pairs={{0,192},{4,196},{8,200},{12,204},{16,208},{20,212},{24,216},{28,22... | collective-permute-start | bytes 12296 | tf_op jit(solution)/shard_map/ppermute | solution.py:285
  169.8 2.1 %collective-permute-start.19 = (f32[8,128]{1,0:T(8,128)S(1)}, f32[8,128]{1,0:T(8,128)S(1)}, u32[]{:S(2)}, u32[]{:S(2)}) collective-permute-start(f32[8,128]{1,0:T(8,128)S(1)} %add_add_fusion.1), channel_id=1, source_target_pairs={{0,128},{4,132},{8,136},{12,140},{16,144},{20,148},{24,152},{28,15... | collective-permute-start | bytes 12296 | tf_op jit(solution)/shard_map/ppermute | solution.py:285
  172.7 4.5 %collective-permute-done.19 = f32[8,128]{1,0:T(8,128)S(1)} collective-permute-done((f32[8,128]{1,0:T(8,128)S(1)}, f32[8,128]{1,0:T(8,128)S(1)}, u32[]{:S(2)}, u32[]{:S(2)}) %collective-permute-start.19) | collective-permute-done | bytes 4128 | tf_op jit(solution)/shard_map/ppermute | solution.py:285
  177.3 2.0 %shard_map.118 = (f32[3,256,128]{2,1,0:T(8,128)}, f32[3,256,128]{2,1,0:T(8,128)}) custom-call(bf16[512,768]{1,0:T(8,128)(2,1)S(1)} %bitcast.25, f32[4,256,128]{2,1,0:T(8,128)S(1)} %bitcast.33, bf16[512,512]{1,0:T(8,128)(2,1)S(1)} %copy-done.2, bf16[256,256]{1,0:T(8,128)(2,1)S(1)} %copy-done.7, f32[3,256,128]{2,1,0:T(8,128)S(1)} %copy-done.11, ...), custom_call_target="tpu_custom_call" | custom-call | flops 805306368 | bytes 3547136 | tf_op jit(solution)/shard_map/pallas_call | solution.py:264
  (61 shorter events, 9.8 us)
Async XLA Ops:
  0.6 39.1 %copy-start.7 = (bf16[256,256]{1,0:T(8,128)(2,1)S(1)}, bf16[256,256]{1,0:T(8,128)(2,1)}, u32[]{:S(2)}) copy-start(bf16[256,256]{1,0:T(8,128)(2,1)} %constant.15.clone.zi) | copy-start | bytes 393220
  0.6 39.1 %copy-start.8 = (bf16[256,256]{1,0:T(8,128)(2,1)S(1)}, bf16[256,256]{1,0:T(8,128)(2,1)}, u32[]{:S(2)}) copy-start(bf16[256,256]{1,0:T(8,128)(2,1)} %constant.14.clone.zf) | copy-start | bytes 393220
  4.3 35.4 %copy-start = (f32[4,2,16384]{2,1,0:T(2,128)S(1)}, f32[4,2,16384]{2,1,0:T(2,128)}, u32[]{:S(2)}) copy-start(f32[4,2,16384]{2,1,0:T(2,128)} %param.11) | copy-start | bytes 1572868
  4.3 35.4 %copy-start.2 = (bf16[512,512]{1,0:T(8,128)(2,1)S(1)}, bf16[512,512]{1,0:T(8,128)(2,1)}, u32[]{:S(2)}) copy-start(bf16[512,512]{1,0:T(8,128)(2,1)} %constant.17.clone.yi) | copy-start | bytes 1572868
  4.3 35.4 %copy-start.5 = (bf16[512,512]{1,0:T(8,128)(2,1)S(1)}, bf16[512,512]{1,0:T(8,128)(2,1)}, u32[]{:S(2)}) copy-start(bf16[512,512]{1,0:T(8,128)(2,1)} %constant.16.clone.yf) | copy-start | bytes 1572868
  43.8 29.2 %copy-start.4 = (bf16[512,512]{1,0:T(8,128)(2,1)S(1)}, bf16[512,512]{1,0:T(8,128)(2,1)}, u32[]{:S(2)}) copy-start(bf16[512,512]{1,0:T(8,128)(2,1)} %constant.18.clone.xf) | copy-start | bytes 1572868
  43.8 29.2 %all-to-all-start.1 = ((bf16[64,8,768]{2,1,0:T(8,128)(2,1)}), bf16[64,8,768]{2,1,0:T(8,128)(2,1)S(1)}, u32[]{:S(2)}, u32[]{:S(2)}) async-start(bf16[64,8,768]{2,1,0:T(8,128)(2,1)} %bitcast.5), calls=%async_computation.1 | async-start | bytes 1572864 | tf_op jit(solution)/shard_map/all_to_all | solution.py:276
  49.8 3.2 %collective-permute-start.2 = (f32[8,128]{1,0:T(8,128)S(1)}, f32[8,128]{1,0:T(8,128)S(1)}, u32[]{:S(2)}, u32[]{:S(2)}) collective-permute-start(f32[8,128]{1,0:T(8,128)S(1)} %get-tuple-element.23.here), channel_id=1, source_target_pairs={{0,12},{4,8},{8,4},{12,0},{16,28},{20,24},{24,20},{28,16},{32,44},... | collective-permute-start | bytes 12296 | tf_op jit(solution)/shard_map/ppermute | solution.py:285
  50.0 3.6 %collective-permute-start.1 = (f32[8,128]{1,0:T(8,128)S(1)}, f32[8,128]{1,0:T(8,128)S(1)}, u32[]{:S(2)}, u32[]{:S(2)}) collective-permute-start(f32[8,128]{1,0:T(8,128)S(1)} %get-tuple-element.23.here), channel_id=1, source_target_pairs={{0,8},{4,12},{8,0},{12,4},{16,24},{20,28},{24,16},{28,20},{32,40},... | collective-permute-start | bytes 12296 | tf_op jit(solution)/shard_map/ppermute | solution.py:285
  51.7 1.9 %collective-permute-start = (f32[8,128]{1,0:T(8,128)S(1)}, f32[8,128]{1,0:T(8,128)S(1)}, u32[]{:S(2)}, u32[]{:S(2)}) collective-permute-start(f32[8,128]{1,0:T(8,128)S(1)} %get-tuple-element.23.here), channel_id=1, source_target_pairs={{0,4},{4,0},{8,12},{12,8},{16,20},{20,16},{24,28},{28,24},{32,36},... | collective-permute-start | bytes 12296 | tf_op jit(solution)/shard_map/ppermute | solution.py:285
  53.6 16.8 %collective-permute-start.5 = (f32[8,128]{1,0:T(8,128)S(1)}, f32[8,128]{1,0:T(8,128)S(1)}, u32[]{:S(2)}, u32[]{:S(2)}) collective-permute-start(f32[8,128]{1,0:T(8,128)S(1)} %add_add_fusion.6), channel_id=1, source_target_pairs={{0,48},{4,52},{8,56},{12,60},{16,32},{20,36},{24,40},{28,44},{32,1... | collective-permute-start | bytes 12296 | tf_op jit(solution)/shard_map/ppermute | solution.py:285
  57.2 13.3 %collective-permute-start.4 = (f32[8,128]{1,0:T(8,128)S(1)}, f32[8,128]{1,0:T(8,128)S(1)}, u32[]{:S(2)}, u32[]{:S(2)}) collective-permute-start(f32[8,128]{1,0:T(8,128)S(1)} %add_add_fusion.6), channel_id=1, source_target_pairs={{0,32},{4,36},{8,40},{12,44},{16,48},{20,52},{24,56},{28,60},{32,0... | collective-permute-start | bytes 12296 | tf_op jit(solution)/shard_map/ppermute | solution.py:285
  57.7 12.7 %collective-permute-start.3 = (f32[8,128]{1,0:T(8,128)S(1)}, f32[8,128]{1,0:T(8,128)S(1)}, u32[]{:S(2)}, u32[]{:S(2)}) collective-permute-start(f32[8,128]{1,0:T(8,128)S(1)} %add_add_fusion.6), channel_id=1, source_target_pairs={{0,16},{4,20},{8,24},{12,28},{16,0},{20,4},{24,8},{28,12},{32,48},... | collective-permute-start | bytes 12296 | tf_op jit(solution)/shard_map/ppermute | solution.py:285
  75.0 29.6 %all-to-all-start.2 = ((bf16[64,8,768]{2,1,0:T(8,128)(2,1)}), bf16[64,8,768]{2,1,0:T(8,128)(2,1)S(1)}, u32[]{:S(2)}, u32[]{:S(2)}) async-start(bf16[64,8,768]{2,1,0:T(8,128)(2,1)} %bitcast.7), calls=%async_computation.2 | async-start | bytes 1572864 | tf_op jit(solution)/shard_map/all_to_all | solution.py:276
  81.1 21.3 %collective-permute-start.8 = (f32[8,128]{1,0:T(8,128)S(1)}, f32[8,128]{1,0:T(8,128)S(1)}, u32[]{:S(2)}, u32[]{:S(2)}) collective-permute-start(f32[8,128]{1,0:T(8,128)S(1)} %add_add_fusion.5), channel_id=1, source_target_pairs={{0,192},{4,196},{8,200},{12,204},{16,208},{20,212},{24,216},{28,22... | collective-permute-start | bytes 12296 | tf_op jit(solution)/shard_map/ppermute | solution.py:285
  85.0 19.6 %collective-permute-start.7 = (f32[8,128]{1,0:T(8,128)S(1)}, f32[8,128]{1,0:T(8,128)S(1)}, u32[]{:S(2)}, u32[]{:S(2)}) collective-permute-start(f32[8,128]{1,0:T(8,128)S(1)} %add_add_fusion.5), channel_id=1, source_target_pairs={{0,128},{4,132},{8,136},{12,140},{16,144},{20,148},{24,152},{28,15... | collective-permute-start | bytes 12296 | tf_op jit(solution)/shard_map/ppermute | solution.py:285
  87.2 17.5 %collective-permute-start.6 = (f32[8,128]{1,0:T(8,128)S(1)}, f32[8,128]{1,0:T(8,128)S(1)}, u32[]{:S(2)}, u32[]{:S(2)}) collective-permute-start(f32[8,128]{1,0:T(8,128)S(1)} %add_add_fusion.5), channel_id=1, source_target_pairs={{0,64},{4,68},{8,72},{12,76},{16,80},{20,84},{24,88},{28,92},{32,9... | collective-permute-start | bytes 12296 | tf_op jit(solution)/shard_map/ppermute | solution.py:285
  139.2 38.1 %copy-start.11 = (f32[3,256,128]{2,1,0:T(8,128)S(1)}, f32[3,256,128]{2,1,0:T(8,128)}, u32[]{:S(2)}) copy-start(f32[3,256,128]{2,1,0:T(8,128)} %copy-done.9) | copy-start | bytes 1179652
  139.2 38.1 %copy-start.13 = (f32[3,256,128]{2,1,0:T(8,128)S(1)}, f32[3,256,128]{2,1,0:T(8,128)}, u32[]{:S(2)}) copy-start(f32[3,256,128]{2,1,0:T(8,128)} %copy-done.12) | copy-start | bytes 1179652
  139.2 38.1 %all-to-all-start.4 = ((bf16[64,8,768]{2,1,0:T(8,128)(2,1)}), bf16[64,8,768]{2,1,0:T(8,128)(2,1)S(1)}, u32[]{:S(2)}, u32[]{:S(2)}) async-start(bf16[64,8,768]{2,1,0:T(8,128)(2,1)} %bitcast.11), calls=%async_computation.4 | async-start | bytes 1572864 | tf_op jit(solution)/shard_map/all_to_all | solution.py:276
  145.1 4.9 %collective-permute-start.11 = (f32[8,128]{1,0:T(8,128)S(1)}, f32[8,128]{1,0:T(8,128)S(1)}, u32[]{:S(2)}, u32[]{:S(2)}) collective-permute-start(f32[8,128]{1,0:T(8,128)S(1)} %get-tuple-element.35), channel_id=1, source_target_pairs={{0,3},{1,2},{2,1},{3,0},{4,7},{5,6},{6,5},{7,4},{8,11},{9,10},{10,... | collective-permute-start | bytes 12296 | tf_op jit(solution)/shard_map/ppermute | solution.py:285
  148.2 5.1 %collective-permute-start.10 = (f32[8,128]{1,0:T(8,128)S(1)}, f32[8,128]{1,0:T(8,128)S(1)}, u32[]{:S(2)}, u32[]{:S(2)}) collective-permute-start(f32[8,128]{1,0:T(8,128)S(1)} %get-tuple-element.35), channel_id=1, source_target_pairs={{0,2},{1,3},{2,0},{3,1},{4,6},{5,7},{6,4},{7,5},{8,10},{9,11},{10,... | collective-permute-start | bytes 12296 | tf_op jit(solution)/shard_map/ppermute | solution.py:285
  148.9 4.5 %collective-permute-start.9 = (f32[8,128]{1,0:T(8,128)S(1)}, f32[8,128]{1,0:T(8,128)S(1)}, u32[]{:S(2)}, u32[]{:S(2)}) collective-permute-start(f32[8,128]{1,0:T(8,128)S(1)} %get-tuple-element.35), channel_id=1, source_target_pairs={{0,1},{1,0},{2,3},{3,2},{4,5},{5,4},{6,7},{7,6},{8,9},{9,8},{10,11... | collective-permute-start | bytes 12296 | tf_op jit(solution)/shard_map/ppermute | solution.py:285
  153.3 3.2 %collective-permute-start.14 = (f32[8,128]{1,0:T(8,128)S(1)}, f32[8,128]{1,0:T(8,128)S(1)}, u32[]{:S(2)}, u32[]{:S(2)}) collective-permute-start(f32[8,128]{1,0:T(8,128)S(1)} %add_add_fusion.3), channel_id=1, source_target_pairs={{0,12},{4,8},{8,4},{12,0},{16,28},{20,24},{24,20},{28,16},{32,44},... | collective-permute-start | bytes 12296 | tf_op jit(solution)/shard_map/ppermute | solution.py:285
  153.4 3.7 %collective-permute-start.13 = (f32[8,128]{1,0:T(8,128)S(1)}, f32[8,128]{1,0:T(8,128)S(1)}, u32[]{:S(2)}, u32[]{:S(2)}) collective-permute-start(f32[8,128]{1,0:T(8,128)S(1)} %add_add_fusion.3), channel_id=1, source_target_pairs={{0,8},{4,12},{8,0},{12,4},{16,24},{20,28},{24,16},{28,20},{32,40},... | collective-permute-start | bytes 12296 | tf_op jit(solution)/shard_map/ppermute | solution.py:285
  154.1 3.1 %collective-permute-start.12 = (f32[8,128]{1,0:T(8,128)S(1)}, f32[8,128]{1,0:T(8,128)S(1)}, u32[]{:S(2)}, u32[]{:S(2)}) collective-permute-start(f32[8,128]{1,0:T(8,128)S(1)} %add_add_fusion.3), channel_id=1, source_target_pairs={{0,4},{4,0},{8,12},{12,8},{16,20},{20,16},{24,28},{28,24},{32,36},... | collective-permute-start | bytes 12296 | tf_op jit(solution)/shard_map/ppermute | solution.py:285
  157.2 8.6 %collective-permute-start.17 = (f32[8,128]{1,0:T(8,128)S(1)}, f32[8,128]{1,0:T(8,128)S(1)}, u32[]{:S(2)}, u32[]{:S(2)}) collective-permute-start(f32[8,128]{1,0:T(8,128)S(1)} %add_add_fusion.2), channel_id=1, source_target_pairs={{0,48},{4,52},{8,56},{12,60},{16,32},{20,36},{24,40},{28,44},{32,1... | collective-permute-start | bytes 12296 | tf_op jit(solution)/shard_map/ppermute | solution.py:285
  160.2 5.6 %collective-permute-start.16 = (f32[8,128]{1,0:T(8,128)S(1)}, f32[8,128]{1,0:T(8,128)S(1)}, u32[]{:S(2)}, u32[]{:S(2)}) collective-permute-start(f32[8,128]{1,0:T(8,128)S(1)} %add_add_fusion.2), channel_id=1, source_target_pairs={{0,32},{4,36},{8,40},{12,44},{16,48},{20,52},{24,56},{28,60},{32,0... | collective-permute-start | bytes 12296 | tf_op jit(solution)/shard_map/ppermute | solution.py:285
  161.1 5.1 %collective-permute-start.15 = (f32[8,128]{1,0:T(8,128)S(1)}, f32[8,128]{1,0:T(8,128)S(1)}, u32[]{:S(2)}, u32[]{:S(2)}) collective-permute-start(f32[8,128]{1,0:T(8,128)S(1)} %add_add_fusion.2), channel_id=1, source_target_pairs={{0,16},{4,20},{8,24},{12,28},{16,0},{20,4},{24,8},{28,12},{32,48},... | collective-permute-start | bytes 12296 | tf_op jit(solution)/shard_map/ppermute | solution.py:285
  166.2 6.5 %collective-permute-start.20 = (f32[8,128]{1,0:T(8,128)S(1)}, f32[8,128]{1,0:T(8,128)S(1)}, u32[]{:S(2)}, u32[]{:S(2)}) collective-permute-start(f32[8,128]{1,0:T(8,128)S(1)} %add_add_fusion.1), channel_id=1, source_target_pairs={{0,192},{4,196},{8,200},{12,204},{16,208},{20,212},{24,216},{28,22... | collective-permute-start | bytes 12296 | tf_op jit(solution)/shard_map/ppermute | solution.py:285
  169.8 7.5 %collective-permute-start.19 = (f32[8,128]{1,0:T(8,128)S(1)}, f32[8,128]{1,0:T(8,128)S(1)}, u32[]{:S(2)}, u32[]{:S(2)}) collective-permute-start(f32[8,128]{1,0:T(8,128)S(1)} %add_add_fusion.1), channel_id=1, source_target_pairs={{0,128},{4,132},{8,136},{12,140},{16,144},{20,148},{24,152},{28,15... | collective-permute-start | bytes 12296 | tf_op jit(solution)/shard_map/ppermute | solution.py:285
  171.9 5.4 %collective-permute-start.18 = (f32[8,128]{1,0:T(8,128)S(1)}, f32[8,128]{1,0:T(8,128)S(1)}, u32[]{:S(2)}, u32[]{:S(2)}) collective-permute-start(f32[8,128]{1,0:T(8,128)S(1)} %add_add_fusion.1), channel_id=1, source_target_pairs={{0,64},{4,68},{8,72},{12,76},{16,80},{20,84},{24,88},{28,92},{32,9... | collective-permute-start | bytes 12296 | tf_op jit(solution)/shard_map/ppermute | solution.py:285
  (7 other events, 90.6 us)

commit v8 on v7

--- a/solution.py
+++ b/solution.py
@@ -156,13 +156,14 @@
     return product(yf, jnp.concatenate(columns, 1)).astype(jnp.bfloat16)
 
 
-def fold_rows(values):
-    rows = values.sum(0, keepdims=True)
-    return sum(rows[:, at : at + LANES] for at in range(0, rows.shape[1], LANES))
-
-
 def row_of(one, other):
-    return fold_rows(one.astype(jnp.float32) * other.astype(jnp.float32))
+    total = None
+    for at in range(0, one.shape[1], LANES):
+        for row in range(0, one.shape[0], 64):
+            block = (slice(row, row + 64), slice(at, at + LANES))
+            term = one[block].astype(jnp.float32) * other[block].astype(jnp.float32)
+            total = term if total is None else total + term
+    return total.sum(0, keepdims=True)
 
 
 def group_step(sums):

time: 180 us -> 180 us (level)
  no operation moved by 1% of the time
where the time goes in v8:
time: 180 us; the launch traced here: 179 us
  blocking collectives  64 us (36%)
  starting transfers between devices  49.3 us (27%)
  waiting for transfers between devices  47.5 us (26%)
  Pallas kernels  14.1 us (8%)
  local copies, waits for them, and re-layouts  3.46 us (2%)
    all_to_all x2, blocking collectives, exchange(): lax.all_to_all(values, 'slab', split_axis=0, concat_axis=0, tiled=True)  64 us
    ppermute x21, waiting for transfers between devices, sum_over(): lax.ppermute(values, axis, exclusive(axis, flips * low))  45 us
    ppermute x21, starting transfers between devices, sum_over(): lax.ppermute(values, axis, exclusive(axis, flips * low))  31.3 us
    all_to_all x3, starting transfers between devices, exchange(): lax.all_to_all(values, 'slab', split_axis=0, concat_axis=0, tiled=True)  18 us
    pallas_call x6, Pallas kernels, call(): pl.pallas_call(body, out_shape=shapes, in_specs=[pl.BlockSpec(memory_spac...  14.1 us
  transfers between devices with their start and end apart: 24, of which 13 were waited for; matrix products, arithmetic and copies ran while one was open for 0% of the time, Pallas kernels for 0%

profile of v8, /device:TPU:2, one launch (start us, length us, event | category | flops | bytes accessed | tf_op | source)
XLA Modules:
  0.0 179.3 jit_solution(13533473577447844816)
XLA Ops:
  0.7 3.6 %shard_map.113 = (bf16[512,768]{1,0:T(8,128)(2,1)}, f32[1,128]{1,0:T(1,128)}) custom-call(bf16[3,4,128,256]{3,2,1,0:T(8,128)(2,1)} %kspace_at.1, s32[3,128,128]{2,1,0:T(8,128)} %sampling.3, bf16[256,256]{1,0:T(8,128)(2,1)} %constant.20.clone.order_at, bf16[512,512]{1,0:T(8,128)(2,1)} %constant.19.clone.xi_at.xi), custom_call_target="tpu_custom_call" | custom-call | flops 805306368 | bytes 2425344 | tf_op jit(solution)/shard_map/pallas_call | solution.py:265
  4.3 35.3 %all_to_all.56 = bf16[64,8,768]{2,1,0:T(8,128)(2,1)S(1)} all-to-all(bf16[64,8,768]{2,1,0:T(8,128)(2,1)} %bitcast.34), channel_id=1, replica_groups=mesh['slab'=64,'comp'=4] {'slab'}, dimensions={0} | all-to-all | bytes 1572864 | tf_op jit(solution)/shard_map/all_to_all | solution.py:277
  40.3 2.7 %shard_map.114 = (f32[3,256,128]{2,1,0:T(8,128)S(1)}, f32[8,128]{1,0:T(8,128)S(1)}, bf16[512,768]{1,0:T(8,128)(2,1)}) custom-call(bf16[512,768]{1,0:T(8,128)(2,1)S(1)} %bitcast.29, f32[4,256,128]{2,1,0:T(8,128)S(1)} %bitcast.31, bf16[512,512]{1,0:T(8,128)(2,1)S(1)} %copy-done.2, bf16[256,256]{1,0:T(8,128)(2,1)S(1)} %copy-done.7, ...), custom_call_target="tpu_custom_call" | custom-call | flops 1207959552 | bytes 3805696 | tf_op jit(solution)/shard_map/pallas_call | solution.py:265
  43.8 5.9 %all-to-all-start.1 = ((bf16[64,8,768]{2,1,0:T(8,128)(2,1)}), bf16[64,8,768]{2,1,0:T(8,128)(2,1)S(1)}, u32[]{:S(2)}, u32[]{:S(2)}) async-start(bf16[64,8,768]{2,1,0:T(8,128)(2,1)} %bitcast.5), calls=%async_computation.1 | async-start | bytes 1572864 | tf_op jit(solution)/shard_map/all_to_all | solution.py:277
  50.0 1.7 collective-permute-start.1
  51.7 1.3 collective-permute-done.2
  53.6 3.6 %collective-permute-start.5 = (f32[8,128]{1,0:T(8,128)S(1)}, f32[8,128]{1,0:T(8,128)S(1)}, u32[]{:S(2)}, u32[]{:S(2)}) collective-permute-start(f32[8,128]{1,0:T(8,128)S(1)} %add_add_fusion.6), channel_id=1, source_target_pairs={{0,48},{4,52},{8,56},{12,60},{16,32},{20,36},{24,40},{28,44},{32,1... | collective-permute-start | bytes 12296 | tf_op jit(solution)/shard_map/ppermute | solution.py:286
  58.7 11.8 %collective-permute-done.5 = f32[8,128]{1,0:T(8,128)S(1)} collective-permute-done((f32[8,128]{1,0:T(8,128)S(1)}, f32[8,128]{1,0:T(8,128)S(1)}, u32[]{:S(2)}, u32[]{:S(2)}) %collective-permute-start.5) | collective-permute-done | bytes 4128 | tf_op jit(solution)/shard_map/ppermute | solution.py:286
  70.4 2.6 %all-to-all-done.1 = bf16[64,8,768]{2,1,0:T(8,128)(2,1)S(1)} async-done(((bf16[64,8,768]{2,1,0:T(8,128)(2,1)}), bf16[64,8,768]{2,1,0:T(8,128)(2,1)S(1)}, u32[]{:S(2)}, u32[]{:S(2)}) %all-to-all-start.1) | async-done | bytes 786464 | tf_op jit(solution)/shard_map/all_to_all | solution.py:277
  73.0 2.0 %shard_map.115 = (bf16[512,768]{1,0:T(8,128)(2,1)}, f32[1,128]{1,0:T(1,128)S(1)}) custom-call(bf16[512,768]{1,0:T(8,128)(2,1)S(1)} %bitcast.26, s32[3,128,128]{2,1,0:T(8,128)S(1)} %copy-done.1, bf16[512,512]{1,0:T(8,128)(2,1)S(1)} %copy-done.4, bf16[512,512]{1,0:T(8,128)(2,1)S(1)} %copy-done.3), custom_call_target="tpu_custom_call" | custom-call | flops 805306368 | bytes 2818560 | tf_op jit(solution)/shard_map/pallas_call | solution.py:265
  75.0 6.1 %all-to-all-start.2 = ((bf16[64,8,768]{2,1,0:T(8,128)(2,1)}), bf16[64,8,768]{2,1,0:T(8,128)(2,1)S(1)}, u32[]{:S(2)}, u32[]{:S(2)}) async-start(bf16[64,8,768]{2,1,0:T(8,128)(2,1)} %bitcast.7), calls=%async_computation.2 | async-start | bytes 1572864 | tf_op jit(solution)/shard_map/all_to_all | solution.py:277
  81.1 3.9 %collective-permute-start.8 = (f32[8,128]{1,0:T(8,128)S(1)}, f32[8,128]{1,0:T(8,128)S(1)}, u32[]{:S(2)}, u32[]{:S(2)}) collective-permute-start(f32[8,128]{1,0:T(8,128)S(1)} %add_add_fusion.5), channel_id=1, source_target_pairs={{0,192},{4,196},{8,200},{12,204},{16,208},{20,212},{24,216},{28,22... | collective-permute-start | bytes 12296 | tf_op jit(solution)/shard_map/ppermute | solution.py:286
  85.0 2.1 %collective-permute-start.7 = (f32[8,128]{1,0:T(8,128)S(1)}, f32[8,128]{1,0:T(8,128)S(1)}, u32[]{:S(2)}, u32[]{:S(2)}) collective-permute-start(f32[8,128]{1,0:T(8,128)S(1)} %add_add_fusion.5), channel_id=1, source_target_pairs={{0,128},{4,132},{8,136},{12,140},{16,144},{20,148},{24,152},{28,15... | collective-permute-start | bytes 12296 | tf_op jit(solution)/shard_map/ppermute | solution.py:286
  87.7 14.7 %collective-permute-done.8 = f32[8,128]{1,0:T(8,128)S(1)} collective-permute-done((f32[8,128]{1,0:T(8,128)S(1)}, f32[8,128]{1,0:T(8,128)S(1)}, u32[]{:S(2)}, u32[]{:S(2)}) %collective-permute-start.8) | collective-permute-done | bytes 4128 | tf_op jit(solution)/shard_map/ppermute | solution.py:286
  102.4 2.2 %collective-permute-done.7 = f32[8,128]{1,0:T(8,128)S(1)} collective-permute-done((f32[8,128]{1,0:T(8,128)S(1)}, f32[8,128]{1,0:T(8,128)S(1)}, u32[]{:S(2)}, u32[]{:S(2)}) %collective-permute-start.7) | collective-permute-done | bytes 4128 | tf_op jit(solution)/shard_map/ppermute | solution.py:286
  104.6 1.0 copy-done.6
  105.7 1.0 copy-done.10
  106.7 1.9 %shard_map.116 = (f32[3,256,128]{2,1,0:T(8,128)S(1)}, f32[8,128]{1,0:T(8,128)S(1)}, bf16[512,768]{1,0:T(8,128)(2,1)S(1)}) custom-call(bf16[512,768]{1,0:T(8,128)(2,1)S(1)} %bitcast.27, f32[4,256,128]{2,1,0:T(8,128)S(1)} %bitcast.32, bf16[512,512]{1,0:T(8,128)(2,1)S(1)} %copy-done.2, bf16[256,256]{1,0:T(8,128)(2,1)S(1)} %copy-done.7, ...), custom_call_target="tpu_custom_call" | custom-call | flops 1207959552 | bytes 4202496 | tf_op jit(solution)/shard_map/pallas_call | solution.py:265
  108.5 28.6 %all_to_all.57 = bf16[64,8,768]{2,1,0:T(8,128)(2,1)S(1)} all-to-all(bf16[64,8,768]{2,1,0:T(8,128)(2,1)S(1)} %bitcast.30), channel_id=1, replica_groups=mesh['slab'=64,'comp'=4] {'slab'}, dimensions={0} | all-to-all | bytes 1572864 | tf_op jit(solution)/shard_map/all_to_all | solution.py:277
  137.2 1.9 %shard_map.117 = (bf16[512,768]{1,0:T(8,128)(2,1)}, f32[8,128]{1,0:T(8,128)S(1)}) custom-call(bf16[512,768]{1,0:T(8,128)(2,1)S(1)} %bitcast.28, s32[3,128,128]{2,1,0:T(8,128)S(1)} %copy-done.1, bf16[512,512]{1,0:T(8,128)(2,1)S(1)} %copy-done.4, bf16[512,512]{1,0:T(8,128)(2,1)S(1)} %copy-done.3, f32[8,128]{1,0:T(8,128)S(1)} %add_add_fusion.4.group, ...), custom_call_target="tpu_custom_call" | custom-call | flops 805306368 | bytes 2834944 | tf_op jit(solution)/shard_map/pallas_call | solution.py:265
  139.1 5.9 %all-to-all-start.4 = ((bf16[64,8,768]{2,1,0:T(8,128)(2,1)}), bf16[64,8,768]{2,1,0:T(8,128)(2,1)S(1)}, u32[]{:S(2)}, u32[]{:S(2)}) async-start(bf16[64,8,768]{2,1,0:T(8,128)(2,1)} %bitcast.11), calls=%async_computation.4 | async-start | bytes 1572864 | tf_op jit(solution)/shard_map/all_to_all | solution.py:277
  145.1 3.1 %collective-permute-start.11 = (f32[8,128]{1,0:T(8,128)S(1)}, f32[8,128]{1,0:T(8,128)S(1)}, u32[]{:S(2)}, u32[]{:S(2)}) collective-permute-start(f32[8,128]{1,0:T(8,128)S(1)} %get-tuple-element.35), channel_id=1, source_target_pairs={{0,3},{1,2},{2,1},{3,0},{4,7},{5,6},{6,5},{7,4},{8,11},{9,10},{10,... | collective-permute-start | bytes 12296 | tf_op jit(solution)/shard_map/ppermute | solution.py:286
  150.0 3.3 %collective-permute-done.10 = f32[8,128]{1,0:T(8,128)S(1)} collective-permute-done((f32[8,128]{1,0:T(8,128)S(1)}, f32[8,128]{1,0:T(8,128)S(1)}, u32[]{:S(2)}, u32[]{:S(2)}) %collective-permute-start.10) | collective-permute-done | bytes 4128 | tf_op jit(solution)/shard_map/ppermute | solution.py:286
  154.0 1.2 collective-permute-start.12
  155.3 1.2 collective-permute-done.14
  157.1 3.1 %collective-permute-start.17 = (f32[8,128]{1,0:T(8,128)S(1)}, f32[8,128]{1,0:T(8,128)S(1)}, u32[]{:S(2)}, u32[]{:S(2)}) collective-permute-start(f32[8,128]{1,0:T(8,128)S(1)} %add_add_fusion.2), channel_id=1, source_target_pairs={{0,48},{4,52},{8,56},{12,60},{16,32},{20,36},{24,40},{28,44},{32,1... | collective-permute-start | bytes 12296 | tf_op jit(solution)/shard_map/ppermute | solution.py:286
  161.1 1.1 collective-permute-start.15
  162.2 3.5 %collective-permute-done.17 = f32[8,128]{1,0:T(8,128)S(1)} collective-permute-done((f32[8,128]{1,0:T(8,128)S(1)}, f32[8,128]{1,0:T(8,128)S(1)}, u32[]{:S(2)}, u32[]{:S(2)}) %collective-permute-start.17) | collective-permute-done | bytes 4128 | tf_op jit(solution)/shard_map/ppermute | solution.py:286
  166.2 3.5 %collective-permute-start.20 = (f32[8,128]{1,0:T(8,128)S(1)}, f32[8,128]{1,0:T(8,128)S(1)}, u32[]{:S(2)}, u32[]{:S(2)}) collective-permute-start(f32[8,128]{1,0:T(8,128)S(1)} %add_add_fusion.1), channel_id=1, source_target_pairs={{0,192},{4,196},{8,200},{12,204},{16,208},{20,212},{24,216},{28,22... | collective-permute-start | bytes 12296 | tf_op jit(solution)/shard_map/ppermute | solution.py:286
  169.7 2.1 %collective-permute-start.19 = (f32[8,128]{1,0:T(8,128)S(1)}, f32[8,128]{1,0:T(8,128)S(1)}, u32[]{:S(2)}, u32[]{:S(2)}) collective-permute-start(f32[8,128]{1,0:T(8,128)S(1)} %add_add_fusion.1), channel_id=1, source_target_pairs={{0,128},{4,132},{8,136},{12,140},{16,144},{20,148},{24,152},{28,15... | collective-permute-start | bytes 12296 | tf_op jit(solution)/shard_map/ppermute | solution.py:286
  172.7 4.5 %collective-permute-done.19 = f32[8,128]{1,0:T(8,128)S(1)} collective-permute-done((f32[8,128]{1,0:T(8,128)S(1)}, f32[8,128]{1,0:T(8,128)S(1)}, u32[]{:S(2)}, u32[]{:S(2)}) %collective-permute-start.19) | collective-permute-done | bytes 4128 | tf_op jit(solution)/shard_map/ppermute | solution.py:286
  177.3 2.0 %shard_map.118 = (f32[3,256,128]{2,1,0:T(8,128)}, f32[3,256,128]{2,1,0:T(8,128)}) custom-call(bf16[512,768]{1,0:T(8,128)(2,1)S(1)} %bitcast.25, f32[4,256,128]{2,1,0:T(8,128)S(1)} %bitcast.33, bf16[512,512]{1,0:T(8,128)(2,1)S(1)} %copy-done.2, bf16[256,256]{1,0:T(8,128)(2,1)S(1)} %copy-done.7, f32[3,256,128]{2,1,0:T(8,128)S(1)} %copy-done.11, ...), custom_call_target="tpu_custom_call" | custom-call | flops 805306368 | bytes 3547136 | tf_op jit(solution)/shard_map/pallas_call | solution.py:265
  (61 shorter events, 9.8 us)
Async XLA Ops:
  0.6 39.0 %copy-start.7 = (bf16[256,256]{1,0:T(8,128)(2,1)S(1)}, bf16[256,256]{1,0:T(8,128)(2,1)}, u32[]{:S(2)}) copy-start(bf16[256,256]{1,0:T(8,128)(2,1)} %constant.15.clone.zi) | copy-start | bytes 393220
  0.6 39.0 %copy-start.8 = (bf16[256,256]{1,0:T(8,128)(2,1)S(1)}, bf16[256,256]{1,0:T(8,128)(2,1)}, u32[]{:S(2)}) copy-start(bf16[256,256]{1,0:T(8,128)(2,1)} %constant.14.clone.zf) | copy-start | bytes 393220
  4.3 35.4 %copy-start = (f32[4,2,16384]{2,1,0:T(2,128)S(1)}, f32[4,2,16384]{2,1,0:T(2,128)}, u32[]{:S(2)}) copy-start(f32[4,2,16384]{2,1,0:T(2,128)} %param.11) | copy-start | bytes 1572868
  4.3 35.4 %copy-start.2 = (bf16[512,512]{1,0:T(8,128)(2,1)S(1)}, bf16[512,512]{1,0:T(8,128)(2,1)}, u32[]{:S(2)}) copy-start(bf16[512,512]{1,0:T(8,128)(2,1)} %constant.17.clone.yi) | copy-start | bytes 1572868
  4.3 35.4 %copy-start.5 = (bf16[512,512]{1,0:T(8,128)(2,1)S(1)}, bf16[512,512]{1,0:T(8,128)(2,1)}, u32[]{:S(2)}) copy-start(bf16[512,512]{1,0:T(8,128)(2,1)} %constant.16.clone.yf) | copy-start | bytes 1572868
  43.8 29.2 %copy-start.4 = (bf16[512,512]{1,0:T(8,128)(2,1)S(1)}, bf16[512,512]{1,0:T(8,128)(2,1)}, u32[]{:S(2)}) copy-start(bf16[512,512]{1,0:T(8,128)(2,1)} %constant.18.clone.xf) | copy-start | bytes 1572868
  43.8 29.2 %all-to-all-start.1 = ((bf16[64,8,768]{2,1,0:T(8,128)(2,1)}), bf16[64,8,768]{2,1,0:T(8,128)(2,1)S(1)}, u32[]{:S(2)}, u32[]{:S(2)}) async-start(bf16[64,8,768]{2,1,0:T(8,128)(2,1)} %bitcast.5), calls=%async_computation.1 | async-start | bytes 1572864 | tf_op jit(solution)/shard_map/all_to_all | solution.py:277
  49.8 3.2 %collective-permute-start.2 = (f32[8,128]{1,0:T(8,128)S(1)}, f32[8,128]{1,0:T(8,128)S(1)}, u32[]{:S(2)}, u32[]{:S(2)}) collective-permute-start(f32[8,128]{1,0:T(8,128)S(1)} %get-tuple-element.23.here), channel_id=1, source_target_pairs={{0,12},{4,8},{8,4},{12,0},{16,28},{20,24},{24,20},{28,16},{32,44},... | collective-permute-start | bytes 12296 | tf_op jit(solution)/shard_map/ppermute | solution.py:286
  50.0 3.6 %collective-permute-start.1 = (f32[8,128]{1,0:T(8,128)S(1)}, f32[8,128]{1,0:T(8,128)S(1)}, u32[]{:S(2)}, u32[]{:S(2)}) collective-permute-start(f32[8,128]{1,0:T(8,128)S(1)} %get-tuple-element.23.here), channel_id=1, source_target_pairs={{0,8},{4,12},{8,0},{12,4},{16,24},{20,28},{24,16},{28,20},{32,40},... | collective-permute-start | bytes 12296 | tf_op jit(solution)/shard_map/ppermute | solution.py:286
  51.6 1.9 %collective-permute-start = (f32[8,128]{1,0:T(8,128)S(1)}, f32[8,128]{1,0:T(8,128)S(1)}, u32[]{:S(2)}, u32[]{:S(2)}) collective-permute-start(f32[8,128]{1,0:T(8,128)S(1)} %get-tuple-element.23.here), channel_id=1, source_target_pairs={{0,4},{4,0},{8,12},{12,8},{16,20},{20,16},{24,28},{28,24},{32,36},... | collective-permute-start | bytes 12296 | tf_op jit(solution)/shard_map/ppermute | solution.py:286
  53.6 16.8 %collective-permute-start.5 = (f32[8,128]{1,0:T(8,128)S(1)}, f32[8,128]{1,0:T(8,128)S(1)}, u32[]{:S(2)}, u32[]{:S(2)}) collective-permute-start(f32[8,128]{1,0:T(8,128)S(1)} %add_add_fusion.6), channel_id=1, source_target_pairs={{0,48},{4,52},{8,56},{12,60},{16,32},{20,36},{24,40},{28,44},{32,1... | collective-permute-start | bytes 12296 | tf_op jit(solution)/shard_map/ppermute | solution.py:286
  57.2 13.3 %collective-permute-start.4 = (f32[8,128]{1,0:T(8,128)S(1)}, f32[8,128]{1,0:T(8,128)S(1)}, u32[]{:S(2)}, u32[]{:S(2)}) collective-permute-start(f32[8,128]{1,0:T(8,128)S(1)} %add_add_fusion.6), channel_id=1, source_target_pairs={{0,32},{4,36},{8,40},{12,44},{16,48},{20,52},{24,56},{28,60},{32,0... | collective-permute-start | bytes 12296 | tf_op jit(solution)/shard_map/ppermute | solution.py:286
  57.7 12.7 %collective-permute-start.3 = (f32[8,128]{1,0:T(8,128)S(1)}, f32[8,128]{1,0:T(8,128)S(1)}, u32[]{:S(2)}, u32[]{:S(2)}) collective-permute-start(f32[8,128]{1,0:T(8,128)S(1)} %add_add_fusion.6), channel_id=1, source_target_pairs={{0,16},{4,20},{8,24},{12,28},{16,0},{20,4},{24,8},{28,12},{32,48},... | collective-permute-start | bytes 12296 | tf_op jit(solution)/shard_map/ppermute | solution.py:286
  75.0 29.6 %all-to-all-start.2 = ((bf16[64,8,768]{2,1,0:T(8,128)(2,1)}), bf16[64,8,768]{2,1,0:T(8,128)(2,1)S(1)}, u32[]{:S(2)}, u32[]{:S(2)}) async-start(bf16[64,8,768]{2,1,0:T(8,128)(2,1)} %bitcast.7), calls=%async_computation.2 | async-start | bytes 1572864 | tf_op jit(solution)/shard_map/all_to_all | solution.py:277
  81.1 21.3 %collective-permute-start.8 = (f32[8,128]{1,0:T(8,128)S(1)}, f32[8,128]{1,0:T(8,128)S(1)}, u32[]{:S(2)}, u32[]{:S(2)}) collective-permute-start(f32[8,128]{1,0:T(8,128)S(1)} %add_add_fusion.5), channel_id=1, source_target_pairs={{0,192},{4,196},{8,200},{12,204},{16,208},{20,212},{24,216},{28,22... | collective-permute-start | bytes 12296 | tf_op jit(solution)/shard_map/ppermute | solution.py:286
  85.0 19.6 %collective-permute-start.7 = (f32[8,128]{1,0:T(8,128)S(1)}, f32[8,128]{1,0:T(8,128)S(1)}, u32[]{:S(2)}, u32[]{:S(2)}) collective-permute-start(f32[8,128]{1,0:T(8,128)S(1)} %add_add_fusion.5), channel_id=1, source_target_pairs={{0,128},{4,132},{8,136},{12,140},{16,144},{20,148},{24,152},{28,15... | collective-permute-start | bytes 12296 | tf_op jit(solution)/shard_map/ppermute | solution.py:286
  87.1 17.5 %collective-permute-start.6 = (f32[8,128]{1,0:T(8,128)S(1)}, f32[8,128]{1,0:T(8,128)S(1)}, u32[]{:S(2)}, u32[]{:S(2)}) collective-permute-start(f32[8,128]{1,0:T(8,128)S(1)} %add_add_fusion.5), channel_id=1, source_target_pairs={{0,64},{4,68},{8,72},{12,76},{16,80},{20,84},{24,88},{28,92},{32,9... | collective-permute-start | bytes 12296 | tf_op jit(solution)/shard_map/ppermute | solution.py:286
  139.1 38.1 %copy-start.11 = (f32[3,256,128]{2,1,0:T(8,128)S(1)}, f32[3,256,128]{2,1,0:T(8,128)}, u32[]{:S(2)}) copy-start(f32[3,256,128]{2,1,0:T(8,128)} %copy-done.9) | copy-start | bytes 1179652
  139.1 38.1 %copy-start.13 = (f32[3,256,128]{2,1,0:T(8,128)S(1)}, f32[3,256,128]{2,1,0:T(8,128)}, u32[]{:S(2)}) copy-start(f32[3,256,128]{2,1,0:T(8,128)} %copy-done.12) | copy-start | bytes 1179652
  139.1 38.1 %all-to-all-start.4 = ((bf16[64,8,768]{2,1,0:T(8,128)(2,1)}), bf16[64,8,768]{2,1,0:T(8,128)(2,1)S(1)}, u32[]{:S(2)}, u32[]{:S(2)}) async-start(bf16[64,8,768]{2,1,0:T(8,128)(2,1)} %bitcast.11), calls=%async_computation.4 | async-start | bytes 1572864 | tf_op jit(solution)/shard_map/all_to_all | solution.py:277
  145.1 4.9 %collective-permute-start.11 = (f32[8,128]{1,0:T(8,128)S(1)}, f32[8,128]{1,0:T(8,128)S(1)}, u32[]{:S(2)}, u32[]{:S(2)}) collective-permute-start(f32[8,128]{1,0:T(8,128)S(1)} %get-tuple-element.35), channel_id=1, source_target_pairs={{0,3},{1,2},{2,1},{3,0},{4,7},{5,6},{6,5},{7,4},{8,11},{9,10},{10,... | collective-permute-start | bytes 12296 | tf_op jit(solution)/shard_map/ppermute | solution.py:286
  148.2 5.1 %collective-permute-start.10 = (f32[8,128]{1,0:T(8,128)S(1)}, f32[8,128]{1,0:T(8,128)S(1)}, u32[]{:S(2)}, u32[]{:S(2)}) collective-permute-start(f32[8,128]{1,0:T(8,128)S(1)} %get-tuple-element.35), channel_id=1, source_target_pairs={{0,2},{1,3},{2,0},{3,1},{4,6},{5,7},{6,4},{7,5},{8,10},{9,11},{10,... | collective-permute-start | bytes 12296 | tf_op jit(solution)/shard_map/ppermute | solution.py:286
  148.8 4.5 %collective-permute-start.9 = (f32[8,128]{1,0:T(8,128)S(1)}, f32[8,128]{1,0:T(8,128)S(1)}, u32[]{:S(2)}, u32[]{:S(2)}) collective-permute-start(f32[8,128]{1,0:T(8,128)S(1)} %get-tuple-element.35), channel_id=1, source_target_pairs={{0,1},{1,0},{2,3},{3,2},{4,5},{5,4},{6,7},{7,6},{8,9},{9,8},{10,11... | collective-permute-start | bytes 12296 | tf_op jit(solution)/shard_map/ppermute | solution.py:286
  153.3 3.2 %collective-permute-start.14 = (f32[8,128]{1,0:T(8,128)S(1)}, f32[8,128]{1,0:T(8,128)S(1)}, u32[]{:S(2)}, u32[]{:S(2)}) collective-permute-start(f32[8,128]{1,0:T(8,128)S(1)} %add_add_fusion.3), channel_id=1, source_target_pairs={{0,12},{4,8},{8,4},{12,0},{16,28},{20,24},{24,20},{28,16},{32,44},... | collective-permute-start | bytes 12296 | tf_op jit(solution)/shard_map/ppermute | solution.py:286
  153.4 3.7 %collective-permute-start.13 = (f32[8,128]{1,0:T(8,128)S(1)}, f32[8,128]{1,0:T(8,128)S(1)}, u32[]{:S(2)}, u32[]{:S(2)}) collective-permute-start(f32[8,128]{1,0:T(8,128)S(1)} %add_add_fusion.3), channel_id=1, source_target_pairs={{0,8},{4,12},{8,0},{12,4},{16,24},{20,28},{24,16},{28,20},{32,40},... | collective-permute-start | bytes 12296 | tf_op jit(solution)/shard_map/ppermute | solution.py:286
  154.0 3.1 %collective-permute-start.12 = (f32[8,128]{1,0:T(8,128)S(1)}, f32[8,128]{1,0:T(8,128)S(1)}, u32[]{:S(2)}, u32[]{:S(2)}) collective-permute-start(f32[8,128]{1,0:T(8,128)S(1)} %add_add_fusion.3), channel_id=1, source_target_pairs={{0,4},{4,0},{8,12},{12,8},{16,20},{20,16},{24,28},{28,24},{32,36},... | collective-permute-start | bytes 12296 | tf_op jit(solution)/shard_map/ppermute | solution.py:286
  157.1 8.6 %collective-permute-start.17 = (f32[8,128]{1,0:T(8,128)S(1)}, f32[8,128]{1,0:T(8,128)S(1)}, u32[]{:S(2)}, u32[]{:S(2)}) collective-permute-start(f32[8,128]{1,0:T(8,128)S(1)} %add_add_fusion.2), channel_id=1, source_target_pairs={{0,48},{4,52},{8,56},{12,60},{16,32},{20,36},{24,40},{28,44},{32,1... | collective-permute-start | bytes 12296 | tf_op jit(solution)/shard_map/ppermute | solution.py:286
  160.2 5.6 %collective-permute-start.16 = (f32[8,128]{1,0:T(8,128)S(1)}, f32[8,128]{1,0:T(8,128)S(1)}, u32[]{:S(2)}, u32[]{:S(2)}) collective-permute-start(f32[8,128]{1,0:T(8,128)S(1)} %add_add_fusion.2), channel_id=1, source_target_pairs={{0,32},{4,36},{8,40},{12,44},{16,48},{20,52},{24,56},{28,60},{32,0... | collective-permute-start | bytes 12296 | tf_op jit(solution)/shard_map/ppermute | solution.py:286
  161.1 5.1 %collective-permute-start.15 = (f32[8,128]{1,0:T(8,128)S(1)}, f32[8,128]{1,0:T(8,128)S(1)}, u32[]{:S(2)}, u32[]{:S(2)}) collective-permute-start(f32[8,128]{1,0:T(8,128)S(1)} %add_add_fusion.2), channel_id=1, source_target_pairs={{0,16},{4,20},{8,24},{12,28},{16,0},{20,4},{24,8},{28,12},{32,48},... | collective-permute-start | bytes 12296 | tf_op jit(solution)/shard_map/ppermute | solution.py:286
  166.2 6.5 %collective-permute-start.20 = (f32[8,128]{1,0:T(8,128)S(1)}, f32[8,128]{1,0:T(8,128)S(1)}, u32[]{:S(2)}, u32[]{:S(2)}) collective-permute-start(f32[8,128]{1,0:T(8,128)S(1)} %add_add_fusion.1), channel_id=1, source_target_pairs={{0,192},{4,196},{8,200},{12,204},{16,208},{20,212},{24,216},{28,22... | collective-permute-start | bytes 12296 | tf_op jit(solution)/shard_map/ppermute | solution.py:286
  169.7 7.5 %collective-permute-start.19 = (f32[8,128]{1,0:T(8,128)S(1)}, f32[8,128]{1,0:T(8,128)S(1)}, u32[]{:S(2)}, u32[]{:S(2)}) collective-permute-start(f32[8,128]{1,0:T(8,128)S(1)} %add_add_fusion.1), channel_id=1, source_target_pairs={{0,128},{4,132},{8,136},{12,140},{16,144},{20,148},{24,152},{28,15... | collective-permute-start | bytes 12296 | tf_op jit(solution)/shard_map/ppermute | solution.py:286
  171.8 5.4 %collective-permute-start.18 = (f32[8,128]{1,0:T(8,128)S(1)}, f32[8,128]{1,0:T(8,128)S(1)}, u32[]{:S(2)}, u32[]{:S(2)}) collective-permute-start(f32[8,128]{1,0:T(8,128)S(1)} %add_add_fusion.1), channel_id=1, source_target_pairs={{0,64},{4,68},{8,72},{12,76},{16,80},{20,84},{24,88},{28,92},{32,9... | collective-permute-start | bytes 12296 | tf_op jit(solution)/shard_map/ppermute | solution.py:286
  (7 other events, 90.6 us)
